TPU v7x, 32 devices: a whole 2x2x4 slice. The times are simulated.
32 devices in a mesh: ws: 4 (over y, x), ctx: 8 (over z, core).
Axes of the slice: x: 2, y: 2, z: 4, core: 2. Of those that a mesh axis runs over, the one named last changes fastest.
Arguments:
- inputs: bfloat16 [8, 8192, 1600], P('ws', 'ctx'), may hold values from -6 to 6
- cotangent: bfloat16 [8, 8192, 1600], P('ws', 'ctx'), may hold values from -6 to 6
- block_ids: int32 [8, 8192], P('ws', 'ctx'), may hold values from 0 to 63, never falling along the last dimension, each value on 1 to 256 neighbouring positions
- first_gain: bfloat16 [1600], P('ws'), may hold values from 0.5 to 1.5
- first_shift: bfloat16 [1600], P('ws'), may hold values from -2 to 2
- weight_in: bfloat16 [1600, 800], P('ws'), may hold values from -0.15625 to 0.15625
- second_gain: bfloat16 [800], P('ws'), may hold values from 0.5 to 1.5
- second_shift: bfloat16 [800], P('ws'), may hold values from -2 to 2
- weight_conv: bfloat16 [5, 800, 800], P(None, 'ws'), may hold values from -0.09375 to 0.09375
- third_gain: bfloat16 [800], P('ws'), may hold values from 0.5 to 1.5
- third_shift: bfloat16 [800], P('ws'), may hold values from -2 to 2
- weight_out: bfloat16 [800, 1600], P('ws'), may hold values from -0.3125 to 0.3125
- output_bias: bfloat16 [1600], P('ws'), may hold values from -2 to 2
Outputs:
- block_output: bfloat16 [8, 8192, 1600], P('ws', 'ctx')
- input_grad: bfloat16 [8, 8192, 1600], P('ws', 'ctx')
- first_gain_grad: float32 [1600], P('ws')
- first_shift_grad: float32 [1600], P('ws')
- weight_in_grad: float32 [1600, 800], P('ws')
- second_gain_grad: float32 [800], P('ws')
- second_shift_grad: float32 [800], P('ws')
- weight_conv_grad: float32 [5, 800, 800], P(None, 'ws')
- third_gain_grad: float32 [800], P('ws')
- third_shift_grad: float32 [800], P('ws')
- weight_out_grad: float32 [800, 1600], P('ws')
- output_bias_grad: float32 [1600], P('ws')
Inputs may be any that keep to these rules, and one draw needn't show every extreme that they name: `block_ids`: within a sequence the ids never fall, start at 0 and take every value up to 63; a block holds 1 to 256 tokens, and some block exactly 256.
All inputs are finite; a program needn't handle non-finite values.
Results may differ from a plain program's by a relative error of at most 0.017.
Values may be sent and summed in bfloat16 or wider, within the bound.
No kernel may reach another device: no remote copies, remote signals or barrier semaphores. Data moves between devices by JAX's collectives and lax.ppermute only.
A program may use at most 256 MiB of HBM per device.

v0:
```python
import jax
import jax.numpy as jnp
from jax import lax
from jax.sharding import PartitionSpec as P

KERNEL_TAPS = 5
DILATION_STEP = 16


EPS = 1e-05


def extended_2(x, sides, width):
    for axis, dim in sides:
        peers, length = (lax.axis_size(axis), x.shape[dim])
        up = [(i, (i + 1) % peers) for i in range(peers - 1)]
        down = [(j, i) for i, j in up]
        last = lax.slice_in_dim(x, length - width, length, axis=dim)
        initial = lax.slice_in_dim(x, 0, width, axis=dim)
        before = lax.ppermute(last, axis, up)
        after = lax.ppermute(initial, axis, down)
        x = jnp.concatenate([before, x, after], axis=dim)
    return x


def shifted(x, axis, by):
    peers = lax.axis_size(axis)
    pairs = [(i, i + by) for i in range(peers) if 0 <= i + by < peers]
    return lax.ppermute(x, axis, pairs)


def shortened(x):
    return jax.tree.map(lambda a: a.astype(jnp.bfloat16) if a.dtype == jnp.float32 else a, x)


def norm_parts(values, gain, shift):
    middle = jnp.mean(values, axis=-1, keepdims=True)
    centred = values - middle
    spread = jnp.mean(centred * centred, axis=-1, keepdims=True)
    scale = lax.rsqrt(spread + EPS)
    normed = centred * scale
    return (normed, scale, normed * gain + shift)


def norm_back(upstream, pre_act, normed, scale, gain):
    sigma = jax.nn.sigmoid(pre_act)
    grad_pre = upstream * (sigma * (1.0 + pre_act * (1.0 - sigma)))
    grad_gain = jnp.sum(grad_pre * normed, axis=0)
    grad_shift = jnp.sum(grad_pre, axis=0)
    scaled = grad_pre * gain
    grad_input = scale * (
        scaled
        - jnp.mean(scaled, axis=-1, keepdims=True)
        - normed * jnp.mean(scaled * normed, axis=-1, keepdims=True)
    )
    return (grad_input, grad_gain, grad_shift)


def one_sequence(seq_rows, seq_grad, own_ids, ahead_ids, whole):
    (
        first_gain,
        first_shift,
        weight_in,
        second_gain,
        second_shift,
        weight_conv,
        third_gain,
        third_shift,
        weight_out,
        output_bias,
    ) = whole
    gain_one = first_gain.astype(jnp.float32)
    gain_two = second_gain.astype(jnp.float32)
    gain_three = third_gain.astype(jnp.float32)
    length = seq_rows.shape[0]
    inner_width = weight_in.shape[1]
    border_width = KERNEL_TAPS // 2 * DILATION_STEP
    rows_float = seq_rows.astype(jnp.float32)
    normed_one, scale_one, pre_one = norm_parts(
        rows_float, gain_one, first_shift.astype(jnp.float32)
    )
    first_activation = jax.nn.silu(pre_one).astype(jnp.bfloat16)
    proj_one = jnp.dot(first_activation, weight_in, preferred_element_type=jnp.float32)
    normed_two, scale_two, pre_two = norm_parts(
        proj_one, gain_two, second_shift.astype(jnp.float32)
    )
    act_two = jax.nn.silu(pre_two).astype(jnp.bfloat16)
    extended = extended_2(act_two, (("ctx", 0),), border_width)
    ids_after = jnp.concatenate([own_ids, ahead_ids], axis=0)
    tap_list = []
    mask_list = []
    for kernel_tap_index in range(KERNEL_TAPS):
        tap_displacement = (kernel_tap_index - KERNEL_TAPS // 2) * DILATION_STEP
        tap_rows = lax.slice_in_dim(
            extended,
            border_width + tap_displacement,
            border_width + tap_displacement + length,
            axis=0,
        )
        if tap_displacement > 0:
            keep_mask = (
                lax.slice_in_dim(ids_after, tap_displacement, tap_displacement + length, axis=0)
                == own_ids
            ).astype(jnp.bfloat16)[:, None]
            tap_rows = tap_rows * keep_mask
            mask_list.append(keep_mask.astype(jnp.float32))
        else:
            mask_list.append(None)
        tap_list.append(tap_rows)
    stacked_taps = jnp.concatenate(tap_list, axis=1)
    conv_flat = weight_conv.reshape(KERNEL_TAPS * inner_width, inner_width)
    conv = jnp.dot(stacked_taps, conv_flat, preferred_element_type=jnp.float32)
    normed_three, scale_three, pre_three = norm_parts(
        conv, gain_three, third_shift.astype(jnp.float32)
    )
    act_three = jax.nn.silu(pre_three).astype(jnp.bfloat16)
    proj_two = jnp.dot(act_three, weight_out, preferred_element_type=jnp.float32)
    result = (rows_float + proj_two + output_bias.astype(jnp.float32)).astype(jnp.bfloat16)
    grad_out = seq_grad.astype(jnp.float32)
    bias_grad = jnp.sum(grad_out, axis=0)
    out_weight_grad = jnp.einsum(
        "ti,td->id", act_three, seq_grad, preferred_element_type=jnp.float32
    )
    grad_act_three = jnp.einsum(
        "td,id->ti", seq_grad, weight_out, preferred_element_type=jnp.float32
    )
    grad_conv, third_gain_grad, third_shift_grad = norm_back(
        grad_act_three, pre_three, normed_three, scale_three, gain_three
    )
    grad_conv_low = grad_conv.astype(jnp.bfloat16)
    conv_weight_grad = jnp.einsum(
        "tk,ti->ki", stacked_taps, grad_conv_low, preferred_element_type=jnp.float32
    ).reshape(KERNEL_TAPS, inner_width, inner_width)
    grad_stack = jnp.einsum(
        "ti,ki->tk", grad_conv_low, conv_flat, preferred_element_type=jnp.float32
    )
    grad_extended = jnp.zeros((length + 2 * border_width, inner_width), jnp.float32)
    for kernel_tap_index in range(KERNEL_TAPS):
        tap_displacement = (kernel_tap_index - KERNEL_TAPS // 2) * DILATION_STEP
        tap_grad = grad_stack[
            :, kernel_tap_index * inner_width : (kernel_tap_index + 1) * inner_width
        ]
        if mask_list[kernel_tap_index] is not None:
            tap_grad = tap_grad * mask_list[kernel_tap_index]
        grad_extended = grad_extended + jnp.pad(
            tap_grad, ((border_width + tap_displacement, border_width - tap_displacement), (0, 0))
        )
    rim_rows = jnp.concatenate(
        [grad_extended[:border_width], grad_extended[length + border_width :]], axis=0
    )
    received = extended_2(rim_rows.astype(jnp.bfloat16), (("ctx", 0),), border_width).astype(
        rim_rows.dtype
    )
    from_before = received[:border_width]
    from_after = received[3 * border_width :]
    grad_act_two = grad_extended[border_width : border_width + length]
    grad_act_two = grad_act_two + jnp.pad(from_before, ((0, length - border_width), (0, 0)))
    grad_act_two = grad_act_two + jnp.pad(from_after, ((length - border_width, 0), (0, 0)))
    grad_one, second_gain_grad, second_shift_grad = norm_back(
        grad_act_two, pre_two, normed_two, scale_two, gain_two
    )
    grad_one_low = grad_one.astype(jnp.bfloat16)
    in_weight_grad = jnp.einsum(
        "td,ti->di", first_activation, grad_one_low, preferred_element_type=jnp.float32
    )
    grad_act_one = jnp.einsum(
        "ti,di->td", grad_one_low, weight_in, preferred_element_type=jnp.float32
    )
    grad_branch, first_gain_grad, first_shift_grad = norm_back(
        grad_act_one, pre_one, normed_one, scale_one, gain_one
    )
    in_rows_grad = (grad_out + grad_branch).astype(jnp.bfloat16)
    terms = (
        first_gain_grad,
        first_shift_grad,
        in_weight_grad,
        second_gain_grad,
        second_shift_grad,
        conv_weight_grad,
        third_gain_grad,
        third_shift_grad,
        out_weight_grad,
        bias_grad,
    )
    return (result, in_rows_grad, terms)


def shards(
    inputs,
    cotangent,
    block_ids,
    first_gain,
    first_shift,
    weight_in,
    second_gain,
    second_shift,
    weight_conv,
    third_gain,
    third_shift,
    weight_out,
    output_bias,
):
    border_width = KERNEL_TAPS // 2 * DILATION_STEP
    ahead_all = shifted(block_ids[:, :border_width], "ctx", -1)
    totals = None
    outputs = []
    in_grads = []
    for micro_index in range(inputs.shape[0]):
        whole = (
            lax.all_gather(first_gain, "ws", axis=0, tiled=True),
            lax.all_gather(first_shift, "ws", axis=0, tiled=True),
            lax.all_gather(weight_in, "ws", axis=0, tiled=True),
            lax.all_gather(second_gain, "ws", axis=0, tiled=True),
            lax.all_gather(second_shift, "ws", axis=0, tiled=True),
            lax.all_gather(weight_conv, "ws", axis=1, tiled=True),
            lax.all_gather(third_gain, "ws", axis=0, tiled=True),
            lax.all_gather(third_shift, "ws", axis=0, tiled=True),
            lax.all_gather(weight_out, "ws", axis=0, tiled=True),
            lax.all_gather(output_bias, "ws", axis=0, tiled=True),
        )
        result, in_rows_grad, terms = one_sequence(
            inputs[micro_index],
            cotangent[micro_index],
            block_ids[micro_index],
            ahead_all[micro_index],
            whole,
        )
        outputs.append(result)
        in_grads.append(in_rows_grad)
        if totals is None:
            totals = terms
        else:
            totals = tuple((total + extra for total, extra in zip(totals, terms)))
    summed = jax.tree.map(lambda part: part.astype(jnp.float32), lax.psum(shortened(totals), "ctx"))
    owned = (
        lax.psum_scatter(
            summed[0].astype(jnp.bfloat16), "ws", scatter_dimension=0, tiled=True
        ).astype(jnp.float32),
        lax.psum_scatter(
            summed[1].astype(jnp.bfloat16), "ws", scatter_dimension=0, tiled=True
        ).astype(jnp.float32),
        lax.psum_scatter(
            summed[2].astype(jnp.bfloat16), "ws", scatter_dimension=0, tiled=True
        ).astype(jnp.float32),
        lax.psum_scatter(
            summed[3].astype(jnp.bfloat16), "ws", scatter_dimension=0, tiled=True
        ).astype(jnp.float32),
        lax.psum_scatter(
            summed[4].astype(jnp.bfloat16), "ws", scatter_dimension=0, tiled=True
        ).astype(jnp.float32),
        lax.psum_scatter(
            summed[5].astype(jnp.bfloat16), "ws", scatter_dimension=1, tiled=True
        ).astype(jnp.float32),
        lax.psum_scatter(
            summed[6].astype(jnp.bfloat16), "ws", scatter_dimension=0, tiled=True
        ).astype(jnp.float32),
        lax.psum_scatter(
            summed[7].astype(jnp.bfloat16), "ws", scatter_dimension=0, tiled=True
        ).astype(jnp.float32),
        lax.psum_scatter(
            summed[8].astype(jnp.bfloat16), "ws", scatter_dimension=0, tiled=True
        ).astype(jnp.float32),
        lax.psum_scatter(
            summed[9].astype(jnp.bfloat16), "ws", scatter_dimension=0, tiled=True
        ).astype(jnp.float32),
    )
    return (
        jnp.stack(outputs),
        jnp.stack(in_grads),
        owned[0],
        owned[1],
        owned[2],
        owned[3],
        owned[4],
        owned[5],
        owned[6],
        owned[7],
        owned[8],
        owned[9],
    )


def solution(mesh):
    placed = (
        P("ws", "ctx", None),
        P("ws", "ctx", None),
        P("ws", "ctx"),
        P("ws"),
        P("ws"),
        P("ws", None),
        P("ws"),
        P("ws"),
        P(None, "ws", None),
        P("ws"),
        P("ws"),
        P("ws", None),
        P("ws"),
    )
    return jax.shard_map(
        shards,
        mesh=mesh,
        in_specs=placed,
        out_specs=(
            P("ws", "ctx", None),
            P("ws", "ctx", None),
            P("ws"),
            P("ws"),
            P("ws", None),
            P("ws"),
            P("ws"),
            P(None, "ws", None),
            P("ws"),
            P("ws"),
            P("ws", None),
            P("ws"),
        ),
        check_vma=False,
    )
```

profile of v0, /device:TPU:0, one launch (start us, length us, event | category | flops | bytes accessed | tf_op | source)
XLA Modules:
  0.0 587.2 jit_solution(4776017566277598994)
XLA Ops:
  11.6 1.3 fusion.124
  20.0 17.7 %all-reduce.34 = (bf16[1600]{0:T(1024)(128)(2,1)S(1)}, bf16[1600]{0:T(1024)(128)(2,1)S(1)}, bf16[800]{0:T(1024)(128)(2,1)S(1)}, bf16[800]{0:T(1024)(128)(2,1)S(1...) all-reduce(bf16[1600]{0:T(1024)(128)(2,1)S(1)} %dynamic-update-slic, ...), channel_id=1, replica_groups=mesh['ws'=4,'ctx'=8] {'ws'}, use_global_device_ids=true, to_apply=%add.15 | all-reduce | flops 6400 | bytes 25600
  37.8 4.5 convert_reduce_fusion.3
  42.6 1.7 fusion.47
  44.4 6.6 %fusion.23 = (bf16[1024,1600]{0,1:T(8,128)(2,1)S(1)}, bf16[1024,1600]{0,1:T(8,128)(2,1)}) fusion(f32[1024]{0:T(1024)S(1)} %add_rsqrt_fusion.2, f32[1024]{0:T(1024)S(1)} %get-tuple-element.141, f32[1600]{0:T(1024)S(1)} %convert_element_type.231, f32[1600]{0:T(1024)S(1)} %convert_element_type.230, bf16[2,1024,1600]{1,2,0:T(8,128)(2,1)S(1)} %copy-done, ...), kind=kLoop, calls=%fused_computation.32 | loop fusion | flops 32768000 | bytes 13136384 | tf_op jit(solution)/shard_map/convert_element_type | solution.py:82
  52.7 1.7 all-gather.4.cloned.1.call-done
  54.4 5.1 fusion.125
  60.0 2.7 copy-done.10
  62.7 3.3 fusion.126
  66.5 2.9 multiply_convert_fusion.5
  69.5 1.7 collective-permute-start
  71.3 1.3 collective-permute-start.4
  72.6 4.3 collective-permute-start.3
  77.0 1.3 collective-permute-start.1
  80.0 1.9 fusion.81
  82.0 2.0 fusion.89
  86.0 1.4 constant_dynamic-update-slice_fusion.1
  87.5 2.4 copy-done.18
  89.8 2.2 fusion.79
  92.1 2.2 fusion.88
  94.3 39.4 %all-gather.6.cloned.1.call-done = bf16[5,800,800]{2,1,0:T(8,128)(2,1)} async-done(((bf16[5,200,800]{2,1,0:T(8,128)(2,1)}), bf16[5,800,800]{2,1,0:T(8,128)(2,1)}) %all-gather.6.cloned.1.call-update) | async-done | bytes 6400016 | tf_op jit(solution)/shard_map/all_gather | solution.py:215
  133.7 12.9 %fusion.127 = (f32[1024]{0:T(1024)S(1)}, f32[1024,800]{0,1:T(8,128)S(1)}) fusion(bf16[1024,4000]{0,1:T(8,128)(2,1)} %copy-done.18, bf16[4000,800]{1,0:T(8,128)(2,1)} %bitcast.212), kind=kOutput, calls=%fused_computation.234 | convolution fusion | flops 6554418176 | bytes 17872896 | tf_op jit(solution)/shard_map/dot_general | solution.py:112
  147.0 10.8 %fusion.128 = (f32[1024]{0:T(1024)S(1)}, f32[1024,800]{0,1:T(8,128)S(1)}) fusion(bf16[1024,4000]{0,1:T(8,128)(2,1)} %fusion.88, bf16[4000,800]{1,0:T(8,128)(2,1)S(1)} %bitcast.217), kind=kOutput, calls=%fused_computation.235 | convolution fusion | flops 6554418176 | bytes 17872896 | tf_op jit(solution)/shard_map/dot_general | solution.py:112
  157.8 1.6 copy-done.12
  159.8 15.7 %all-gather.8.cloned.1.call-done = bf16[800,1600]{1,0:T(8,128)(2,1)} async-done(((bf16[200,1600]{1,0:T(8,128)(2,1)}), bf16[800,1600]{1,0:T(8,128)(2,1)}) %all-gather.8.cloned.1.call-update) | async-done | bytes 2560016 | tf_op jit(solution)/shard_map/all_gather | solution.py:218
  175.6 8.6 %multiply_reduce_fusion.2 = (f32[800]{0:T(1024)S(1)}, f32[1024]{0:T(1024)S(1)}, f32[1024]{0:T(1024)S(1)}, f32[800]{0:T(1024)S(1)}, f32[1024,800]{0,1:T(8,128)S(1)}) fusion(f32[1024,800]{0,1:T(8,128)} %copy-done.12, f32[1024]{0:T(1024)S(1)} %add_rsqrt_fusion, f32[1024]{0:T(1024)S(1)} %broadcast_multiply_fusion.8, f32[800]{0:T(1024)S(1)} %convert_element_type.238, ...), kind=kOutput, calls=%fused_computation.90 | convolution fusion | flops 2637001216 | bytes 12521984 | tf_op jit(solution)/shard_map/td,id->ti/dot_general | solution.py:124
  184.2 7.8 %multiply_reduce_fusion.3 = (f32[800]{0:T(1024)S(1)}, f32[1024]{0:T(1024)S(1)}, f32[1024]{0:T(1024)S(1)}, f32[800]{0:T(1024)S(1)}, bf16[1024,800]{0,1:T(8,128)(2,1)S(1)}, /*index=5*/f32[1024,800]{0,1:T(8,128)S(1)}) fusion(f32[1024,800]{0,1:T(8,128)S(1)} %get-tuple-element.135, f32[1024]{0:T(1024)S(1)} %add_rsqrt_fusion.3, ...), kind=kOutput, calls=%fused_computation.91 | convolution fusion | flops 2643554816 | bytes 20627968 | tf_op jit(solution)/shard_map/td,id->ti/dot_general | solution.py:124
  192.0 13.8 %fusion.130 = f32[4000,800]{0,1:T(8,128)} fusion(bf16[1024,4000]{0,1:T(8,128)(2,1)} %fusion.88, bf16[1024,800]{0,1:T(8,128)(2,1)S(1)} %get-tuple-element.125), kind=kOutput, calls=%fused_computation.237 | convolution fusion | flops 6553600000 | bytes 22630400 | tf_op jit(solution)/shard_map/tk,ti->ki/dot_general | solution.py:131
  206.7 14.5 %fusion.131 = f32[1024,4000]{0,1:T(8,128)} fusion(bf16[4000,800]{1,0:T(8,128)(2,1)} %bitcast.213, bf16[1024,800]{0,1:T(8,128)(2,1)S(1)} %multiply_convert_fusion.3), kind=kOutput, calls=%fused_computation.238 | convolution fusion | flops 6553600000 | bytes 24422400 | tf_op jit(solution)/shard_map/ti,ki->tk/dot_general | solution.py:134
  221.2 11.9 %add_convert_fusion = bf16[4000,800]{0,1:T(8,128)(2,1)} fusion(f32[4000,800]{0,1:T(8,128)} %fusion.130, bf16[1024,4000]{0,1:T(8,128)(2,1)S(1)} %bitcast.209, bf16[1024,800]{0,1:T(8,128)(2,1)S(1)} %multiply_convert_fusion.3), kind=kOutput, calls=%fused_computation | convolution fusion | flops 6560000000 | bytes 29030400 | tf_op jit(solution)/shard_map/tk,ti->ki/dot_general | solution.py:131
  233.1 10.4 %copy.27 = bf16[4000,800]{1,0:T(8,128)(2,1)} copy(bf16[4000,800]{0,1:T(8,128)(2,1)} %add_convert_fusion) | data formatting | bytes 12800000 | tf_op jit(solution)/shard_map/convert_element_type | solution.py:33
  244.2 8.3 %fusion.116 = (f32[1024,800]{0,1:T(8,128)S(1)}, f32[1024,800]{0,1:T(8,128)S(1)}, f32[1024,800]{0,1:T(8,128)S(1)}, f32[1024,800]{0,1:T(8,128)S(1)}, f32[1024,800]{0,1:T(8,128)S(1)}) fusion(f32[1024,4000]{0,1:T(8,128)} %fusion.131, f32[1024]{0:T(1024)S(1)} %copy-done.45, f32[1024]{0:T(1024)S(1)} %copy-done.46), kind=kLoop, calls=%fused_computation.223 | loop fusion | flops 1638400 | bytes 32776192 | tf_op jit(solution)/shard_map/slice | solution.py:140
  252.5 5.4 fusion.110
  258.7 2.0 collective-permute-start.5
  260.7 1.4 collective-permute-start.6
  262.1 11.4 %fusion.132 = f32[1024,4000]{0,1:T(8,128)S(1)} fusion(bf16[4000,800]{1,0:T(8,128)(2,1)} %bitcast.214, bf16[1024,800]{0,1:T(8,128)(2,1)S(1)} %copy-done.57), kind=kOutput, calls=%fused_computation.239 | convolution fusion | flops 6553600000 | bytes 24422400 | tf_op jit(solution)/shard_map/ti,ki->tk/dot_general | solution.py:134
  273.6 5.5 fusion.115
  279.1 8.2 %fusion.104 = (bf16[1088,800]{0,1:T(8,128)(2,1)S(1)}, f32[1088,800]{0,1:T(8,128)}) fusion(f32[1024,800]{0,1:T(8,128)} %get-tuple-element.83, f32[1024,800]{0,1:T(8,128)} %get-tuple-element.84, f32[1024,800]{0,1:T(8,128)} %get-tuple-element.85, f32[1024,800]{0,1:T(8,128)} %get-tuple-element.86, f32[1024,800]{0,1:T(8,128)S(1)} %get-tuple-element.82), kind=kLoop, calls=%fused_computation.216 | loop fusion | flops 4352000 | bytes 21606400 | tf_op jit(solution)/shard_map/convert.2
  288.1 4.1 collective-permute-start.7
  292.2 1.9 collective-permute-start.8
  294.1 6.6 %fusion.63 = f32[800,1600]{1,0:T(8,128)S(1)} fusion(bf16[2,1024,1600]{1,2,0:T(8,128)(2,1)} %param.14, f32[1024,800]{0,1:T(8,128)S(1)} %get-tuple-element.135, f32[800]{0:T(1024)S(1)} %convert_element_type.239, f32[800]{0:T(1024)S(1)} %convert_element_type.238, f32[1024]{0:T(1024)S(1)} %add_rsqrt_fusion.3, f32[1024]{0:T(1024)S(1)} %broadcast_multiply_fusion.10), kind=kOutput, calls=%fused_computation.86 | convolution fusion | flops 2628812800 | bytes 11688192 | tf_op jit(solution)/shard_map/ti,td->id/dot_general | solution.py:121
  300.8 5.3 add_convert_fusion.2
  306.3 1.6 maximum_convert_fusion
  308.1 2.1 maximum_convert_fusion.1
  310.4 10.2 %multiply_reduce_fusion.4 = (f32[800]{0:T(1024)S(1)}, f32[1024]{0:T(1024)S(1)}, f32[1024]{0:T(1024)S(1)}, f32[800]{0:T(1024)S(1)}, f32[1024,800]{0,1:T(8,128)S(1...) fusion(f32[1024,800]{0,1:T(8,128)S(1)} %copy-done.2, ...), kind=kLoop, calls=%fused_computation.92 | loop fusion | flops 34399104 | bytes 20122368 | tf_op jit(solution)/shard_map/reduce_sum | solution.py:48
  320.8 2.5 multiply_convert_fusion
  323.4 5.7 fusion.26
  329.1 12.2 %fusion.46 = (f32[1600]{0:T(1024)S(1)}, f32[1024]{0:T(1024)S(1)}, f32[1024]{0:T(1024)S(1)}, f32[1600]{0:T(1024)S(1)}, f32[1024]{0:T(1024)S(1)}, /*index=5*/f32[1...) fusion(f32[1024]{0:T(1024)S(1)} %copy-done.36, f32[1024]{0:T(1024)S(1)} %copy-done.28, ...), kind=kOutput, calls=%fused_computation.55 | convolution fusion | flops 2670581760 | bytes 23930368 | tf_op jit(solution)/shard_map/ti,di->td/dot_general | solution.py:166
  341.4 3.6 fusion.129
  345.0 5.0 add_convert_fusion.1
  350.2 14.8 %fusion.55 = (bf16[1,1024,1600]{1,2,0:T(8,128)(2,1)S(1)}, bf16[1,1024,1600]{1,2,0:T(8,128)(2,1)}, f32[1600]{0:T(1024)S(1)}, f32[1600]{0:T(1024)S(1)}) fusion(f32[1024,1600]{0,1:T(8,128)} %get-tuple-element.140, f32[1024]{0:T(1024)S(1)} %broadcast_multiply_fusion.14, f32[1024]{0:T(1024)S(1)} %broadcast_multiply_fusion.15, f32[1600]{0:T(1024)S(1)} %copy-done.24, ...), kind=kLoop, calls=%fused_computation.72 | loop fusion | flops 39318400 | bytes 32819968 | tf_op jit(solution)/shard_map/stack | solution.py:269
  365.0 16.2 %all-reduce.33 = (bf16[1600]{0:T(1024)(128)(2,1)S(1)}, bf16[1600]{0:T(1024)(128)(2,1)S(1)}, bf16[1600]{0:T(1024)(128)(2,1)S(1)}, bf16[800]{0:T(1024)(128)(2,1)S(...) all-reduce(bf16[1600]{0:T(1024)(128)(2,1)S(1)} %copy-done.48, ...), channel_id=1, replica_groups=mesh['ws'=4,'ctx'=8] {'ws'}, use_global_device_ids=true, to_apply=%add.20 | all-reduce | flops 9600 | bytes 38400
  381.7 15.7 %all-reduce.31 = (bf16[400]{0:T(512)(128)(2,1)S(1)}, bf16[400]{0:T(512)(128)(2,1)S(1)}, bf16[200]{0:T(256)(128)(2,1)S(1)}, bf16[200]{0:T(256)(128)(2,1)S(1)}, bf...) all-reduce(bf16[400]{0:T(512)(128)(2,1)S(1)} %dynamic-slice.8, ...), channel_id=1, replica_groups=mesh['ws'=4,'ctx'=8] {'ctx'}, use_global_device_ids=true, to_apply=%region_26.27 | all-reduce | flops 2000 | bytes 8000 | tf_op jit(solution)/shard_map/psum | solution.py:234
  401.4 5.5 pad_maximum_fusion.1
  406.9 7.6 %fusion.67 = bf16[1,1024,1600]{1,2,0:T(8,128)(2,1)} fusion(f32[1600]{0:T(1024)S(1)} %convert_element_type.241, bf16[800,1600]{1,0:T(8,128)(2,1)S(1)} %copy-done.55, bf16[2,1024,1600]{1,2,0:T(8,128)(2,1)} %param.13, f32[1024,800]{0,1:T(8,128)S(1)} %copy-done.15, f32[1024]{0:T(1024)S(1)} %add_rsqrt_fusion, f32[1024]{0:T(1024)S(1)} %broadcast_multiply_fusion.8, ...), kind=kOutput, calls=%fused_computation.120 | convolution fusion | flops 2635366400 | bytes 12411392 | tf_op jit(solution)/shard_map/dot_general | solution.py:117
  414.5 3.0 constant_dynamic-slice_fusion
  417.5 29.0 %reduce-scatter.10.cloned.1.call-done = bf16[200,1600]{1,0:T(8,128)(2,1)} async-done(((bf16[800,1600]{1,0:T(8,128)(2,1)}), bf16[200,1600]{1,0:T(8,128)(2,1)}) %reduce-scatter.10.cloned.1.call-update) | async-done | bytes 640016
  446.5 45.4 %reduce-scatter.8.cloned.1.call-done = bf16[400,800]{1,0:T(8,128)(2,1)} async-done(((bf16[1600,800]{1,0:T(8,128)(2,1)}), bf16[400,800]{1,0:T(8,128)(2,1)}) %reduce-scatter.8.cloned.1.call-update) | async-done | bytes 640016
  491.9 7.2 %fusion.68 = bf16[1,1024,1600]{1,2,0:T(8,128)(2,1)S(1)} fusion(f32[1600]{0:T(1024)S(1)} %convert_element_type.241, bf16[800,1600]{1,0:T(8,128)(2,1)} %all-gather.8.cloned.1.call-done, bf16[2,1024,1600]{1,2,0:T(8,128)(2,1)} %param.13, f32[1024,800]{0,1:T(8,128)S(1)} %copy-done.6, f32[800]{0:T(1024)S(1)} %convert_element_type.239, ...), kind=kOutput, calls=%fused_computation.121 | convolution fusion | flops 2635366400 | bytes 12411392 | tf_op jit(solution)/shard_map/dot_general | solution.py:117
  499.2 3.4 pad_maximum_fusion
  502.5 70.7 %all-reduce.40.cloned.1.call-done = (bf16[400,800]{1,0:T(8,128)(2,1)}, bf16[5,200,800]{2,1,0:T(8,128)(2,1)}, bf16[200,1600]{1,0:T(8,128)(2,1)}) async-done(((bf16[400,800]{1,0:T(8,128)(2,1)}, bf16[5,200,800]{2,1,0:T(8,128)(2,1)}, bf16[200,1600]{1,0:T(8,128)(2,1)}), (bf16[400,800]{1,0:T(8,128)(2,1)}, bf16[5,200,800]{2,1,0:T(8,128)(2,1)}, bf16[200,1600]{1,0:T(8,128)(2,1)})) %all-reduce.40.cloned.1.call-update) | async-done | bytes 2880016 | tf_op jit(solution)/shard_map/psum | solution.py:234
  573.2 2.4 convert_element_type.270
  575.6 2.2 convert_element_type.283
  577.9 2.0 convert_element_type.277
  (244 shorter events, 24.9 us)
Async XLA Ops:
  7.2 12.6 %copy-start.49 = (bf16[400]{0:T(512)(128)(2,1)S(1)}, bf16[400]{0:T(512)(128)(2,1)}, u32[]{:S(2)}) copy-start(bf16[400]{0:T(512)(128)(2,1)} %param.16) | copy-start | bytes 2404
  7.2 47.2 %all-gather.4.cloned.1.call-start = ((), (), s32[]{:S(2)}) async-start(), calls=%async_computation.2 | async-start | bytes 3584000 | tf_op jit(solution)/shard_map/all_gather | solution.py:212
  7.9 125.8 %all-gather.6.cloned.1.call-start = ((), (), s32[]{:S(2)}) async-start(), calls=%async_computation.3 | async-start | bytes 8960000 | tf_op jit(solution)/shard_map/all_gather | solution.py:215
  8.7 166.9 %all-gather.8.cloned.1.call-start = ((), (), s32[]{:S(2)}) async-start(), calls=%async_computation.4 | async-start | bytes 3328000 | tf_op jit(solution)/shard_map/all_gather | solution.py:218
  9.4 41.9 %collective-permute-start.2 = (s32[2,32]{1,0:T(2,128)S(1)}, s32[2,32]{1,0:T(2,128)S(1)}, u32[]{:S(2)}, u32[]{:S(2)}) collective-permute-start(s32[2,32]{1,0:T(2,128)S(1)} %slice.158), channel_id=1, source_target_pairs={{1,0},{2,1},{3,2},{4,3},{5,4},{6,5},{7,6},{9,8},{10,9},{11,10},{12... | collective-permute-start | bytes 776 | tf_op jit(solution)/shard_map/ppermute | solution.py:29
  10.7 403.8 %all-reduce.38.cloned.1.call-start = ((), (), s32[]{:S(2)}) async-start(), calls=%async_computation.5 | async-start | bytes 14336000
  37.7 6.6 %copy-start.41 = (f32[1600]{0:T(1024)}, f32[1600]{0:T(1024)S(1)}, u32[]{:S(2)}) copy-start(f32[1600]{0:T(1024)S(1)} %convert_element_type.231) | copy-start | bytes 19204
  37.8 28.6 %copy-start.29 = (f32[800]{0:T(1024)}, f32[800]{0:T(1024)S(1)}, u32[]{:S(2)}) copy-start(f32[800]{0:T(1024)S(1)} %convert_element_type.233) | copy-start | bytes 9604
  37.8 6.6 %copy-start.23 = (f32[1600]{0:T(1024)}, f32[1600]{0:T(1024)S(1)}, u32[]{:S(2)}) copy-start(f32[1600]{0:T(1024)S(1)} %convert_element_type.230) | copy-start | bytes 19204
  37.8 4.8 copy-start
  44.3 6.7 %copy-start.35 = (f32[1024]{0:T(1024)}, f32[1024]{0:T(1024)S(1)}, u32[]{:S(2)}) copy-start(f32[1024]{0:T(1024)S(1)} %add_rsqrt_fusion.5) | copy-start | bytes 12292
  44.4 6.6 %copy-start.37 = (f32[1024]{0:T(1024)}, f32[1024]{0:T(1024)S(1)}, u32[]{:S(2)}) copy-start(f32[1024]{0:T(1024)S(1)} %add_rsqrt_fusion.2) | copy-start | bytes 12292
  44.4 6.6 %copy-start.50 = (bf16[400]{0:T(512)(128)(2,1)S(1)}, bf16[400]{0:T(512)(128)(2,1)}, u32[]{:S(2)}) copy-start(bf16[400]{0:T(512)(128)(2,1)} %param.25) | copy-start | bytes 2404
  51.0 8.5 %copy-start.8 = (bf16[1024,1600]{0,1:T(8,128)(2,1)}, bf16[1024,1600]{0,1:T(8,128)(2,1)S(1)}, u32[]{:S(2)}) copy-start(bf16[1024,1600]{0,1:T(8,128)(2,1)S(1)} %get-tuple-element.94) | copy-start | bytes 9830404
  51.0 15.4 %copy-start.39 = (f32[800]{0:T(1024)}, f32[800]{0:T(1024)S(1)}, u32[]{:S(2)}) copy-start(f32[800]{0:T(1024)S(1)} %convert_element_type.234) | copy-start | bytes 9604
  51.3 8.2 %copy-start.47 = (bf16[1600]{0:T(1024)(128)(2,1)}, bf16[1600]{0:T(1024)(128)(2,1)S(1)}, u32[]{:S(2)}) copy-start(bf16[1600]{0:T(1024)(128)(2,1)S(1)} %dynamic-update-slice.6) | copy-start | bytes 9604
  54.4 5.6 copy-start.51
  59.5 6.9 %copy-start.1 = (f32[1024,800]{0,1:T(8,128)}, f32[1024,800]{0,1:T(8,128)S(1)}, u32[]{:S(2)}) copy-start(f32[1024,800]{0,1:T(8,128)S(1)} %get-tuple-element.131) | copy-start | bytes 9830404
  59.6 6.9 %copy-start.19 = (f32[1024]{0:T(1024)}, f32[1024]{0:T(1024)S(1)}, u32[]{:S(2)}) copy-start(f32[1024]{0:T(1024)S(1)} %broadcast_multiply_fusion.9) | copy-start | bytes 12292
  60.0 6.5 %copy-start.31 = (f32[1024]{0:T(1024)}, f32[1024]{0:T(1024)S(1)}, u32[]{:S(2)}) copy-start(f32[1024]{0:T(1024)S(1)} %add_rsqrt_fusion.1) | copy-start | bytes 12292
  69.5 8.8 %collective-permute-start = (bf16[32,800]{0,1:T(8,128)(2,1)S(1)}, bf16[32,800]{0,1:T(8,128)(2,1)S(1)}, u32[]{:S(2)}, u32[]{:S(2)}) collective-permute-start(bf16[32,800]{0,1:T(8,128)(2,1)S(1)} %get-tuple-element.105), channel_id=1, source_target_pairs={{0,1},{1,2},{2,3},{3,4},{4,5},{5,6},{6,7},{8,9},{9,10},{10,11},{11... | collective-permute-start | bytes 153608 | tf_op jit(solution)/shard_map/ppermute | solution.py:20
  71.3 16.1 %collective-permute-start.4 = (bf16[32,800]{0,1:T(8,128)(2,1)S(1)}, bf16[32,800]{0,1:T(8,128)(2,1)S(1)}, u32[]{:S(2)}, u32[]{:S(2)}) collective-permute-start(bf16[32,800]{0,1:T(8,128)(2,1)S(1)} %get-tuple-element.102), channel_id=1, source_target_pairs={{1,0},{2,1},{3,2},{4,3},{5,4},{6,5},{7,6},{9,8},{10,9},{11,10},{12... | collective-permute-start | bytes 153608 | tf_op jit(solution)/shard_map/ppermute | solution.py:21
  72.6 7.4 %collective-permute-start.3 = (bf16[32,800]{0,1:T(8,128)(2,1)S(1)}, bf16[32,800]{0,1:T(8,128)(2,1)S(1)}, u32[]{:S(2)}, u32[]{:S(2)}) collective-permute-start(bf16[32,800]{0,1:T(8,128)(2,1)S(1)} %get-tuple-element.103), channel_id=1, source_target_pairs={{0,1},{1,2},{2,3},{3,4},{4,5},{5,6},{6,7},{8,9},{9,10},{10,11},{11... | collective-permute-start | bytes 153608 | tf_op jit(solution)/shard_map/ppermute | solution.py:20
  77.0 7.0 %collective-permute-start.1 = (bf16[32,800]{0,1:T(8,128)(2,1)S(1)}, bf16[32,800]{0,1:T(8,128)(2,1)S(1)}, u32[]{:S(2)}, u32[]{:S(2)}) collective-permute-start(bf16[32,800]{0,1:T(8,128)(2,1)S(1)} %get-tuple-element.104), channel_id=1, source_target_pairs={{1,0},{2,1},{3,2},{4,3},{5,4},{6,5},{7,6},{9,8},{10,9},{11,10},{12... | collective-permute-start | bytes 153608 | tf_op jit(solution)/shard_map/ppermute | solution.py:21
  133.7 13.3 %slice-start.6 = ((s8[7168000]{0:T(1024)(128)(4,1)}), s8[4194304]{0:T(1024)(128)(4,1)S(1)}, s32[]{:S(2)}) async-start(s8[7168000]{0:T(1024)(128)(4,1)} %bitcast.215), calls=%async_computation.15 | async-start | bytes 8388608
  133.7 13.3 %slice-start.7 = ((s8[7168000]{0:T(1024)(128)(4,1)}), s8[2973696]{0:T(1024)(128)(4,1)S(1)}, s32[]{:S(2)}) async-start(s8[7168000]{0:T(1024)(128)(4,1)} %bitcast.215), calls=%async_computation.16 | async-start | bytes 5947392
  146.6 147.5 %copy-start.5 = (f32[1024,800]{0,1:T(8,128)}, f32[1024,800]{0,1:T(8,128)S(1)}, u32[]{:S(2)}) copy-start(f32[1024,800]{0,1:T(8,128)S(1)} %get-tuple-element.135) | copy-start | bytes 9830404
  175.6 8.6 %copy-start.13 = (f32[1024,800]{0,1:T(8,128)S(1)}, f32[1024,800]{0,1:T(8,128)}, u32[]{:S(2)}) copy-start(f32[1024,800]{0,1:T(8,128)} %copy-done.12) | copy-start | bytes 9830404
  175.6 8.6 %copy-start.54 = (bf16[800,1600]{1,0:T(8,128)(2,1)S(1)}, bf16[800,1600]{1,0:T(8,128)(2,1)}, u32[]{:S(2)}) copy-start(bf16[800,1600]{1,0:T(8,128)(2,1)} %all-gather.8.cloned.1.call-done) | copy-start | bytes 7680004
  192.0 13.8 %copy-start.56 = (bf16[1024,800]{0,1:T(8,128)(2,1)}, bf16[1024,800]{0,1:T(8,128)(2,1)S(1)}, u32[]{:S(2)}) copy-start(bf16[1024,800]{0,1:T(8,128)(2,1)S(1)} %get-tuple-element.125) | copy-start | bytes 4915204
  205.8 15.4 %slice-start.4 = ((s8[8192000]{0:T(1024)(128)(4,1)}), s8[4194304]{0:T(1024)(128)(4,1)S(1)}, s32[]{:S(2)}) async-start(s8[8192000]{0:T(1024)(128)(4,1)} %bitcast.208), calls=%async_computation.13 | async-start | bytes 8388608
  206.7 14.5 %slice-start.5 = ((s8[8192000]{0:T(1024)(128)(4,1)}), s8[3997696]{0:T(1024)(128)(4,1)S(1)}, s32[]{:S(2)}) async-start(s8[8192000]{0:T(1024)(128)(4,1)} %bitcast.208), calls=%async_computation.14 | async-start | bytes 7995392
  243.5 203.0 %reduce-scatter.10.cloned.1.call-start = ((), (), s32[]{:S(2)}) async-start(), calls=%async_computation.7 | async-start | bytes 3328000
  252.5 9.6 %copy-start.57 = (bf16[1024,800]{0,1:T(8,128)(2,1)S(1)}, bf16[1024,800]{0,1:T(8,128)(2,1)}, u32[]{:S(2)}) copy-start(bf16[1024,800]{0,1:T(8,128)(2,1)} %copy-done.56) | copy-start | bytes 4915204
  258.7 47.6 %collective-permute-start.5 = (bf16[32,800]{0,1:T(8,128)(2,1)S(1)}, bf16[32,800]{0,1:T(8,128)(2,1)}, u32[]{:S(2)}, u32[]{:S(2)}) collective-permute-start(bf16[32,800]{0,1:T(8,128)(2,1)S(1)} %get-tuple-element.100), channel_id=1, source_target_pairs={{0,1},{1,2},{2,3},{3,4},{4,5},{5,6},{6,7},{8,9},{9,10},{10,11},{11... | collective-permute-start | bytes 153608 | tf_op jit(solution)/shard_map/ppermute | solution.py:20
  260.7 12.8 %copy-start.43 = (f32[1024]{0:T(1024)S(1)}, f32[1024]{0:T(1024)}, u32[]{:S(2)}) copy-start(f32[1024]{0:T(1024)} %get-tuple-element.73) | copy-start | bytes 12292
  260.7 12.8 %copy-start.44 = (f32[1024]{0:T(1024)S(1)}, f32[1024]{0:T(1024)}, u32[]{:S(2)}) copy-start(f32[1024]{0:T(1024)} %get-tuple-element.119) | copy-start | bytes 12292
  260.7 45.6 %collective-permute-start.6 = (bf16[32,800]{0,1:T(8,128)(2,1)}, bf16[32,800]{0,1:T(8,128)(2,1)}, u32[]{:S(2)}, u32[]{:S(2)}) collective-permute-start(bf16[32,800]{0,1:T(8,128)(2,1)} %get-tuple-element.101), channel_id=1, source_target_pairs={{1,0},{2,1},{3,2},{4,3},{5,4},{6,5},{7,6},{9,8},{10,9},{11,10},{12... | collective-permute-start | bytes 153608 | tf_op jit(solution)/shard_map/ppermute | solution.py:21
  288.1 20.0 %collective-permute-start.7 = (bf16[32,800]{0,1:T(8,128)(2,1)}, bf16[32,800]{0,1:T(8,128)(2,1)}, u32[]{:S(2)}, u32[]{:S(2)}) collective-permute-start(bf16[32,800]{0,1:T(8,128)(2,1)} %get-tuple-element.98), channel_id=1, source_target_pairs={{0,1},{1,2},{2,3},{3,4},{4,5},{5,6},{6,7},{8,9},{9,10},{10,11},{11... | collective-permute-start | bytes 153608 | tf_op jit(solution)/shard_map/ppermute | solution.py:20
  292.2 8.6 %slice-start.2 = ((s8[6553600]{0:T(1024)(128)(4,1)}), s8[4194304]{0:T(1024)(128)(4,1)S(1)}, s32[]{:S(2)}) async-start(s8[6553600]{0:T(1024)(128)(4,1)} %bitcast.206), calls=%async_computation.11 | async-start | bytes 8388608
  292.2 8.6 %slice-start.3 = ((s8[6553600]{0:T(1024)(128)(4,1)}), s8[2359296]{0:T(1024)(128)(4,1)S(1)}, s32[]{:S(2)}) async-start(s8[6553600]{0:T(1024)(128)(4,1)} %bitcast.206), calls=%async_computation.12 | async-start | bytes 4718592
  292.2 8.6 %copy-start.14 = (f32[1024,800]{0,1:T(8,128)S(1)}, f32[1024,800]{0,1:T(8,128)}, u32[]{:S(2)}) copy-start(f32[1024,800]{0,1:T(8,128)} %copy-done.12) | copy-start | bytes 9830404
  292.2 15.9 %collective-permute-start.8 = (bf16[32,800]{0,1:T(8,128)(2,1)}, bf16[32,800]{0,1:T(8,128)(2,1)}, u32[]{:S(2)}, u32[]{:S(2)}) collective-permute-start(bf16[32,800]{0,1:T(8,128)(2,1)} %get-tuple-element.99), channel_id=1, source_target_pairs={{1,0},{2,1},{3,2},{4,3},{5,4},{6,5},{7,6},{9,8},{10,9},{11,10},{12... | collective-permute-start | bytes 153608 | tf_op jit(solution)/shard_map/ppermute | solution.py:21
  306.2 4.2 copy-start.2
  306.2 4.2 copy-start.20
  306.2 4.2 copy-start.22
  306.2 4.2 copy-start.30
  306.2 4.2 copy-start.32
  306.2 185.7 %reduce-scatter.8.cloned.1.call-start = ((), (), s32[]{:S(2)}) async-start(), calls=%async_computation.6 | async-start | bytes 3584000
  306.3 17.0 %slice-start = ((s8[6553600]{0:T(1024)(128)(4,1)}), s8[4194304]{0:T(1024)(128)(4,1)S(1)}, s32[]{:S(2)}) async-start(s8[6553600]{0:T(1024)(128)(4,1)} %bitcast.203), calls=%async_computation.9 | async-start | bytes 8388608
  310.4 10.3 %copy-start.4 = (f32[1024,800]{0,1:T(8,128)S(1)}, f32[1024,800]{0,1:T(8,128)}, u32[]{:S(2)}) copy-start(f32[1024,800]{0,1:T(8,128)} %copy-done.3) | copy-start | bytes 9830404
  310.4 12.9 %slice-start.1 = ((s8[6553600]{0:T(1024)(128)(4,1)}), s8[2359296]{0:T(1024)(128)(4,1)S(1)}, s32[]{:S(2)}) async-start(s8[6553600]{0:T(1024)(128)(4,1)} %bitcast.203), calls=%async_computation.10 | async-start | bytes 4718592
  323.4 5.7 copy-start.28
  323.4 5.7 copy-start.36
  323.4 5.7 copy-start.53
  329.1 12.3 %copy-start.7 = (f32[1024,1600]{0,1:T(8,128)}, f32[1024,1600]{0,1:T(8,128)S(1)}, u32[]{:S(2)}) copy-start(f32[1024,1600]{0,1:T(8,128)S(1)} %fusion.26) | copy-start | bytes 19660804
  329.1 12.3 %copy-start.11 = (bf16[1024,1600]{0,1:T(8,128)(2,1)S(1)}, bf16[1024,1600]{0,1:T(8,128)(2,1)}, u32[]{:S(2)}) copy-start(bf16[1024,1600]{0,1:T(8,128)(2,1)} %get-tuple-element.95) | copy-start | bytes 9830404
  350.0 223.2 %all-reduce.40.cloned.1.call-start = ((), (), s32[]{:S(2)}) async-start(), calls=%async_computation.8 | async-start | bytes 6348800 | tf_op jit(solution)/shard_map/psum | solution.py:234
  350.2 14.8 %copy-start.48 = (bf16[1600]{0:T(1024)(128)(2,1)S(1)}, bf16[1600]{0:T(1024)(128)(2,1)}, u32[]{:S(2)}) copy-start(bf16[1600]{0:T(1024)(128)(2,1)} %copy-done.47) | copy-start | bytes 9604
  401.4 5.5 copy-start.15
  401.4 5.5 copy-start.55
  414.5 77.4 %copy-start.6 = (f32[1024,800]{0,1:T(8,128)S(1)}, f32[1024,800]{0,1:T(8,128)}, u32[]{:S(2)}) copy-start(f32[1024,800]{0,1:T(8,128)} %copy-done.5) | copy-start | bytes 9830404
  491.9 7.2 %copy-start.16 = (bf16[1,1024,1600]{1,2,0:T(8,128)(2,1)S(1)}, bf16[1,1024,1600]{1,2,0:T(8,128)(2,1)}, u32[]{:S(2)}) copy-start(bf16[1,1024,1600]{1,2,0:T(8,128)(2,1)} %fusion.67) | copy-start | bytes 9830404
  573.2 4.7 copy-start.17
  (18 other events, 48.6 us)
Sparse Core Ops, SparseCore 0:
  9.9 44.4 all-gather.3
  56.2 77.4 all-gather.5
  135.5 39.9 all-gather.7
  243.7 153.7 all-reduce.37
  400.3 46.1 reduce-scatter.9
  449.4 42.4 reduce-scatter.7
  494.7 78.5 all-reduce.39
where the time goes:
time: 597 us; the launch traced here: 587 us
  waiting for transfers between devices  203 us (34%)
  matrix products  153 us (26%)
  other arithmetic  110 us (18%)
  blocking collectives  49.6 us (8%)
  local copies, waits for them, and re-layouts  33.1 us (6%)
  starting transfers between devices  19.5 us (3%)
  between operations  18.5 us (3%)
    unnamed x10, waiting for transfers between devices  75.8 us
    psum x1, waiting for transfers between devices, shards(): lax.psum(shortened(totals), 'ctx')  70.7 us
    all_gather x1, waiting for transfers between devices, shards(): lax.all_gather(weight_conv, 'ws', axis=1, tiled=True)  39.4 us
    unnamed x2, blocking collectives  33.9 us
    dot_general x2, matrix products, one_sequence(): jnp.einsum('ti,ki->tk', grad_conv_low, conv_flat, preferred_element_type=...  25.9 us
    dot_general x2, matrix products, one_sequence(): jnp.einsum('tk,ti->ki', stacked_taps, grad_conv_low, preferred_element_ty...  25.7 us
    dot_general x2, matrix products, one_sequence(): conv = jnp.dot(stacked_taps, conv_flat, preferred_element_type=jnp.float32)  23.6 us
    another operation x2, other arithmetic, shards(): jnp.stack(in_grads)  20.3 us
  transfers between devices with their start and end apart: 16, of which 6 were waited for; matrix products, arithmetic and copies ran while one was open for 36% of the time, Pallas kernels for 0%

commit v1 on v0

v1 whole, which is shorter than its diff:
```python
import functools
import jax
import jax.numpy as jnp
from jax import lax
from jax.experimental import pallas as pl
from jax.experimental.pallas import tpu as pltpu
from jax.sharding import PartitionSpec as P

KERNEL_TAPS = 5
DILATION_STEP = 16
EPS = 1e-05
LANES = 128
BORDER = KERNEL_TAPS // 2 * DILATION_STEP
F32 = jnp.float32
BF16 = jnp.bfloat16
VMEM_BYTES = 60 * 2**20

NN = (((1,), (0,)), ((), ()))
NT = (((1,), (1,)), ((), ()))


def params(steps=0):
    return pltpu.CompilerParams(
        dimension_semantics=("arbitrary",) * steps or None, vmem_limit_bytes=VMEM_BYTES
    )


def cost(flops, bytes_accessed):
    return pl.CostEstimate(flops=flops, bytes_accessed=bytes_accessed, transcendentals=0)


def shape(dims, dtype=BF16):
    return jax.ShapeDtypeStruct(dims, dtype)


def dot(left, right, dims=NN):
    return lax.dot_general(left, right, dims, preferred_element_type=F32)


def wide(column, lanes):
    return jnp.concatenate([column] * (lanes // LANES), axis=1)


def folded(values):
    total = values[:, :LANES]
    for at in range(LANES, values.shape[1], LANES):
        total = total + values[:, at : at + LANES]
    return total


def logistic(x):
    return 0.5 * jnp.tanh(0.5 * x) + 0.5


def vector(rows, block):
    return pl.BlockSpec((rows, LANES), lambda *_: (block, 0))


def here(rows, lanes, seq=0):
    return pl.BlockSpec((1, rows, lanes), lambda s, t: (s + seq, 0, t))


def held(dims):
    return pl.BlockSpec(dims, lambda *_: (0,) * len(dims))


def each(count, body, init, unroll=5):
    return lax.fori_loop(0, count, body, init, unroll=unroll)


def rows_at(index, size):
    return pl.ds(pl.multiple_of(index * size, size), size)


def row_stats(load, channels, chunk, lanes):
    steps = channels // chunk
    zero = jnp.zeros((chunk, lanes), F32)
    total = each(steps, lambda i, t: t + load(i), zero)
    mean = jnp.sum(total, axis=0, keepdims=True) * (1.0 / channels)

    def square(i, t):
        centred = load(i) - mean
        return t + centred * centred

    squares = each(steps, square, zero)
    spread = jnp.sum(squares, axis=0, keepdims=True) * (1.0 / channels)
    return mean, lax.rsqrt(spread + EPS)


def back_first(u, normed, gain, shift):
    pre = normed * gain + shift
    sigma = logistic(pre)
    p = u * (sigma * (1.0 + pre * (1.0 - sigma)))
    return pre, sigma, p, p * gain


def first_step():
    return (pl.program_id(0) == 0) & (pl.program_id(1) == 0)


def last_step():
    return (pl.program_id(0) == pl.num_programs(0) - 1) & (
        pl.program_id(1) == pl.num_programs(1) - 1
    )


def cleared(sums):
    @pl.when(first_step())
    def _():
        sums[...] = jnp.zeros_like(sums)


def handed(sums, out):
    @pl.when(last_step())
    def _():
        out[...] = sums[...]


def open_kernel(x, gain, shift, act1, stats, *, chunk):
    lanes, width = x.shape[2], x.shape[1]
    load = lambda i: x[0, rows_at(i, chunk), :].astype(F32)
    mean, scale = row_stats(load, width, chunk, lanes)

    def activate(i, carry):
        at = rows_at(i, chunk)
        normed = (load(i) - mean) * scale
        pre = normed * wide(gain[at, :], lanes) + wide(shift[at, :], lanes)
        act1[0, at, :] = (pre * logistic(pre)).astype(BF16)
        return carry

    each(width // chunk, activate, 0)
    stats[0] = jnp.concatenate([mean, scale, jnp.zeros((6, lanes), F32)], axis=0)


def open_block(x, vectors, lanes=512, chunk=32):
    seqs, width, length = x.shape
    return pl.pallas_call(
        functools.partial(open_kernel, chunk=chunk),
        grid=(seqs, length // lanes),
        in_specs=[here(width, lanes), vector(width, 0), vector(width, 1)],
        out_specs=[here(width, lanes), here(8, lanes)],
        out_shape=[shape(x.shape), shape((seqs, 8, length), F32)],
        compiler_params=params(2),
        cost_estimate=cost(40 * x.size, 4 * x.size),
        name="open_block",
    )(x, vectors, vectors)


def enter_kernel(act1, w_in, gain, shift, act2, turned, normed2, stats, proj, *, chunk):
    lanes, inner = act1.shape[2], act2.shape[1]
    proj[...] = dot(w_in[...], act1[0])
    load = lambda i: proj[rows_at(i, chunk), :]
    mean, scale = row_stats(load, inner, chunk, lanes)

    def activate(i, carry):
        at = rows_at(i, chunk)
        normed = (load(i) - mean) * scale
        normed2[0, at, :] = normed
        pre = normed * wide(gain[at, :], lanes) + wide(shift[at, :], lanes)
        act2[0, at, :] = (pre * logistic(pre)).astype(BF16)
        return carry

    each(inner // chunk, activate, 0)
    turned[0] = act2[0].T
    stats[0] = jnp.concatenate([scale, jnp.zeros((7, lanes), F32)], axis=0)


def enter(act1, w_in_t, vectors, lanes=512, chunk=32):
    seqs, width, length = act1.shape
    inner = w_in_t.shape[0]
    return pl.pallas_call(
        functools.partial(enter_kernel, chunk=chunk),
        grid=(seqs, length // lanes),
        in_specs=[here(width, lanes), held((inner, width)), vector(inner, 6), vector(inner, 7)],
        out_specs=[
            here(inner, lanes),
            pl.BlockSpec((1, lanes, inner), lambda s, t: (s, t, 0)),
            here(inner, lanes),
            here(8, lanes),
        ],
        out_shape=[
            shape((seqs, inner, length)),
            shape((seqs, length, inner)),
            shape((seqs, inner, length), F32),
            shape((seqs, 8, length), F32),
        ],
        scratch_shapes=[pltpu.VMEM((inner, lanes), F32)],
        compiler_params=params(2),
        cost_estimate=cost(2 * act1.size * inner, seqs * length * (2 * width + 8 * inner)),
        name="enter",
    )(act1, w_in_t, vectors, vectors)


def project_kernel(weight, columns, out, grads, sums, *, chunk):
    cleared(sums)
    out[0] = dot(weight[...], columns[0])

    def body(i, carry):
        at = rows_at(i, chunk)
        sums[at, :] += folded(columns[0, at, :].astype(F32))
        return carry

    each(columns.shape[1] // chunk, body, 0)
    handed(sums, grads)


def project(weight, columns, lanes=512, chunk=32):
    seqs, depth, length = columns.shape
    rows = weight.shape[0]
    return pl.pallas_call(
        functools.partial(project_kernel, chunk=chunk),
        grid=(seqs, length // lanes),
        in_specs=[held((rows, depth)), here(depth, lanes)],
        out_specs=[here(rows, lanes), held((depth, LANES))],
        out_shape=[shape((seqs, rows, length), F32), shape((depth, LANES), F32)],
        scratch_shapes=[pltpu.VMEM((depth, LANES), F32)],
        compiler_params=params(2),
        cost_estimate=cost(2 * columns.size * rows, seqs * length * (2 * depth + 4 * rows)),
        name="project",
    )(weight, columns)


def extend(rows, before, after, mask, whole, masked, seq, sign):
    length = rows.shape[1]
    whole[:BORDER, :] = before[seq]
    whole[BORDER : BORDER + length, :] = rows[seq]
    whole[BORDER + length :, :] = after[seq]
    inner = rows.shape[2]
    chunk = 128
    for later in range(KERNEL_TAPS // 2):
        by = sign * (later + 1) * DILATION_STEP

        def body(i, carry, later=later, by=by):
            kept = mask[seq, later, rows_at(i, chunk), :]
            kept = jnp.concatenate([kept] * -(-inner // LANES), axis=1)[:, :inner]
            start = pl.multiple_of(i * chunk + BORDER + by, DILATION_STEP)
            masked[later, rows_at(i, chunk), :] = whole[pl.ds(start, chunk), :] * kept
            return carry

        each(length // chunk, body, 0, 1)


def tap_rows(whole, masked, tap, sign, start, count):
    by = (tap - KERNEL_TAPS // 2) * DILATION_STEP
    if by > 0:
        return masked[tap - KERNEL_TAPS // 2 - 1, pl.ds(start, count), :]
    return whole[pl.ds(start + (BORDER + sign * by), count), :]


def conv_kernel(rows, before, after, mask, w_conv, gain, shift, upstream, act3, turned, grads, whole, masked, conv, scaled, low, sums, *, chunk):
    tile = pl.program_id(1)
    lanes, inner = act3.shape[2], act3.shape[1]
    cleared(sums)

    @pl.when(tile == 0)
    def _():
        extend(rows, before, after, mask, whole, masked, 0, 1)

    start = pl.multiple_of(tile * lanes, lanes)
    total = None
    for tap in range(KERNEL_TAPS):
        part = dot(w_conv[tap], tap_rows(whole, masked, tap, 1, start, lanes), NT)
        total = part if total is None else total + part
    conv[...] = total
    load = lambda i: conv[rows_at(i, chunk), :]
    mean, scale = row_stats(load, inner, chunk, lanes)

    def first(i, carry):
        at = rows_at(i, chunk)
        normed = (load(i) - mean) * scale
        gains = wide(gain[at, :], lanes)
        pre, sigma, p, q = back_first(upstream[0, at, :], normed, gains, wide(shift[at, :], lanes))
        act3[0, at, :] = (pre * sigma).astype(BF16)
        conv[at, :] = normed
        scaled[at, :] = q
        sums[0, at, :] += folded(p * normed)
        sums[1, at, :] += folded(p)
        return carry[0] + q, carry[1] + q * normed

    zero = jnp.zeros((chunk, lanes), F32)
    one, two = each(inner // chunk, first, (zero, zero))
    one = jnp.sum(one, axis=0, keepdims=True) * (1.0 / inner)
    two = jnp.sum(two, axis=0, keepdims=True) * (1.0 / inner)

    def second(i, carry):
        at = rows_at(i, chunk)
        low[at, :] = (scale * (scaled[at, :] - one - conv[at, :] * two)).astype(BF16)
        return carry

    each(inner // chunk, second, 0)
    turned[0] = low[...].T
    handed(sums, grads)


def conv_block(rows, before, after, mask, w_conv_t, vectors, upstream, lanes=512, chunk=16):
    seqs, length, inner = rows.shape
    seq = lambda *dims: pl.BlockSpec((1, *dims), lambda s, t: (s,) + (0,) * len(dims))
    return pl.pallas_call(
        functools.partial(conv_kernel, chunk=chunk),
        grid=(seqs, length // lanes),
        in_specs=[
            seq(length, inner),
            seq(BORDER, inner),
            seq(BORDER, inner),
            seq(2, length, LANES),
            held(w_conv_t.shape),
            vector(inner, 8),
            vector(inner, 9),
            here(inner, lanes),
        ],
        out_specs=[
            here(inner, lanes),
            pl.BlockSpec((1, lanes, inner), lambda s, t: (s, t, 0)),
            held((2, inner, LANES)),
        ],
        out_shape=[
            shape((seqs, inner, length)),
            shape((seqs, length, inner)),
            shape((2, inner, LANES), F32),
        ],
        scratch_shapes=[
            pltpu.VMEM((length + 2 * BORDER, inner), BF16),
            pltpu.VMEM((KERNEL_TAPS // 2, length, inner), BF16),
            pltpu.VMEM((inner, lanes), F32),
            pltpu.VMEM((inner, lanes), F32),
            pltpu.VMEM((inner, lanes), BF16),
            pltpu.VMEM((2, inner, LANES), F32),
        ],
        compiler_params=params(2),
        cost_estimate=cost(2 * rows.size * w_conv_t.size // inner, 12 * rows.size),
        name="conv_block",
    )(rows, before, after, mask, w_conv_t, vectors, vectors, upstream)


def conv_back_kernel(rows, before, after, mask, w_conv, gain, shift, normed2, stats, *rest, chunk):
    out, grads, whole, masked, grad, scaled, sums = rest[-7:]
    tile = pl.program_id(1)
    lanes, inner = out.shape[2], out.shape[1]
    cleared(sums)

    @pl.when(tile == 0)
    def _():
        extend(rows, before, after, mask, whole, masked, 0, -1)

    start = pl.multiple_of(tile * lanes, lanes)
    total = None
    for tap in range(KERNEL_TAPS):
        part = dot(w_conv[tap], tap_rows(whole, masked, tap, -1, start, lanes), NT)
        total = part if total is None else total + part
    grad[...] = total
    scale = stats[0, 0:1, :]

    def first(i, carry):
        at = rows_at(i, chunk)
        normed = normed2[0, at, :]
        _, _, p, q = back_first(
            grad[at, :], normed, wide(gain[at, :], lanes), wide(shift[at, :], lanes)
        )
        scaled[at, :] = q
        sums[0, at, :] += folded(p * normed)
        sums[1, at, :] += folded(p)
        return carry[0] + q, carry[1] + q * normed

    zero = jnp.zeros((chunk, lanes), F32)
    one, two = each(inner // chunk, first, (zero, zero))
    one = jnp.sum(one, axis=0, keepdims=True) * (1.0 / inner)
    two = jnp.sum(two, axis=0, keepdims=True) * (1.0 / inner)

    def second(i, carry):
        at = rows_at(i, chunk)
        out[0, at, :] = (scale * (scaled[at, :] - one - normed2[0, at, :] * two)).astype(BF16)
        return carry

    each(inner // chunk, second, 0)
    handed(sums, grads)


def conv_back(rows, before, after, mask, w_conv, vectors, normed2, stats, first, count, into=None, lanes=512, chunk=16):
    seqs, length, inner = rows.shape
    seq = lambda *dims: pl.BlockSpec((1, *dims), lambda s, t: (s + first,) + (0,) * len(dims))
    more = () if into is None else (into,)
    return pl.pallas_call(
        functools.partial(conv_back_kernel, chunk=chunk),
        grid=(count, length // lanes),
        in_specs=[
            seq(length, inner),
            seq(BORDER, inner),
            seq(BORDER, inner),
            seq(2, length, LANES),
            held(w_conv.shape),
            vector(inner, 6),
            vector(inner, 7),
            here(inner, lanes, first),
            here(8, lanes, first),
        ]
        + [pl.BlockSpec(memory_space=pl.ANY)] * len(more),
        out_specs=[here(inner, lanes, first), held((2, inner, LANES))],
        input_output_aliases={9: 0} if more else {},
        out_shape=[shape((seqs, inner, length)), shape((2, inner, LANES), F32)],
        scratch_shapes=[
            pltpu.VMEM((length + 2 * BORDER, inner), BF16),
            pltpu.VMEM((KERNEL_TAPS // 2, length, inner), BF16),
            pltpu.VMEM((inner, lanes), F32),
            pltpu.VMEM((inner, lanes), F32),
            pltpu.VMEM((2, inner, LANES), F32),
        ],
        compiler_params=params(2),
        cost_estimate=cost(2 * rows.size * w_conv.size * count // (seqs * inner), 10 * rows.size * count // seqs),
        name="conv_back",
    )(rows, before, after, mask, w_conv, vectors, vectors, normed2, stats, *more)


def leave_kernel(low, w_in, x, g, gain, shift, stats, *rest, chunk):
    out, grads, grad, sums = rest[-4:]
    lanes, width = out.shape[2], out.shape[1]
    cleared(sums)
    grad[...] = dot(w_in[...], low[0])
    mean = stats[0, 0:1, :]
    scale = stats[0, 1:2, :]
    norm = lambda at: (x[0, at, :].astype(F32) - mean) * scale

    def first(i, carry):
        at = rows_at(i, chunk)
        normed = norm(at)
        _, _, p, q = back_first(
            grad[at, :], normed, wide(gain[at, :], lanes), wide(shift[at, :], lanes)
        )
        grad[at, :] = q
        sums[0, at, :] += folded(p * normed)
        sums[1, at, :] += folded(p)
        return carry[0] + q, carry[1] + q * normed

    zero = jnp.zeros((chunk, lanes), F32)
    one, two = each(width // chunk, first, (zero, zero))
    one = jnp.sum(one, axis=0, keepdims=True) * (1.0 / width)
    two = jnp.sum(two, axis=0, keepdims=True) * (1.0 / width)

    def second(i, carry):
        at = rows_at(i, chunk)
        branch = scale * (grad[at, :] - one - norm(at) * two)
        out[0, at, :] = (g[0, at, :].astype(F32) + branch).astype(BF16)
        return carry

    each(width // chunk, second, 0)
    handed(sums, grads)


def leave(low, w_in, x, g, vectors, stats, first, count, into=None, lanes=512, chunk=16):
    seqs, inner, length = low.shape
    width = x.shape[1]
    more = () if into is None else (into,)
    return pl.pallas_call(
        functools.partial(leave_kernel, chunk=chunk),
        grid=(count, length // lanes),
        in_specs=[
            here(inner, lanes, first),
            held((width, inner)),
            here(width, lanes, first),
            here(width, lanes, first),
            vector(width, 0),
            vector(width, 1),
            here(8, lanes, first),
        ]
        + [pl.BlockSpec(memory_space=pl.ANY)] * len(more),
        input_output_aliases={7: 0} if more else {},
        out_specs=[here(width, lanes, first), held((2, width, LANES))],
        out_shape=[shape(x.shape), shape((2, width, LANES), F32)],
        scratch_shapes=[pltpu.VMEM((width, lanes), F32), pltpu.VMEM((2, width, LANES), F32)],
        compiler_params=params(2),
        cost_estimate=cost(2 * low.size * width * count // seqs, (2 * low.size + 6 * x.size) * count // seqs),
        name="leave",
    )(low, w_in, x, g, vectors, vectors, stats, *more)


def finish_kernel(w_out, act3, x, bias, *rest, chunk):
    out, proj = rest[-2:]
    lanes, width = out.shape[2], out.shape[1]
    proj[...] = dot(w_out[...], act3[0])

    def body(i, carry):
        at = rows_at(i, chunk)
        out[0, at, :] = (x[0, at, :].astype(F32) + proj[at, :] + wide(bias[at, :], lanes)).astype(BF16)
        return carry

    each(width // chunk, body, 0)


def finish(w_out_t, act3, x, vectors, first, count, into=None, lanes=512, chunk=32):
    more = () if into is None else (into,)
    seqs, inner, length = act3.shape
    width = x.shape[1]
    return pl.pallas_call(
        functools.partial(finish_kernel, chunk=chunk),
        grid=(count, length // lanes),
        in_specs=[held((width, inner)), here(inner, lanes, first), here(width, lanes, first), vector(width, 2)]
        + [pl.BlockSpec(memory_space=pl.ANY)] * len(more),
        input_output_aliases={4: 0} if more else {},
        out_specs=here(width, lanes, first),
        out_shape=shape(x.shape),
        scratch_shapes=[pltpu.VMEM((width, lanes), F32)],
        compiler_params=params(2),
        cost_estimate=cost(2 * act3.size * width * count // seqs, (2 * act3.size + 4 * x.size) * count // seqs),
        name="finish",
    )(w_out_t, act3, x, vectors, *more)


def outer_kernel(at, left, right, *rest, count):
    got, outs, total = rest[:-3] if count else (), rest[-3:-1] if count else rest[-2:-1], rest[-1]
    value = None
    for s in range(left.shape[0]):
        part = dot(left[s], right[s], NT)
        value = part if value is None else value + part
    if not count:
        outs[0][...] = value.astype(BF16)
        return
    total[...] = value + got[0][...].astype(F32)
    rows = outs[0].shape[0]
    for step, out in enumerate(outs):
        start = pl.multiple_of((at[1] ^ step) * rows, 8)
        out[...] = total[pl.ds(start, rows), :].astype(BF16)


def outer(at, left, right, got=None):
    seqs, height, length = left.shape
    width = right.shape[1]
    half = height // 2
    specs = [
        pl.BlockSpec((seqs, half, length), lambda i, at: (0, at[0], 0)),
        pl.BlockSpec((seqs, width, length), lambda i, at: (0, 0, 0)),
    ]
    if got is None:
        outs, out_specs = shape((half, width)), held((half, width))
    else:
        specs.append(held((half, width)))
        outs = [shape((half // 2, width))] * 2
        out_specs = [held((half // 2, width))] * 2
    return pl.pallas_call(
        functools.partial(outer_kernel, count=0 if got is None else 2),
        grid_spec=pltpu.PrefetchScalarGridSpec(
            num_scalar_prefetch=1,
            grid=(1,),
            in_specs=specs,
            out_specs=out_specs,
            scratch_shapes=[pltpu.VMEM((half, width) if got is not None else (8, LANES), F32)],
        ),
        out_shape=outs,
        compiler_params=params(1),
        cost_estimate=cost(seqs * length * height * width, 2 * seqs * length * (height + width)),
        name="outer",
    )(at, left, right, *(() if got is None else (got,)))


def outer_taps_kernel(at, left, rows, before, after, mask, *rest, first, groups, keep):
    got = rest[0] if keep else None
    outs = rest[1:3] if keep else rest[: len(groups)]
    whole, masked, total = rest[-3:]
    seqs, length = rows.shape[0], rows.shape[1]
    for seq in range(seqs):
        extend(rows, before, after, mask, whole.at[seq], masked.at[seq], seq, -1)
    places = [(group, i) for group, size in enumerate(groups) for i in range(size)]
    for step, (group, i) in enumerate(places):
        value = None
        for seq in range(seqs):
            right = tap_rows(whole.at[seq], masked.at[seq], first + step, -1, 0, length)
            part = dot(left[seq], right)
            value = part if value is None else value + part
        if not keep:
            outs[group][i] = value.astype(BF16)
            continue
        total[...] = value + got[i].astype(F32)
        size = outs[0].shape[1]
        for place, out in enumerate(outs):
            start = pl.multiple_of((at[1] ^ place) * size, 8)
            out[i] = total[pl.ds(start, size), :].astype(BF16)


def outer_taps(at, left, rows, before, after, mask, first, groups, got=None):
    seqs, length, inner = rows.shape
    half = inner // 2
    keep = got is not None
    specs = [
        pl.BlockSpec((seqs, half, length), lambda i, at: (0, at[0], 0)),
        held(rows.shape),
        held(before.shape),
        held(after.shape),
        held(mask.shape),
    ]
    if keep:
        specs.append(held((groups[0], half, inner)))
        dims = [(groups[0], half // 2, inner)] * 2
    else:
        dims = [(count, half, inner) for count in groups]
    return pl.pallas_call(
        functools.partial(outer_taps_kernel, first=first, groups=groups, keep=keep),
        grid_spec=pltpu.PrefetchScalarGridSpec(
            num_scalar_prefetch=1,
            grid=(1,),
            in_specs=specs,
            out_specs=[held(d) for d in dims],
            scratch_shapes=[
                pltpu.VMEM((seqs, length + 2 * BORDER, inner), BF16),
                pltpu.VMEM((seqs, KERNEL_TAPS // 2, length, inner), BF16),
                pltpu.VMEM((half, inner), F32),
            ],
        ),
        out_shape=[shape(d) for d in dims],
        compiler_params=params(1),
        cost_estimate=cost(rows.size * inner * sum(groups), 4 * rows.size),
        name="outer_taps",
    )(at, left, rows, before, after, mask, *((got,) if keep else ()))


def flip_kernel(w, out):
    for tap in range(w.shape[0]):
        out[tap] = w[tap].T


def flip(w):
    taps, rows, columns = w.shape
    return pl.pallas_call(
        flip_kernel,
        out_shape=shape((taps, columns, rows)),
        compiler_params=params(),
        cost_estimate=cost(0, 4 * w.size),
        name="flip",
    )(w)


def assemble_kernel(at, own, mine, other, natural, turned, whole, *, gap):
    rows, half = own.shape[0], mine.shape[1]
    whole[pl.ds(pl.multiple_of(at[0] * rows, 8), rows), :] = own[...].astype(F32)
    for step in range(mine.shape[0]):
        for pieces, core in ((mine, at[1]), (other, 1 - at[1])):
            start = (at[0] ^ (step + 1)) * rows + core * (rows - half)
            whole[pl.ds(pl.multiple_of(start, 8), half), :] = pieces[step].astype(F32)
    natural[...] = whole[...].astype(BF16)
    turned[...] = natural[...].T


def assemble(at, own, mine, other):
    rows, columns = own.shape
    full = rows * (mine.shape[0] + 1)
    dims = [(full, columns), (columns, full)]
    return pl.pallas_call(
        functools.partial(assemble_kernel, gap=0),
        grid_spec=pltpu.PrefetchScalarGridSpec(
            num_scalar_prefetch=1,
            grid=(1,),
            in_specs=[held(own.shape), held(mine.shape), held(other.shape)],
            out_specs=[held(d) for d in dims],
            scratch_shapes=[pltpu.VMEM((full, columns), F32)],
        ),
        out_shape=[shape(d) for d in dims],
        compiler_params=params(1),
        cost_estimate=cost(0, 6 * full * columns),
        name="assemble",
    )(at, own, mine, other)


def join_kernel(pieces, natural, turned, whole, *, rows):
    count, half = pieces.shape[0], pieces.shape[3]
    for shard in range(count):
        for core in range(2):
            start = shard * rows + core * (rows - half)
            whole[start : start + half, :] = pieces[shard, core, 0].astype(F32)
    natural[0] = whole[...].astype(BF16)
    turned[0] = natural[0].T


def join(pieces, rows):
    count, cores, taps, half, columns = pieces.shape
    full = count * rows
    dims = [(taps, full, columns), (taps, columns, full)]
    return pl.pallas_call(
        functools.partial(join_kernel, rows=rows),
        grid=(taps,),
        in_specs=[pl.BlockSpec((count, cores, 1, half, columns), lambda t: (0, 0, t, 0, 0))],
        out_specs=[pl.BlockSpec((1, *d[1:]), lambda t: (t, 0, 0)) for d in dims],
        out_shape=[shape(d) for d in dims],
        scratch_shapes=[pltpu.VMEM((full, columns), F32)],
        compiler_params=params(1),
        cost_estimate=cost(0, 6 * taps * full * columns),
        name="join",
    )(pieces)


def spread_kernel(at, parts, out, rows, *, sizes):
    count = parts.shape[0]
    for i in range(count):
        rows[pl.ds(at[0] ^ i, 1), :] = parts[i : i + 1, :]
    start, base = 0, 0
    for size in sizes:
        for shard in range(count):
            row = rows[shard : shard + 1, start : start + size]
            out[base : base + size, :] = jnp.broadcast_to(row, (LANES, size)).T
            base += size
        start += size


def spread(at, parts, sizes):
    total = parts.size
    return pl.pallas_call(
        functools.partial(spread_kernel, sizes=sizes),
        grid_spec=pltpu.PrefetchScalarGridSpec(
            num_scalar_prefetch=1,
            grid=(1,),
            in_specs=[held(parts.shape)],
            out_specs=held((total, LANES)),
            scratch_shapes=[pltpu.VMEM(parts.shape, F32)],
        ),
        out_shape=shape((total, LANES), F32),
        compiler_params=params(1),
        cost_estimate=cost(0, 4 * LANES * total),
        name="spread",
    )(at, parts)


def after(value, *others):
    return lax.optimization_barrier((value, *others))[0] if others else value


def swapped(x):
    return lax.ppermute(x, "core", [(0, 1), (1, 0)])


def from_ws(x, bit):
    return lax.ppermute(x, "ws", [(i, i ^ bit) for i in range(lax.axis_size("ws"))])


def neighbours(first, last):
    runs = lax.axis_size("run") * 2
    up = [(i, i + 1) for i in range(runs - 1)]
    down = [(i + 1, i) for i in range(runs - 1)]
    return lax.ppermute(last, ("run", "core"), up), lax.ppermute(first, ("run", "core"), down)


def square():
    return lax.axis_size("ws") == 4 and lax.axis_size("run") == 4


def halved(rows):
    return -(-rows // 16) * 8


def fetched(shard):
    rows = shard.shape[0]
    half = halved(rows)
    own = lax.dynamic_slice_in_dim(shard, lax.axis_index("core") * (rows - half), half, axis=0)
    return [from_ws(own, bit) for bit in (1, 2, 3)]


def whole_weight(at, shard, pieces):
    if pieces is None:
        natural = lax.all_gather(shard, "ws", axis=0, tiled=True)
        return natural, flip(natural[None])[0]
    mine = jnp.stack(pieces)
    return assemble(at, shard, mine, swapped(mine))


def conv_weights(shard):
    taps, rows, columns = shard.shape
    half = halved(rows)
    own = lax.dynamic_slice_in_dim(shard, lax.axis_index("core") * (rows - half), half, axis=1)
    pieces = lax.all_gather(own, ("ws", "core"), axis=0)
    return pieces.reshape(-1, 2, taps, half, columns)


def summed(*terms):
    total = terms[0].astype(F32)
    for term in terms[1:]:
        total = total + term.astype(F32)
    return total.astype(BF16)


def active(shard):
    return shard >> 1


class Share:
    def __init__(self, first, second):
        self.sum, self.second, self.came = first, second, ()

    def land(self, *kernels):
        came = after(self.came, *kernels)
        if self.second is None and self.last:
            run = lax.axis_index("run")
            self.sum = jnp.where((run == 1) | (run == 2), self.sum, came[0])
        else:
            self.sum = summed(self.sum, *came)
        self.second = None
        return self.sum

    def spread(self):
        near = [(2 * i + active(i), 2 * (i ^ 1) + active(i)) for i in range(4)]
        far = lambda bit: [(2 * i + 1 - active(i), 2 * (i ^ bit) + 1 - active(i)) for i in range(4)]
        move = lambda x, pairs: lax.ppermute(x, ("ws", "core"), pairs)
        self.came = (move(self.second, near), move(self.sum, far(2)), move(self.second, far(3)))

    def along(self, *pairs):
        every = []
        for shard in range(4):
            every += [((shard * 4 + i) * 2 + active(shard), (shard * 4 + j) * 2 + active(shard)) for i, j in pairs]
        self.came = (lax.ppermute(self.sum, ("ws", "run", "core"), every),)

    def inward(self):
        self.along((0, 1), (3, 2))
        self.last = False

    def middle(self):
        self.along((1, 2), (2, 1))

    def outward(self):
        self.along((1, 0), (2, 3))
        self.last = True

    def both(self):
        shard, core = lax.axis_index("ws"), lax.axis_index("core")
        pairs = [(2 * i + active(i), 2 * i + 1 - active(i)) for i in range(4)]
        other = lax.ppermute(self.sum, ("ws", "core"), pairs)
        return jnp.where(core == active(shard), self.sum, other).astype(F32)


def plain(low, high, axis):
    whole = jnp.concatenate([low, high], axis=axis)
    owned = lax.psum_scatter(whole, "ws", scatter_dimension=axis, tiled=True)
    return lax.psum(owned, ("run", "core")).astype(F32)


def small_sums(sums):
    if not square():
        return lax.psum(sums, ("ws", "run", "core"))
    sums = sums + swapped(sums)
    for axis, bit in (("ws", 1), ("ws", 2), ("run", 1), ("run", 2)):
        sums = sums + lax.ppermute(sums, axis, [(i, i ^ bit) for i in range(4)])
    return sums


def shards(
    inputs,
    cotangent,
    block_ids,
    first_gain,
    first_shift,
    weight_in,
    second_gain,
    second_shift,
    weight_conv,
    third_gain,
    third_shift,
    weight_out,
    output_bias,
):
    x = inputs.transpose(0, 2, 1)
    g = cotangent.transpose(0, 2, 1)
    count, shard, core = lax.axis_size("ws"), lax.axis_index("ws"), lax.axis_index("core")
    easy = square()
    place = jnp.stack([shard, core])
    owned_vectors = (first_gain, first_shift, output_bias, second_gain, second_shift, third_gain, third_shift)
    sizes = tuple(own.size for own in owned_vectors)
    flat = jnp.concatenate(owned_vectors)
    if easy:
        parts = jnp.stack([flat, *[from_ws(flat, bit) for bit in (1, 2, 3)]]).astype(F32)
        vectors = spread(place, parts, sizes)
    else:
        parts = lax.all_gather(flat, "ws", axis=0).astype(F32)
        vectors = spread(jnp.zeros_like(place), parts, sizes)
    in_pieces = fetched(weight_in) if easy else None
    own_conv = conv_weights(weight_conv) if easy else None
    length = block_ids.shape[1]
    ids_before, ids_after = neighbours(block_ids[:, :BORDER], block_ids[:, -BORDER:])
    ids = jnp.concatenate([ids_before, block_ids, ids_after], axis=1)
    same = lambda by: ids[:, BORDER + by : BORDER + by + length] == block_ids
    steps = [DILATION_STEP * (i + 1) for i in range(KERNEL_TAPS // 2)]

    def masks(sign):
        both = jnp.stack([same(sign * by) for by in steps], axis=1)
        return jnp.broadcast_to(both[..., None], (*both.shape, LANES)).astype(BF16)

    mask, mask_back = masks(1), masks(-1)
    act1, stats1 = open_block(x, vectors)
    if easy:
        in_pieces = after(in_pieces, act1)
        out_pieces = fetched(after(weight_out, *in_pieces))
    else:
        out_pieces = None
    w_in, w_in_t = whole_weight(place, weight_in, in_pieces)
    act2, rows2, normed2, stats2 = enter(act1, w_in_t, vectors)
    halo2 = neighbours(rows2[:, :BORDER], rows2[:, -BORDER:])
    if easy:
        out_pieces = after(out_pieces, act2)
    w_out, w_out_t = whole_weight(place, weight_out, out_pieces)
    grad_act3, bias_sums = project(w_out, g)
    if easy:
        w_conv, w_conv_t = join(after(own_conv, grad_act3), weight_conv.shape[1])
    else:
        w_conv = lax.all_gather(weight_conv, "ws", axis=1, tiled=True)
        w_conv_t = flip(w_conv)
    halo2 = after(halo2, grad_act3)
    act3, rows3, sums3 = conv_block(rows2, *halo2, mask, w_conv_t, vectors, grad_act3)
    halo = neighbours(rows3[:, :BORDER], rows3[:, -BORDER:])
    bit = shard & 1
    give, keep = jnp.stack([1 - core, bit]), jnp.stack([core, bit])
    if not easy:
        give, keep = jnp.zeros_like(give), jnp.ones_like(keep)
    seqs = x.shape[0]
    back = lambda rows, seq, number, into: conv_back(
        rows, *halo, mask_back, w_conv, vectors, normed2, stats2, seq, number, into
    )
    close = lambda low, seq, number, into: leave(low, w_in, x, g, vectors, stats1, seq, number, into)
    if not easy:
        taps = (act2, rows3, *halo, mask_back)
        out_grad = plain(outer(give, act3, g), outer(keep, act3, g), 0)
        (low,), (high,) = outer_taps(give, *taps, 0, (5,)), outer_taps(keep, *taps, 0, (5,))
        conv_grad = plain(low, high, 1)
        low2, sums2 = back(rows3, 0, seqs, None)
        in_grad = plain(outer(give, act1, low2), outer(keep, act1, low2), 0)
        input_grad, sums1 = close(low2, 0, seqs, None)
        block_output = finish(w_out_t, act3, x, vectors, 0, seqs)
    else:
        out_send = outer(give, act3, g)
        halo = after(halo, out_send)
        taps = (act2, rows3, *halo, mask_back)
        send_a, send_b = outer_taps(give, *taps, 0, (3, 2))
        got_out = swapped(out_send)
        got_a, got_b = swapped(send_a), swapped(send_b)
        out = Share(*outer(keep, act3, g, after(got_out, send_a)))
        out.spread()
        got_a, got_b = after((got_a, got_b), out.sum)
        tap_a = Share(*outer_taps(keep, *taps, 0, (3,), got_a))
        tap_a.spread()
        tap_b = Share(*outer_taps(keep, *after(taps, tap_a.sum), 3, (2,), got_b))
        tap_b.spread()
        out.land(tap_b.sum)
        out.inward()
        low2, sums2a = back(after(rows3, tap_b.sum, out.sum), 0, 1, None)
        out.land(sums2a)
        out.middle()
        tap_a.land(sums2a)
        tap_a.inward()
        low2, sums2b = back(after(rows3, sums2a, out.sum, tap_a.sum), 1, seqs - 1, low2)
        sums2 = sums2a + sums2b
        tap_b.land(sums2b)
        tap_b.inward()
        in_send = outer(give, *after((act1, low2), tap_b.sum))
        got_in = swapped(in_send)
        out.land(in_send)
        out.outward()
        tap_a.land(in_send)
        tap_a.middle()
        block_output = finish(*after((w_out_t, act3), in_send, out.sum, tap_a.sum), x, vectors, 0, 1)
        inner = Share(*outer(keep, act1, low2, after(got_in, block_output)))
        inner.spread()
        tap_b.land(inner.sum)
        tap_b.middle()
        out.land(inner.sum)
        input_grad, sums1a = close(after(low2, inner.sum, tap_b.sum), 0, 1, None)
        inner.land(sums1a)
        inner.inward()
        tap_a.land(sums1a)
        tap_a.outward()
        input_grad, sums1b = close(after(low2, inner.sum, tap_a.sum), 1, seqs - 1, input_grad)
        sums1 = sums1a + sums1b
        inner.land(sums1b)
        inner.middle()
        tap_b.land(sums1b)
        tap_b.outward()
        tap_a.land(sums1b)
        block_output = finish(
            *after((w_out_t, act3), sums1b, inner.sum, tap_b.sum), x, vectors, 1, seqs - 1, block_output
        )
        inner.land(block_output)
        inner.outward()
        tap_b.land(block_output)
        out_grad = out.both()
        conv_grad = jnp.concatenate([tap_a.both(), tap_b.both()], axis=0)
        inner.land()
        in_grad = inner.both()

    totals = [s.sum(axis=-1) for s in (sums1[0], sums1[1], bias_sums, sums2[0], sums2[1], sums3[0], sums3[1])]
    small = small_sums(jnp.concatenate([t.reshape(count, -1) for t in totals], axis=1))
    small = lax.dynamic_index_in_dim(small, shard, axis=0, keepdims=False)
    at, vector_grads = 0, []
    for size in sizes:
        vector_grads.append(small[at : at + size])
        at += size
    gain1, shift1, bias, gain2, shift2, gain3, shift3 = vector_grads
    return (
        block_output.transpose(0, 2, 1),
        input_grad.transpose(0, 2, 1),
        gain1,
        shift1,
        in_grad,
        gain2,
        shift2,
        conv_grad,
        gain3,
        shift3,
        out_grad,
        bias,
    )


def solution(mesh):
    count, runs = mesh.devices.shape
    split = jax.sharding.Mesh(mesh.devices.reshape(count, runs // 2, 2), ("ws", "run", "core"))
    tokens = P("ws", ("run", "core"), None)
    rows = P("ws", None)
    taps = P(None, "ws", None)
    placed = (tokens, tokens, P("ws", ("run", "core")), P("ws"), P("ws"), rows, P("ws"), P("ws"), taps)
    placed += (P("ws"), P("ws"), rows, P("ws"))
    given = (tokens, tokens, P("ws"), P("ws"), rows, P("ws"), P("ws"), taps, P("ws"), P("ws"), rows, P("ws"))
    return jax.shard_map(shards, mesh=split, in_specs=placed, out_specs=given, check_vma=False)
```

time: 597 us -> 483 us (0.81)
  Pallas kernels: 0 us -> 259 us
  matrix products: 153 us -> 0 us
  waiting for transfers between devices: 203 us -> 53.8 us
  starting transfers between devices: 19.5 us -> 94.1 us
  other arithmetic: 110 us -> 36.6 us
  blocking collectives: 49.6 us -> 0 us
  local copies, waits for them, and re-layouts: 33.1 us -> 17.2 us
    pallas_call x0 -> x21, Pallas kernels: none -> 259 us  [the longest x2 36.6 us: conv_back(): pl.pallas_call(functools.partial(conv_back_kernel, chunk=chunk), grid=(co...]
    dot_general x18 -> x0, matrix products: 153 us -> none  [the longest x2 25.9 us: one_sequence(): jnp.einsum('ti,ki->tk', grad_conv_low, conv_flat, preferred_element_type=...]
    unnamed x10 -> x1, waiting for transfers between devices: 75.8 us -> 0.02 us
    ppermute x9 -> x54, starting transfers between devices: 19.3 us -> 94.1 us  [the longest x12 28 us: along(): self.came = (lax.ppermute(self.sum, ('ws', 'run', 'core'), every),)]
    psum x1 -> x0, waiting for transfers between devices: 70.7 us -> none  [shards(): lax.psum(shortened(totals), 'ctx')]
    all_gather x3 -> x1, waiting for transfers between devices: 56.8 us -> 0.02 us  [conv_weights(): pieces = lax.all_gather(own, ('ws', 'core'), axis=0)]
    ppermute x9 -> x54, waiting for transfers between devices: 0.02 us -> 53.7 us  [the longest x9 22.7 us: from_ws(): lax.ppermute(x, 'ws', [(i, i ^ bit) for i in range(lax.axis_size('ws'))])]
    another operation x5 -> x6, other arithmetic: 37.3 us -> 2.15 us  [the longest x2 1.17 us: shards(): give, keep = (jnp.stack([1 - core, bit]), jnp.stack([core, bit]))]
  transfers between devices with their start and end apart: 16 -> 55, of which waited for: 6 -> 9; matrix products, arithmetic and copies ran while one was open for 36% -> 8% of each run, Pallas kernels for 0% -> 42%
where the time goes in v1:
time: 483 us; the launch traced here: 477 us
  Pallas kernels  259 us (54%)
  starting transfers between devices  94.1 us (19%)
  waiting for transfers between devices  53.8 us (11%)
  other arithmetic  36.6 us (8%)
  local copies, waits for them, and re-layouts  17.2 us (4%)
  between operations  15.6 us (3%)
    pallas_call x2, Pallas kernels, conv_back(): pl.pallas_call(functools.partial(conv_back_kernel, chunk=chunk), grid=(co...  36.6 us
    pallas_call x3, Pallas kernels, outer_taps(): pl.pallas_call(functools.partial(outer_taps_kernel, first=first, groups=g...  35.5 us
    pallas_call x2, Pallas kernels, leave(): pl.pallas_call(functools.partial(leave_kernel, chunk=chunk), grid=(count,...  34.9 us
    pallas_call x1, Pallas kernels, conv_block(): pl.pallas_call(functools.partial(conv_kernel, chunk=chunk), grid=(seqs, l...  34.5 us
    pallas_call x4, Pallas kernels, outer(): pl.pallas_call(functools.partial(outer_kernel, count=0 if got is None els...  34 us
    ppermute x12, starting transfers between devices, along(): self.came = (lax.ppermute(self.sum, ('ws', 'run', 'core'), every),)  28 us
    ppermute x9, waiting for transfers between devices, from_ws(): lax.ppermute(x, 'ws', [(i, i ^ bit) for i in range(lax.axis_size('ws'))])  22.7 us
    ppermute x12, starting transfers between devices, spread(): move = lambda x, pairs: lax.ppermute(x, ('ws', 'core'), pairs)  22 us
  transfers between devices with their start and end apart: 55, of which 9 were waited for; matrix products, arithmetic and copies ran while one was open for 8% of the time, Pallas kernels for 42%

profile of v1, /device:TPU:0, one launch (start us, length us, event | category | flops | bytes accessed | tf_op | source)
XLA Modules:
  0.0 476.5 jit_solution(14859874189972513162)
XLA Ops:
  9.9 4.0 collective-permute-start.5
  14.6 2.9 collective-permute-start.2
  18.7 10.7 %collective-permute-done.4 = bf16[2000]{0:T(1024)(128)(2,1)S(1)} collective-permute-done((bf16[2000]{0:T(1024)(128)(2,1)S(1)}, bf16[2000]{0:T(1024)(128)(2,1)S(1)}, u32[]{:S(2)}, u32[]{:S(2)}) %collective-permute-start.4) | collective-permute-done | bytes 4032 | tf_op jit(solution)/shard_map/ppermute | solution.py:727
  29.4 11.9 %collective-permute-done.3 = bf16[2000]{0:T(1024)(128)(2,1)S(1)} collective-permute-done((bf16[2000]{0:T(1024)(128)(2,1)S(1)}, bf16[2000]{0:T(1024)(128)(2,1)S(1)}, u32[]{:S(2)}, u32[]{:S(2)}) %collective-permute-start.3) | collective-permute-done | bytes 4032 | tf_op jit(solution)/shard_map/ppermute | solution.py:727
  42.0 4.9 %spread.1.gain.shift.bias = f32[8000,128]{1,0:T(8,128)} custom-call(s32[2]{0:T(128)} %pad_add_fusion.1.at, f32[4,2000]{1,0:T(4,128)} %maximum_convert_fusion.1.parts), custom_call_target="tpu_custom_call" | custom-call | bytes 4096000 | tf_op jit(solution)/shard_map/spread/pallas_call | solution.py:702
  46.9 12.5 %open_block.1 = (bf16[2,1600,1024]{2,1,0:T(8,128)(2,1)}, f32[2,8,1024]{2,1,0:T(8,128)}) custom-call(bf16[2,1600,1024]{2,1,0:T(8,128)(2,1)} %bitcast.30, f32[8000,128]{1,0:T(8,128)} %spread.1.gain.shift.bias, f32[8000,128]{1,0:T(8,128)} %spread.1.gain.shift.bias), custom_call_target="tpu_custom_call" | custom-call | flops 131072000 | bytes 13107200 | tf_op jit(solution)/shard_map/open_block/pallas_call | solution.py:137
  60.6 3.4 collective-permute-start.8
  65.0 6.0 %assemble.2 = (bf16[1600,800]{1,0:T(8,128)(2,1)}, bf16[800,1600]{1,0:T(8,128)(2,1)}) custom-call(s32[2]{0:T(128)} %pad_add_fusion.1.at, bf16[400,800]{1,0:T(8,128)(2,1)} %own.2, bf16[3,200,800]{2,1,0:T(8,128)(2,1)} %copy-done.2, bf16[3,200,800]{2,1,0:T(8,128)(2,1)} %copy-done.13), custom_call_target="tpu_custom_call" | custom-call | bytes 7680000 | tf_op jit(solution)/shard_map/assemble/pallas_call | solution.py:644
  70.9 15.8 %enter.1 = (bf16[2,800,1024]{2,1,0:T(8,128)(2,1)}, bf16[2,1024,800]{2,1,0:T(8,128)(2,1)}, f32[2,800,1024]{2,1,0:T(8,128)}, f32[2,8,1024]{2,1,0:T(8,128)}) custom-call(bf16[2,1600,1024]{2,1,0:T(8,128)(2,1)} %get-tuple-element.158.act1.left, bf16[800,1600]{1,0:T(8,128)(2,1)} %get-tuple-element.106.w_in, f32[8000,128]{1,0:T(8,128)} %spread.1.gain.shift.bias, ...), custom_call_target="tpu_custom_call" | custom-call | flops 5242880000 | bytes 19660800 | tf_op jit(solution)/shard_map/enter/pallas_call | solution.py:171
  87.5 2.0 collective-permute-start.16
  91.4 2.2 collective-permute-done.13
  94.8 4.3 collective-permute-start.11
  99.0 1.5 collective-permute-start.12
  101.5 5.9 %assemble.3 = (bf16[800,1600]{1,0:T(8,128)(2,1)}, bf16[1600,800]{1,0:T(8,128)(2,1)}) custom-call(s32[2]{0:T(128)} %pad_add_fusion.1.at, bf16[200,1600]{1,0:T(8,128)(2,1)} %own.3, bf16[3,104,1600]{2,1,0:T(8,128)(2,1)} %copy-done.3, bf16[3,104,1600]{2,1,0:T(8,128)(2,1)} %copy-done.14), custom_call_target="tpu_custom_call" | custom-call | bytes 7680000 | tf_op jit(solution)/shard_map/assemble/pallas_call | solution.py:644
  107.4 11.7 %project.1 = (f32[2,800,1024]{2,1,0:T(8,128)}, f32[1600,128]{1,0:T(8,128)}) custom-call(bf16[800,1600]{1,0:T(8,128)(2,1)} %get-tuple-element.113.weight, bf16[2,1600,1024]{2,1,0:T(8,128)(2,1)} %bitcast.35), custom_call_target="tpu_custom_call" | custom-call | flops 5242880000 | bytes 13107200 | tf_op jit(solution)/shard_map/project/pallas_call | solution.py:210
  119.2 9.6 %join.1 = (bf16[5,800,800]{2,1,0:T(8,128)(2,1)}, bf16[5,800,800]{2,1,0:T(8,128)(2,1)}) custom-call(bf16[4,2,5,104,800]{4,3,2,1,0:T(8,128)(2,1)} %bitcast.41), custom_call_target="tpu_custom_call" | custom-call | bytes 19200000 | tf_op jit(solution)/shard_map/join/pallas_call | solution.py:674
  128.8 1.6 broadcast_in_dim.4.mask
  130.4 34.5 %conv_block.1 = (bf16[2,800,1024]{2,1,0:T(8,128)(2,1)}, bf16[2,1024,800]{2,1,0:T(8,128)(2,1)}, f32[2,800,128]{2,1,0:T(8,128)}) custom-call(bf16[2,1024,800]{2,1,0:T(8,128)(2,1)} %get-tuple-element.112.rows, bf16[2,32,800]{2,1,0:T(8,128)(2,1)} %copy-done.34, bf16[2,32,800]{2,1,0:T(8,128)(2,1)} %copy-done.35, bf16[2,2,1024,128]{3,2,1,0:T(8,128)(2,1)} %broadcast_in_dim.4.mask, ...), custom_call_target="tpu_custom_call" | custom-call | flops 13107200000 | bytes 19660800 | tf_op jit(solution)/shard_map/conv_block/pallas_call | solution.py:298
  165.9 3.0 collective-permute-start.14
  168.9 1.7 collective-permute-start.15
  170.6 8.3 %outer.4 = bf16[400,1600]{1,0:T(8,128)(2,1)} custom-call(s32[2]{0:T(128)} %pad_add_fusion.3.at, bf16[2,800,1024]{2,1,0:T(8,128)(2,1)} %get-tuple-element.182.left.act3, bf16[2,1600,1024]{2,1,0:T(8,128)(2,1)} %bitcast.36), custom_call_target="tpu_custom_call" | custom-call | flops 2621440000 | bytes 9830400 | tf_op jit(solution)/shard_map/outer/pallas_call | solution.py:537
  178.9 1.6 broadcast_in_dim.5.mask
  180.5 14.4 %outer_taps.3 = (bf16[3,400,800]{2,1,0:T(8,128)(2,1)}, bf16[2,400,800]{2,1,0:T(8,128)(2,1)}) custom-call(s32[2]{0:T(128)} %pad_add_fusion.3.at, bf16[2,800,1024]{2,1,0:T(8,128)(2,1)} %get-tuple-element.129.left, bf16[2,1024,800]{2,1,0:T(8,128)(2,1)} %get-tuple-element.150.rows, bf16[2,32,800]{2,1,0:T(8,128)(2,1)} %copy-done.21, ...), custom_call_target="tpu_custom_call" | custom-call | flops 6553600000 | bytes 6553600 | tf_op jit(solution)/shard_map/outer_taps/pallas_call | solution.py:593
  194.9 2.2 collective-permute-start.17
  198.2 6.4 %collective-permute-done.19.rest_0_ = bf16[400,1600]{1,0:T(8,128)(2,1)S(1)} collective-permute-done((bf16[400,1600]{1,0:T(8,128)(2,1)S(1)}, bf16[400,1600]{1,0:T(8,128)(2,1)S(1)}, u32[]{:S(2)}, u32[]{:S(2)}) %collective-permute-start.19) | collective-permute-done | bytes 1280032 | tf_op jit(solution)/shard_map/ppermute | solution.py:723
  205.7 8.6 %outer.5 = (bf16[200,1600]{1,0:T(8,128)(2,1)}, bf16[200,1600]{1,0:T(8,128)(2,1)}) custom-call(s32[2]{0:T(128)} %pad_add_fusion.2.at, bf16[2,800,1024]{2,1,0:T(8,128)(2,1)} %get-tuple-element.182.left.act3, bf16[2,1600,1024]{2,1,0:T(8,128)(2,1)} %bitcast.37, bf16[400,1600]{1,0:T(8,128)(2,1)} %copy-done.11), custom_call_target="tpu_custom_call" | custom-call | flops 2621440000 | bytes 9830400 | tf_op jit(solution)/shard_map/outer/pallas_call | solution.py:537
  214.3 1.9 collective-permute-start.20
  217.5 1.5 collective-permute-start.22
  219.0 11.3 %outer_taps.4 = (bf16[3,200,800]{2,1,0:T(8,128)(2,1)}, bf16[3,200,800]{2,1,0:T(8,128)(2,1)}) custom-call(s32[2]{0:T(128)} %pad_add_fusion.2.at, bf16[2,800,1024]{2,1,0:T(8,128)(2,1)} %get-tuple-element.129.left, bf16[2,1024,800]{2,1,0:T(8,128)(2,1)} %get-tuple-element.150.rows, bf16[2,32,800]{2,1,0:T(8,128)(2,1)} %copy-done.21, ...), custom_call_target="tpu_custom_call" | custom-call | flops 3932160000 | bytes 6553600 | tf_op jit(solution)/shard_map/outer_taps/pallas_call | solution.py:593
  230.4 9.8 %outer_taps.5 = (bf16[2,200,800]{2,1,0:T(8,128)(2,1)}, bf16[2,200,800]{2,1,0:T(8,128)(2,1)}) custom-call(s32[2]{0:T(128)} %pad_add_fusion.2.at, bf16[2,800,1024]{2,1,0:T(8,128)(2,1)} %get-tuple-element.129.left, bf16[2,1024,800]{2,1,0:T(8,128)(2,1)} %get-tuple-element.150.rows, bf16[2,32,800]{2,1,0:T(8,128)(2,1)} %copy-done.21, ...), custom_call_target="tpu_custom_call" | custom-call | flops 2621440000 | bytes 6553600 | tf_op jit(solution)/shard_map/outer_taps/pallas_call | solution.py:593
  242.0 2.2 add_convert_fusion.11
  244.2 4.6 collective-permute-start.23
  250.5 4.0 collective-permute-start.24
  257.0 18.3 %conv_back.2 = (bf16[2,800,1024]{2,1,0:T(8,128)(2,1)}, f32[2,800,128]{2,1,0:T(8,128)}) custom-call(bf16[2,1024,800]{2,1,0:T(8,128)(2,1)} %get-tuple-element.150.rows, bf16[2,32,800]{2,1,0:T(8,128)(2,1)} %copy-done.21, bf16[2,32,800]{2,1,0:T(8,128)(2,1)} %copy-done.22, bf16[2,2,1024,128]{3,2,1,0:T(8,128)(2,1)} %broadcast_in_dim.5.mask, ...), custom_call_target="tpu_custom_call" | custom-call | flops 6553600000 | bytes 8192000 | tf_op jit(solution)/shard_map/conv_back/pallas_call | solution.py:382
  275.4 1.9 collective-permute-start.27
  278.5 1.5 collective-permute-start.29
  280.1 1.5 collective-permute-start.31
  281.6 2.4 add_convert_fusion.2
  284.1 3.5 collective-permute-start.32
  287.5 18.3 %conv_back.3 = (bf16[2,800,1024]{2,1,0:T(8,128)(2,1)}, f32[2,800,128]{2,1,0:T(8,128)}) custom-call(bf16[2,1024,800]{2,1,0:T(8,128)(2,1)} %get-tuple-element.150.rows, bf16[2,32,800]{2,1,0:T(8,128)(2,1)} %copy-done.21, bf16[2,32,800]{2,1,0:T(8,128)(2,1)} %copy-done.22, ...), custom_call_target="tpu_custom_call", output_to_operand_aliasing={{0}: (9, {})} | custom-call | flops 6553600000 | bytes 8192000 | tf_op jit(solution)/shard_map/conv_back/pallas_call | solution.py:382
  305.8 2.1 add_convert_fusion.8
  308.0 8.3 %outer.6 = bf16[800,800]{1,0:T(8,128)(2,1)} custom-call(s32[2]{0:T(128)} %pad_add_fusion.3.at, bf16[2,1600,1024]{2,1,0:T(8,128)(2,1)} %get-tuple-element.158.act1.left, bf16[2,800,1024]{2,1,0:T(8,128)(2,1)} %get-tuple-element.176.right.low), custom_call_target="tpu_custom_call" | custom-call | flops 2621440000 | bytes 9830400 | tf_op jit(solution)/shard_map/outer/pallas_call | solution.py:537
  318.1 2.3 collective-permute-start.36
  320.4 1.5 add.114
  326.1 1.5 add_convert_fusion.1
  327.6 1.9 collective-permute-start.37
  329.5 8.7 %finish.2.rest_0_ = bf16[2,1600,1024]{2,1,0:T(8,128)(2,1)} custom-call(bf16[1600,800]{1,0:T(8,128)(2,1)} %get-tuple-element.181.w_out, bf16[2,800,1024]{2,1,0:T(8,128)(2,1)} %get-tuple-element.182.left.act3, bf16[2,1600,1024]{2,1,0:T(8,128)(2,1)} %bitcast.31, f32[8000,128]{1,0:T(8,128)} %spread.1.gain.shift.bias), custom_call_target="tpu_custom_call" | custom-call | flops 2621440000 | bytes 8192000 | tf_op jit(solution)/shard_map/finish/pallas_call | solution.py:492
  338.2 8.9 %outer.7 = (bf16[400,800]{1,0:T(8,128)(2,1)}, bf16[400,800]{1,0:T(8,128)(2,1)}) custom-call(s32[2]{0:T(128)} %pad_add_fusion.2.at, bf16[2,1600,1024]{2,1,0:T(8,128)(2,1)} %get-tuple-element.158.act1.left, bf16[2,800,1024]{2,1,0:T(8,128)(2,1)} %get-tuple-element.176.right.low, bf16[800,800]{1,0:T(8,128)(2,1)} %collective-permute-done.30.rest_0_), custom_call_target="tpu_custom_call" | custom-call | flops 2621440000 | bytes 9830400 | tf_op jit(solution)/shard_map/outer/pallas_call | solution.py:537
  347.1 3.5 collective-permute-start.33
  354.5 1.6 collective-permute-start.39
  356.1 17.5 %leave.2 = (bf16[2,1600,1024]{2,1,0:T(8,128)(2,1)}, f32[2,1600,128]{2,1,0:T(8,128)}) custom-call(bf16[2,800,1024]{2,1,0:T(8,128)(2,1)} %get-tuple-element.176.right.low, bf16[1600,800]{1,0:T(8,128)(2,1)} %get-tuple-element.169.w_in, bf16[2,1600,1024]{2,1,0:T(8,128)(2,1)} %bitcast.32, bf16[2,1600,1024]{2,1,0:T(8,128)(2,1)} %bitcast.38, ...), custom_call_target="tpu_custom_call" | custom-call | flops 2621440000 | bytes 11468800 | tf_op jit(solution)/shard_map/leave/pallas_call | solution.py:452
  374.8 7.8 %collective-permute-start.53 = (bf16[200,1600]{1,0:T(8,128)(2,1)S(1)}, bf16[200,1600]{1,0:T(8,128)(2,1)}, u32[]{:S(2)}, u32[]{:S(2)}) collective-permute-start(bf16[200,1600]{1,0:T(8,128)(2,1)S(1)} %broadcast_select_fusion.5), channel_id=1, source_target_pairs={{0,1},{8,9},{17,16},{25,24},{2,3},{10,11},{19,18},{27,26},{4,5},{1... | collective-permute-start | bytes 1920008 | tf_op jit(solution)/shard_map/ppermute | solution.py:819
  382.7 2.8 add_convert_fusion.6
  385.4 1.5 add_convert_fusion
  386.9 17.5 %leave.3 = (bf16[2,1600,1024]{2,1,0:T(8,128)(2,1)}, f32[2,1600,128]{2,1,0:T(8,128)}) custom-call(bf16[2,800,1024]{2,1,0:T(8,128)(2,1)} %get-tuple-element.176.right.low, bf16[1600,800]{1,0:T(8,128)(2,1)} %get-tuple-element.169.w_in, bf16[2,1600,1024]{2,1,0:T(8,128)(2,1)} %bitcast.33, ...), custom_call_target="tpu_custom_call", output_to_operand_aliasing={{0}: (7, {})} | custom-call | flops 2621440000 | bytes 11468800 | tf_op jit(solution)/shard_map/leave/pallas_call | solution.py:452
  404.4 2.1 add.113
  409.9 5.7 %collective-permute-start.38 = (bf16[400,800]{1,0:T(8,128)(2,1)}, bf16[400,800]{1,0:T(8,128)(2,1)S(1)}, u32[]{:S(2)}, u32[]{:S(2)}) collective-permute-start(bf16[400,800]{1,0:T(8,128)(2,1)} %add_convert_fusion.6), channel_id=1, source_target_pairs={{0,2},{6,4},{8,10},{14,12},{17,19},{23,21},{25,27},{31,29}} | collective-permute-start | bytes 1920008 | tf_op jit(solution)/shard_map/ppermute | solution.py:803
  419.6 2.2 collective-permute-start.43
  424.5 10.1 %collective-permute-done.43 = f32[4,2000]{1,0:T(4,128)S(1)} collective-permute-done((f32[4,2000]{1,0:T(4,128)S(1)}, f32[4,2000]{1,0:T(4,128)S(1)}, u32[]{:S(2)}, u32[]{:S(2)}) %collective-permute-start.43) | collective-permute-done | bytes 32032 | tf_op jit(solution)/shard_map/ppermute | solution.py:834
  435.9 1.8 collective-permute-start.45
  437.8 1.8 collective-permute-done.44
  439.6 8.7 %finish.3 = bf16[2,1600,1024]{2,1,0:T(8,128)(2,1)} custom-call(bf16[1600,800]{1,0:T(8,128)(2,1)} %get-tuple-element.181.w_out, bf16[2,800,1024]{2,1,0:T(8,128)(2,1)} %get-tuple-element.182.left.act3, bf16[2,1600,1024]{2,1,0:T(8,128)(2,1)} %bitcast.34, f32[8000,128]{1,0:T(8,128)} %spread.1.gain.shift.bias, ...), custom_call_target="tpu_custom_call", output_to_operand_aliasing={{}: (4, {})} | custom-call | flops 2621440000 | bytes 8192000 | tf_op jit(solution)/shard_map/finish/pallas_call | solution.py:492
  456.4 7.8 %collective-permute-done.46 = bf16[400,800]{1,0:T(8,128)(2,1)S(1)} collective-permute-done((bf16[400,800]{1,0:T(8,128)(2,1)S(1)}, bf16[400,800]{1,0:T(8,128)(2,1)S(1)}, u32[]{:S(2)}, u32[]{:S(2)}) %collective-permute-start.46) | collective-permute-done | bytes 640032 | tf_op jit(solution)/shard_map/ppermute | solution.py:803
  465.9 2.0 maximum_convert_fusion
  (207 shorter events, 57.4 us)
Async XLA Ops:
  7.3 111.9 %all-gather.3.cloned.1.call-start = ((), (), s32[]{:S(2)}) async-start(), calls=%async_computation | async-start | bytes 8386560 | tf_op jit(solution)/shard_map/all_gather | solution.py:764
  9.9 8.1 %collective-permute-start.5 = (bf16[2000]{0:T(1024)(128)(2,1)S(1)}, bf16[2000]{0:T(1024)(128)(2,1)S(1)}, u32[]{:S(2)}, u32[]{:S(2)}) collective-permute-start(bf16[2000]{0:T(1024)(128)(2,1)S(1)} %concatenate.21), channel_id=1, source_target_pairs={{0,24},{8,16},{16,8},{24,0},{1,25},{9,17},{17,9},{25,1},{2,26},{10... | collective-permute-start | bytes 12008 | tf_op jit(solution)/shard_map/ppermute | solution.py:727
  13.9 45.4 %collective-permute-start = (bf16[200,800]{1,0:T(8,128)(2,1)S(1)}, bf16[200,800]{1,0:T(8,128)(2,1)S(1)}, u32[]{:S(2)}, u32[]{:S(2)}) collective-permute-start(bf16[200,800]{1,0:T(8,128)(2,1)S(1)} %constant_dynamic-slice_fusion.2), channel_id=1, source_target_pairs={{0,8},{8,0},{16,24},{24,16},{1,9},{9,1},{17,25},{25,17},{2,10},{10... | collective-permute-start | bytes 960008 | tf_op jit(solution)/shard_map/ppermute | solution.py:727
  14.5 44.8 %collective-permute-start.1 = (bf16[200,800]{1,0:T(8,128)(2,1)S(1)}, bf16[200,800]{1,0:T(8,128)(2,1)S(1)}, u32[]{:S(2)}, u32[]{:S(2)}) collective-permute-start(bf16[200,800]{1,0:T(8,128)(2,1)S(1)} %constant_dynamic-slice_fusion.2), channel_id=1, source_target_pairs={{0,16},{8,24},{16,0},{24,8},{1,17},{9,25},{17,1},{25,9},{2,18},{10... | collective-permute-start | bytes 960008 | tf_op jit(solution)/shard_map/ppermute | solution.py:727
  14.6 44.8 %collective-permute-start.2 = (bf16[200,800]{1,0:T(8,128)(2,1)S(1)}, bf16[200,800]{1,0:T(8,128)(2,1)S(1)}, u32[]{:S(2)}, u32[]{:S(2)}) collective-permute-start(bf16[200,800]{1,0:T(8,128)(2,1)S(1)} %constant_dynamic-slice_fusion.2), channel_id=1, source_target_pairs={{0,24},{8,16},{16,8},{24,0},{1,25},{9,17},{17,9},{25,1},{2,26},{10... | collective-permute-start | bytes 960008 | tf_op jit(solution)/shard_map/ppermute | solution.py:727
  17.4 11.9 %collective-permute-start.4 = (bf16[2000]{0:T(1024)(128)(2,1)S(1)}, bf16[2000]{0:T(1024)(128)(2,1)S(1)}, u32[]{:S(2)}, u32[]{:S(2)}) collective-permute-start(bf16[2000]{0:T(1024)(128)(2,1)S(1)} %concatenate.21), channel_id=1, source_target_pairs={{0,16},{8,24},{16,0},{24,8},{1,17},{9,25},{17,1},{25,9},{2,18},{10... | collective-permute-start | bytes 12008 | tf_op jit(solution)/shard_map/ppermute | solution.py:727
  18.0 23.4 %collective-permute-start.3 = (bf16[2000]{0:T(1024)(128)(2,1)S(1)}, bf16[2000]{0:T(1024)(128)(2,1)S(1)}, u32[]{:S(2)}, u32[]{:S(2)}) collective-permute-start(bf16[2000]{0:T(1024)(128)(2,1)S(1)} %concatenate.21), channel_id=1, source_target_pairs={{0,8},{8,0},{16,24},{24,16},{1,9},{9,1},{17,25},{25,17},{2,10},{10... | collective-permute-start | bytes 12008 | tf_op jit(solution)/shard_map/ppermute | solution.py:727
  59.5 4.5 collective-permute-start.9
  60.4 26.3 %collective-permute-start.6 = (bf16[104,1600]{1,0:T(8,128)(2,1)S(1)}, bf16[104,1600]{1,0:T(8,128)(2,1)S(1)}, u32[]{:S(2)}, u32[]{:S(2)}) collective-permute-start(bf16[104,1600]{1,0:T(8,128)(2,1)S(1)} %constant_dynamic-slice_fusion.1), channel_id=1, source_target_pairs={{0,8},{8,0},{16,24},{24,16},{1,9},{9,1},{17,25},{25,17},{2,10},{10... | collective-permute-start | bytes 998408 | tf_op jit(solution)/shard_map/ppermute | solution.py:727
  60.5 26.3 %collective-permute-start.7 = (bf16[104,1600]{1,0:T(8,128)(2,1)S(1)}, bf16[104,1600]{1,0:T(8,128)(2,1)S(1)}, u32[]{:S(2)}, u32[]{:S(2)}) collective-permute-start(bf16[104,1600]{1,0:T(8,128)(2,1)S(1)} %constant_dynamic-slice_fusion.1), channel_id=1, source_target_pairs={{0,16},{8,24},{16,0},{24,8},{1,17},{9,25},{17,1},{25,9},{2,18},{10... | collective-permute-start | bytes 998408 | tf_op jit(solution)/shard_map/ppermute | solution.py:727
  60.6 26.2 %collective-permute-start.8 = (bf16[104,1600]{1,0:T(8,128)(2,1)S(1)}, bf16[104,1600]{1,0:T(8,128)(2,1)S(1)}, u32[]{:S(2)}, u32[]{:S(2)}) collective-permute-start(bf16[104,1600]{1,0:T(8,128)(2,1)S(1)} %constant_dynamic-slice_fusion.1), channel_id=1, source_target_pairs={{0,24},{8,16},{16,8},{24,0},{1,25},{9,17},{17,9},{25,1},{2,26},{10... | collective-permute-start | bytes 998408 | tf_op jit(solution)/shard_map/ppermute | solution.py:727
  86.9 13.6 %copy-start.3 = (bf16[3,104,1600]{2,1,0:T(8,128)(2,1)}, bf16[3,104,1600]{2,1,0:T(8,128)(2,1)S(1)}, u32[]{:S(2)}) copy-start(bf16[3,104,1600]{2,1,0:T(8,128)(2,1)S(1)} %pad_maximum_fusion.1.mine) | copy-start | bytes 2995204
  87.0 13.6 %collective-permute-start.10 = (bf16[3,104,1600]{2,1,0:T(8,128)(2,1)S(1)}, bf16[3,104,1600]{2,1,0:T(8,128)(2,1)S(1)}, u32[]{:S(2)}, u32[]{:S(2)}) collective-permute-start(bf16[3,104,1600]{2,1,0:T(8,128)(2,1)S(1)} %pad_maximum_fusion.1.mine), channel_id=1, source_target_pairs={{0,1},{1,0},{2,3},{3,2},{4,5},{5,4},{6,7},{7,6},{8,9},{9,8},{10,11... | collective-permute-start | bytes 2995208 | tf_op jit(solution)/shard_map/ppermute | solution.py:723
  87.5 6.1 %collective-permute-start.16 = (s32[2,32]{1,0:T(2,128)S(1)}, s32[2,32]{1,0:T(2,128)S(1)}, u32[]{:S(2)}, u32[]{:S(2)}) collective-permute-start(s32[2,32]{1,0:T(2,128)S(1)} %get-tuple-element.213), channel_id=1, source_target_pairs={{0,1},{1,2},{2,3},{3,4},{4,5},{5,6},{6,7},{8,9},{9,10},{10,11},{11... | collective-permute-start | bytes 776 | tf_op jit(solution)/shard_map/ppermute | solution.py:734
  89.5 4.1 collective-permute-start.13
  94.8 24.4 %collective-permute-start.11 = (bf16[2,32,800]{2,1,0:T(8,128)(2,1)S(1)}, bf16[2,32,800]{2,1,0:T(8,128)(2,1)S(1)}, u32[]{:S(2)}, u32[]{:S(2)}) collective-permute-start(bf16[2,32,800]{2,1,0:T(8,128)(2,1)S(1)} %get-tuple-element.199), channel_id=1, source_target_pairs={{0,1},{1,2},{2,3},{3,4},{4,5},{5,6},{6,7},{8,9},{9,10},{10,11},{11... | collective-permute-start | bytes 307208 | tf_op jit(solution)/shard_map/ppermute | solution.py:734
  99.0 20.1 %collective-permute-start.12 = (bf16[2,32,800]{2,1,0:T(8,128)(2,1)S(1)}, bf16[2,32,800]{2,1,0:T(8,128)(2,1)S(1)}, u32[]{:S(2)}, u32[]{:S(2)}) collective-permute-start(bf16[2,32,800]{2,1,0:T(8,128)(2,1)S(1)} %get-tuple-element.198), channel_id=1, source_target_pairs={{1,0},{2,1},{3,2},{4,3},{5,4},{6,5},{7,6},{9,8},{10,9},{11,10},{12... | collective-permute-start | bytes 307208 | tf_op jit(solution)/shard_map/ppermute | solution.py:734
  119.2 9.6 %copy-start.34 = (bf16[2,32,800]{2,1,0:T(8,128)(2,1)}, bf16[2,32,800]{2,1,0:T(8,128)(2,1)S(1)}, u32[]{:S(2)}) copy-start(bf16[2,32,800]{2,1,0:T(8,128)(2,1)S(1)} %collective-permute-done.11.before) | copy-start | bytes 307204
  119.2 9.6 %copy-start.35 = (bf16[2,32,800]{2,1,0:T(8,128)(2,1)}, bf16[2,32,800]{2,1,0:T(8,128)(2,1)S(1)}, u32[]{:S(2)}) copy-start(bf16[2,32,800]{2,1,0:T(8,128)(2,1)S(1)} %collective-permute-done.12.after) | copy-start | bytes 307204
  165.9 13.0 %collective-permute-start.14 = (bf16[2,32,800]{2,1,0:T(8,128)(2,1)S(1)}, bf16[2,32,800]{2,1,0:T(8,128)(2,1)S(1)}, u32[]{:S(2)}, u32[]{:S(2)}) collective-permute-start(bf16[2,32,800]{2,1,0:T(8,128)(2,1)S(1)} %get-tuple-element.197), channel_id=1, source_target_pairs={{0,1},{1,2},{2,3},{3,4},{4,5},{5,6},{6,7},{8,9},{9,10},{10,11},{11... | collective-permute-start | bytes 307208 | tf_op jit(solution)/shard_map/ppermute | solution.py:734
  168.9 10.0 %collective-permute-start.15 = (bf16[2,32,800]{2,1,0:T(8,128)(2,1)S(1)}, bf16[2,32,800]{2,1,0:T(8,128)(2,1)S(1)}, u32[]{:S(2)}, u32[]{:S(2)}) collective-permute-start(bf16[2,32,800]{2,1,0:T(8,128)(2,1)S(1)} %get-tuple-element.196), channel_id=1, source_target_pairs={{1,0},{2,1},{3,2},{4,3},{5,4},{6,5},{7,6},{9,8},{10,9},{11,10},{12... | collective-permute-start | bytes 307208 | tf_op jit(solution)/shard_map/ppermute | solution.py:734
  180.5 16.6 %copy-start.10 = (bf16[400,1600]{1,0:T(8,128)(2,1)S(1)}, bf16[400,1600]{1,0:T(8,128)(2,1)}, u32[]{:S(2)}) copy-start(bf16[400,1600]{1,0:T(8,128)(2,1)} %outer.4) | copy-start | bytes 3840004
  194.9 24.1 %collective-permute-start.17 = (bf16[3,400,800]{2,1,0:T(8,128)(2,1)}, bf16[3,400,800]{2,1,0:T(8,128)(2,1)}, u32[]{:S(2)}, u32[]{:S(2)}) collective-permute-start(bf16[3,400,800]{2,1,0:T(8,128)(2,1)} %get-tuple-element.123), channel_id=1, source_target_pairs={{0,1},{1,0},{2,3},{3,2},{4,5},{5,4},{6,7},{7,6},{8,9},{9,8},{10,11... | collective-permute-start | bytes 5760008 | tf_op jit(solution)/shard_map/ppermute | solution.py:723
  197.1 7.5 %collective-permute-start.19 = (bf16[400,1600]{1,0:T(8,128)(2,1)S(1)}, bf16[400,1600]{1,0:T(8,128)(2,1)S(1)}, u32[]{:S(2)}, u32[]{:S(2)}) collective-permute-start(bf16[400,1600]{1,0:T(8,128)(2,1)S(1)} %copy-done.10), channel_id=1, source_target_pairs={{0,1},{1,0},{2,3},{3,2},{4,5},{5,4},{6,7},{7,6},{8,9},{9,8},{10,11... | collective-permute-start | bytes 3840008 | tf_op jit(solution)/shard_map/ppermute | solution.py:723
  197.1 21.9 %collective-permute-start.18 = (bf16[2,400,800]{2,1,0:T(8,128)(2,1)}, bf16[2,400,800]{2,1,0:T(8,128)(2,1)S(1)}, u32[]{:S(2)}, u32[]{:S(2)}) collective-permute-start(bf16[2,400,800]{2,1,0:T(8,128)(2,1)} %get-tuple-element.124), channel_id=1, source_target_pairs={{0,1},{1,0},{2,3},{3,2},{4,5},{5,4},{6,7},{7,6},{8,9},{9,8},{10,11... | collective-permute-start | bytes 3840008 | tf_op jit(solution)/shard_map/ppermute | solution.py:723
  214.3 25.8 %collective-permute-start.20 = (bf16[200,1600]{1,0:T(8,128)(2,1)}, bf16[200,1600]{1,0:T(8,128)(2,1)S(1)}, u32[]{:S(2)}, u32[]{:S(2)}) collective-permute-start(bf16[200,1600]{1,0:T(8,128)(2,1)} %get-tuple-element.136), channel_id=1, source_target_pairs={{0,8},{8,0},{17,25},{25,17},{2,10},{10,2},{19,27},{27,19},{4,12},{... | collective-permute-start | bytes 1920008 | tf_op jit(solution)/shard_map/ppermute | solution.py:796
  216.2 23.9 %collective-permute-start.21 = (bf16[200,1600]{1,0:T(8,128)(2,1)}, bf16[200,1600]{1,0:T(8,128)(2,1)S(1)}, u32[]{:S(2)}, u32[]{:S(2)}) collective-permute-start(bf16[200,1600]{1,0:T(8,128)(2,1)} %get-tuple-element.126), channel_id=1, source_target_pairs={{1,17},{9,25},{16,0},{24,8},{3,19},{11,27},{18,2},{26,10},{5,21},{... | collective-permute-start | bytes 1920008 | tf_op jit(solution)/shard_map/ppermute | solution.py:796
  217.5 22.6 %collective-permute-start.22 = (bf16[200,1600]{1,0:T(8,128)(2,1)}, bf16[200,1600]{1,0:T(8,128)(2,1)S(1)}, u32[]{:S(2)}, u32[]{:S(2)}) collective-permute-start(bf16[200,1600]{1,0:T(8,128)(2,1)} %get-tuple-element.136), channel_id=1, source_target_pairs={{1,25},{9,17},{16,8},{24,0},{3,27},{11,19},{18,10},{26,2},{5,29},{... | collective-permute-start | bytes 1920008 | tf_op jit(solution)/shard_map/ppermute | solution.py:796
  219.0 11.3 %copy-start.33 = (bf16[2,400,800]{2,1,0:T(8,128)(2,1)}, bf16[2,400,800]{2,1,0:T(8,128)(2,1)S(1)}, u32[]{:S(2)}) copy-start(bf16[2,400,800]{2,1,0:T(8,128)(2,1)S(1)} %collective-permute-done.18.rest_0_) | copy-start | bytes 3840004
  242.0 13.7 %copy-start.16 = (bf16[2,200,800]{2,1,0:T(8,128)(2,1)S(1)}, bf16[2,200,800]{2,1,0:T(8,128)(2,1)}, u32[]{:S(2)}) copy-start(bf16[2,200,800]{2,1,0:T(8,128)(2,1)} %get-tuple-element.135) | copy-start | bytes 1920004
  244.2 31.1 %collective-permute-start.23 = (bf16[200,1600]{1,0:T(8,128)(2,1)S(1)}, bf16[200,1600]{1,0:T(8,128)(2,1)}, u32[]{:S(2)}, u32[]{:S(2)}) collective-permute-start(bf16[200,1600]{1,0:T(8,128)(2,1)S(1)} %add_convert_fusion.11), channel_id=1, source_target_pairs={{0,2},{6,4},{8,10},{14,12},{17,19},{23,21},{25,27},{31,29}} | collective-permute-start | bytes 1920008 | tf_op jit(solution)/shard_map/ppermute | solution.py:803
  249.2 30.9 %collective-permute-start.25 = (bf16[3,200,800]{2,1,0:T(8,128)(2,1)S(1)}, bf16[3,200,800]{2,1,0:T(8,128)(2,1)}, u32[]{:S(2)}, u32[]{:S(2)}) collective-permute-start(bf16[3,200,800]{2,1,0:T(8,128)(2,1)S(1)} %copy-done.12), channel_id=1, source_target_pairs={{1,17},{9,25},{16,0},{24,8},{3,19},{11,27},{18,2},{26,10},{5,21},{... | collective-permute-start | bytes 2880008 | tf_op jit(solution)/shard_map/ppermute | solution.py:796
  250.5 28.1 %collective-permute-start.24 = (bf16[3,200,800]{2,1,0:T(8,128)(2,1)}, bf16[3,200,800]{2,1,0:T(8,128)(2,1)}, u32[]{:S(2)}, u32[]{:S(2)}) collective-permute-start(bf16[3,200,800]{2,1,0:T(8,128)(2,1)} %get-tuple-element.146), channel_id=1, source_target_pairs={{0,8},{8,0},{17,25},{25,17},{2,10},{10,2},{19,27},{27,19},{4,12},{... | collective-permute-start | bytes 2880008 | tf_op jit(solution)/shard_map/ppermute | solution.py:796
  254.4 27.2 %collective-permute-start.26 = (bf16[3,200,800]{2,1,0:T(8,128)(2,1)}, bf16[3,200,800]{2,1,0:T(8,128)(2,1)}, u32[]{:S(2)}, u32[]{:S(2)}) collective-permute-start(bf16[3,200,800]{2,1,0:T(8,128)(2,1)} %get-tuple-element.146), channel_id=1, source_target_pairs={{1,25},{9,17},{16,8},{24,0},{3,27},{11,19},{18,10},{26,2},{5,29},{... | collective-permute-start | bytes 2880008 | tf_op jit(solution)/shard_map/ppermute | solution.py:796
  255.7 50.1 %collective-permute-start.28 = (bf16[2,200,800]{2,1,0:T(8,128)(2,1)S(1)}, bf16[2,200,800]{2,1,0:T(8,128)(2,1)}, u32[]{:S(2)}, u32[]{:S(2)}) collective-permute-start(bf16[2,200,800]{2,1,0:T(8,128)(2,1)S(1)} %copy-done.16), channel_id=1, source_target_pairs={{1,17},{9,25},{16,0},{24,8},{3,19},{11,27},{18,2},{26,10},{5,21},{... | collective-permute-start | bytes 1920008 | tf_op jit(solution)/shard_map/ppermute | solution.py:796
  275.4 30.4 %collective-permute-start.27 = (bf16[2,200,800]{2,1,0:T(8,128)(2,1)}, bf16[2,200,800]{2,1,0:T(8,128)(2,1)}, u32[]{:S(2)}, u32[]{:S(2)}) collective-permute-start(bf16[2,200,800]{2,1,0:T(8,128)(2,1)} %get-tuple-element.153), channel_id=1, source_target_pairs={{0,8},{8,0},{17,25},{25,17},{2,10},{10,2},{19,27},{27,19},{4,12},{... | collective-permute-start | bytes 1920008 | tf_op jit(solution)/shard_map/ppermute | solution.py:796
  278.5 27.3 %collective-permute-start.29 = (bf16[2,200,800]{2,1,0:T(8,128)(2,1)}, bf16[2,200,800]{2,1,0:T(8,128)(2,1)}, u32[]{:S(2)}, u32[]{:S(2)}) collective-permute-start(bf16[2,200,800]{2,1,0:T(8,128)(2,1)} %get-tuple-element.153), channel_id=1, source_target_pairs={{1,25},{9,17},{16,8},{24,0},{3,27},{11,19},{18,10},{26,2},{5,29},{... | collective-permute-start | bytes 1920008 | tf_op jit(solution)/shard_map/ppermute | solution.py:796
  280.1 43.4 %collective-permute-start.31 = (bf16[200,1600]{1,0:T(8,128)(2,1)S(1)}, bf16[200,1600]{1,0:T(8,128)(2,1)}, u32[]{:S(2)}, u32[]{:S(2)}) collective-permute-start(bf16[200,1600]{1,0:T(8,128)(2,1)S(1)} %add_convert_fusion.10), channel_id=1, source_target_pairs={{2,4},{4,2},{10,12},{12,10},{19,21},{21,19},{27,29},{29,27}} | collective-permute-start | bytes 1920008 | tf_op jit(solution)/shard_map/ppermute | solution.py:803
  284.1 42.0 %collective-permute-start.32 = (bf16[3,200,800]{2,1,0:T(8,128)(2,1)S(1)}, bf16[3,200,800]{2,1,0:T(8,128)(2,1)}, u32[]{:S(2)}, u32[]{:S(2)}) collective-permute-start(bf16[3,200,800]{2,1,0:T(8,128)(2,1)S(1)} %add_convert_fusion.2), channel_id=1, source_target_pairs={{0,2},{6,4},{8,10},{14,12},{17,19},{23,21},{25,27},{31,29}} | collective-permute-start | bytes 2880008 | tf_op jit(solution)/shard_map/ppermute | solution.py:803
  307.9 10.1 %copy-start.4 = (bf16[2,200,800]{2,1,0:T(8,128)(2,1)}, bf16[2,200,800]{2,1,0:T(8,128)(2,1)S(1)}, u32[]{:S(2)}) copy-start(bf16[2,200,800]{2,1,0:T(8,128)(2,1)S(1)} %add_convert_fusion.8) | copy-start | bytes 1920004
  316.2 22.0 %collective-permute-start.30 = (bf16[800,800]{1,0:T(8,128)(2,1)}, bf16[800,800]{1,0:T(8,128)(2,1)}, u32[]{:S(2)}, u32[]{:S(2)}) collective-permute-start(bf16[800,800]{1,0:T(8,128)(2,1)} %outer.6), channel_id=1, source_target_pairs={{0,1},{1,0},{2,3},{3,2},{4,5},{5,4},{6,7},{7,6},{8,9},{9,8},{10,11... | collective-permute-start | bytes 3840008 | tf_op jit(solution)/shard_map/ppermute | solution.py:723
  318.1 33.9 %collective-permute-start.36 = (bf16[2,200,800]{2,1,0:T(8,128)(2,1)S(1)}, bf16[2,200,800]{2,1,0:T(8,128)(2,1)}, u32[]{:S(2)}, u32[]{:S(2)}) collective-permute-start(bf16[2,200,800]{2,1,0:T(8,128)(2,1)S(1)} %add_convert_fusion.8), channel_id=1, source_target_pairs={{0,2},{6,4},{8,10},{14,12},{17,19},{23,21},{25,27},{31,29}} | collective-permute-start | bytes 1920008 | tf_op jit(solution)/shard_map/ppermute | solution.py:803
  324.8 29.7 %collective-permute-start.52 = (bf16[200,1600]{1,0:T(8,128)(2,1)S(1)}, bf16[200,1600]{1,0:T(8,128)(2,1)}, u32[]{:S(2)}, u32[]{:S(2)}) collective-permute-start(bf16[200,1600]{1,0:T(8,128)(2,1)S(1)} %add_convert_fusion.9), channel_id=1, source_target_pairs={{2,0},{4,6},{10,8},{12,14},{19,17},{21,23},{27,25},{29,31}} | collective-permute-start | bytes 1920008 | tf_op jit(solution)/shard_map/ppermute | solution.py:803
  327.6 57.8 %collective-permute-start.37 = (bf16[3,200,800]{2,1,0:T(8,128)(2,1)S(1)}, bf16[3,200,800]{2,1,0:T(8,128)(2,1)}, u32[]{:S(2)}, u32[]{:S(2)}) collective-permute-start(bf16[3,200,800]{2,1,0:T(8,128)(2,1)S(1)} %add_convert_fusion.1), channel_id=1, source_target_pairs={{2,4},{4,2},{10,12},{12,10},{19,21},{21,19},{27,29},{29,27}} | collective-permute-start | bytes 2880008 | tf_op jit(solution)/shard_map/ppermute | solution.py:803
  338.2 15.0 %copy-start.5 = (bf16[2,200,800]{2,1,0:T(8,128)(2,1)S(1)}, bf16[2,200,800]{2,1,0:T(8,128)(2,1)}, u32[]{:S(2)}) copy-start(bf16[2,200,800]{2,1,0:T(8,128)(2,1)} %copy-done.4) | copy-start | bytes 1920004
  347.1 27.8 %collective-permute-start.33 = (bf16[400,800]{1,0:T(8,128)(2,1)}, bf16[400,800]{1,0:T(8,128)(2,1)}, u32[]{:S(2)}, u32[]{:S(2)}) collective-permute-start(bf16[400,800]{1,0:T(8,128)(2,1)} %get-tuple-element.166), channel_id=1, source_target_pairs={{0,8},{8,0},{17,25},{25,17},{2,10},{10,2},{19,27},{27,19},{4,12},{... | collective-permute-start | bytes 1920008 | tf_op jit(solution)/shard_map/ppermute | solution.py:796
  350.6 32.0 %collective-permute-start.35 = (bf16[400,800]{1,0:T(8,128)(2,1)}, bf16[400,800]{1,0:T(8,128)(2,1)}, u32[]{:S(2)}, u32[]{:S(2)}) collective-permute-start(bf16[400,800]{1,0:T(8,128)(2,1)} %get-tuple-element.166), channel_id=1, source_target_pairs={{1,25},{9,17},{16,8},{24,0},{3,27},{11,19},{18,10},{26,2},{5,29},{... | collective-permute-start | bytes 1920008 | tf_op jit(solution)/shard_map/ppermute | solution.py:796
  351.9 30.7 %collective-permute-start.34 = (bf16[400,800]{1,0:T(8,128)(2,1)}, bf16[400,800]{1,0:T(8,128)(2,1)}, u32[]{:S(2)}, u32[]{:S(2)}) collective-permute-start(bf16[400,800]{1,0:T(8,128)(2,1)} %get-tuple-element.165), channel_id=1, source_target_pairs={{1,17},{9,25},{16,0},{24,8},{3,19},{11,27},{18,2},{26,10},{5,21},{... | collective-permute-start | bytes 1920008 | tf_op jit(solution)/shard_map/ppermute | solution.py:796
  354.5 63.7 %collective-permute-start.39 = (bf16[2,200,800]{2,1,0:T(8,128)(2,1)S(1)}, bf16[2,200,800]{2,1,0:T(8,128)(2,1)}, u32[]{:S(2)}, u32[]{:S(2)}) collective-permute-start(bf16[2,200,800]{2,1,0:T(8,128)(2,1)S(1)} %add_convert_fusion.7), channel_id=1, source_target_pairs={{2,4},{4,2},{10,12},{12,10},{19,21},{21,19},{27,29},{29,27}} | collective-permute-start | bytes 1920008 | tf_op jit(solution)/shard_map/ppermute | solution.py:803
  356.1 17.5 %copy-start.7 = (bf16[200,1600]{1,0:T(8,128)(2,1)S(1)}, bf16[200,1600]{1,0:T(8,128)(2,1)}, u32[]{:S(2)}) copy-start(bf16[200,1600]{1,0:T(8,128)(2,1)} %copy-done.6) | copy-start | bytes 1920004
  374.8 40.9 %collective-permute-start.53 = (bf16[200,1600]{1,0:T(8,128)(2,1)S(1)}, bf16[200,1600]{1,0:T(8,128)(2,1)}, u32[]{:S(2)}, u32[]{:S(2)}) collective-permute-start(bf16[200,1600]{1,0:T(8,128)(2,1)S(1)} %broadcast_select_fusion.5), channel_id=1, source_target_pairs={{0,1},{8,9},{17,16},{25,24},{2,3},{10,11},{19,18},{27,26},{4,5},{1... | collective-permute-start | bytes 1920008 | tf_op jit(solution)/shard_map/ppermute | solution.py:819
  407.3 1.3 collective-permute-start.40
  408.6 7.0 %collective-permute-start.41 = (f32[4,2000]{1,0:T(4,128)S(1)}, f32[4,2000]{1,0:T(4,128)S(1)}, u32[]{:S(2)}, u32[]{:S(2)}) collective-permute-start(f32[4,2000]{1,0:T(4,128)S(1)} %add.115), channel_id=1, source_target_pairs={{0,8},{8,0},{16,24},{24,16},{1,9},{9,1},{17,25},{25,17},{2,10},{10... | collective-permute-start | bytes 96008 | tf_op jit(solution)/shard_map/ppermute | solution.py:834
  409.9 24.8 %collective-permute-start.38 = (bf16[400,800]{1,0:T(8,128)(2,1)}, bf16[400,800]{1,0:T(8,128)(2,1)S(1)}, u32[]{:S(2)}, u32[]{:S(2)}) collective-permute-start(bf16[400,800]{1,0:T(8,128)(2,1)} %add_convert_fusion.6), channel_id=1, source_target_pairs={{0,2},{6,4},{8,10},{14,12},{17,19},{23,21},{25,27},{31,29}} | collective-permute-start | bytes 1920008 | tf_op jit(solution)/shard_map/ppermute | solution.py:803
  415.6 4.0 collective-permute-start.42
  416.9 32.8 %collective-permute-start.48 = (bf16[3,200,800]{2,1,0:T(8,128)(2,1)S(1)}, bf16[3,200,800]{2,1,0:T(8,128)(2,1)}, u32[]{:S(2)}, u32[]{:S(2)}) collective-permute-start(bf16[3,200,800]{2,1,0:T(8,128)(2,1)S(1)} %add_convert_fusion), channel_id=1, source_target_pairs={{2,0},{4,6},{10,8},{12,14},{19,17},{21,23},{27,25},{29,31}} | collective-permute-start | bytes 2880008 | tf_op jit(solution)/shard_map/ppermute | solution.py:803
  419.6 14.9 %collective-permute-start.43 = (f32[4,2000]{1,0:T(4,128)S(1)}, f32[4,2000]{1,0:T(4,128)S(1)}, u32[]{:S(2)}, u32[]{:S(2)}) collective-permute-start(f32[4,2000]{1,0:T(4,128)S(1)} %add.117), channel_id=1, source_target_pairs={{0,2},{2,0},{4,6},{6,4},{1,3},{3,1},{5,7},{7,5},{8,10},{10,8},{12,... | collective-permute-start | bytes 96008 | tf_op jit(solution)/shard_map/ppermute | solution.py:834
  423.2 25.1 %collective-permute-start.50 = (bf16[2,200,800]{2,1,0:T(8,128)(2,1)S(1)}, bf16[2,200,800]{2,1,0:T(8,128)(2,1)S(1)}, u32[]{:S(2)}, u32[]{:S(2)}) collective-permute-start(bf16[2,200,800]{2,1,0:T(8,128)(2,1)S(1)} %add_convert_fusion.4), channel_id=1, source_target_pairs={{2,0},{4,6},{10,8},{12,14},{19,17},{21,23},{27,25},{29,31}} | collective-permute-start | bytes 1920008 | tf_op jit(solution)/shard_map/ppermute | solution.py:803
  434.6 5.0 %collective-permute-start.44 = (f32[4,2000]{1,0:T(4,128)S(1)}, f32[4,2000]{1,0:T(4,128)S(1)}, u32[]{:S(2)}, u32[]{:S(2)}) collective-permute-start(f32[4,2000]{1,0:T(4,128)S(1)} %add.118), channel_id=1, source_target_pairs={{0,4},{2,6},{4,0},{6,2},{1,5},{3,7},{5,1},{7,3},{8,12},{10,14},{12... | collective-permute-start | bytes 96008 | tf_op jit(solution)/shard_map/ppermute | solution.py:834
  435.9 13.8 %collective-permute-start.45 = (bf16[400,800]{1,0:T(8,128)(2,1)S(1)}, bf16[400,800]{1,0:T(8,128)(2,1)}, u32[]{:S(2)}, u32[]{:S(2)}) collective-permute-start(bf16[400,800]{1,0:T(8,128)(2,1)S(1)} %add_convert_fusion.5), channel_id=1, source_target_pairs={{2,4},{4,2},{10,12},{12,10},{19,21},{21,19},{27,29},{29,27}} | collective-permute-start | bytes 1920008 | tf_op jit(solution)/shard_map/ppermute | solution.py:803
  448.4 17.2 %collective-permute-start.51 = (bf16[2,200,800]{2,1,0:T(8,128)(2,1)S(1)}, bf16[2,200,800]{2,1,0:T(8,128)(2,1)S(1)}, u32[]{:S(2)}, u32[]{:S(2)}) collective-permute-start(bf16[2,200,800]{2,1,0:T(8,128)(2,1)S(1)} %broadcast_select_fusion.2), channel_id=1, source_target_pairs={{0,1},{8,9},{17,16},{25,24},{2,3},{10,11},{19,18},{27,26},{4,5},{1... | collective-permute-start | bytes 1920008 | tf_op jit(solution)/shard_map/ppermute | solution.py:819
  451.0 13.1 %collective-permute-start.46 = (bf16[400,800]{1,0:T(8,128)(2,1)S(1)}, bf16[400,800]{1,0:T(8,128)(2,1)S(1)}, u32[]{:S(2)}, u32[]{:S(2)}) collective-permute-start(bf16[400,800]{1,0:T(8,128)(2,1)S(1)} %add_convert_fusion.3), channel_id=1, source_target_pairs={{2,0},{4,6},{10,8},{12,14},{19,17},{21,23},{27,25},{29,31}} | collective-permute-start | bytes 1920008 | tf_op jit(solution)/shard_map/ppermute | solution.py:803
  453.7 12.0 %collective-permute-start.49 = (bf16[3,200,800]{2,1,0:T(8,128)(2,1)S(1)}, bf16[3,200,800]{2,1,0:T(8,128)(2,1)S(1)}, u32[]{:S(2)}, u32[]{:S(2)}) collective-permute-start(bf16[3,200,800]{2,1,0:T(8,128)(2,1)S(1)} %broadcast_select_fusion), channel_id=1, source_target_pairs={{0,1},{8,9},{17,16},{25,24},{2,3},{10,11},{19,18},{27,26},{4,5},{1... | collective-permute-start | bytes 2880008 | tf_op jit(solution)/shard_map/ppermute | solution.py:819
  464.3 3.7 collective-permute-start.47
  (27 other events, 71.5 us)
Sparse Core Ops, SparseCore 0:
  10.0 68.6 all-gather.2

commit v2 on v1

--- a/solution.py
+++ b/solution.py
@@ -26,7 +26,7 @@
 
 
 def cost(flops, bytes_accessed):
-    return pl.CostEstimate(flops=flops, bytes_accessed=bytes_accessed, transcendentals=0)
+    return pl.CostEstimate(flops=flops // 16, bytes_accessed=bytes_accessed // 16, transcendentals=0)
 
 
 def shape(dims, dtype=BF16):
@@ -499,115 +499,228 @@
         out_shape=shape(x.shape),
         scratch_shapes=[pltpu.VMEM((width, lanes), F32)],
         compiler_params=params(2),
-        cost_estimate=cost(2 * act3.size * width * count // seqs, (2 * act3.size + 4 * x.size) * count // seqs),
+        cost_estimate=cost(0, 0),
         name="finish",
     )(w_out_t, act3, x, vectors, *more)
 
 
-def outer_kernel(at, left, right, *rest, count):
-    got, outs, total = rest[:-3] if count else (), rest[-3:-1] if count else rest[-2:-1], rest[-1]
-    value = None
-    for s in range(left.shape[0]):
-        part = dot(left[s], right[s], NT)
-        value = part if value is None else value + part
-    if not count:
-        outs[0][...] = value.astype(BF16)
-        return
-    total[...] = value + got[0][...].astype(F32)
-    rows = outs[0].shape[0]
-    for step, out in enumerate(outs):
-        start = pl.multiple_of((at[1] ^ step) * rows, 8)
-        out[...] = total[pl.ds(start, rows), :].astype(BF16)
-
-
-def outer(at, left, right, got=None):
-    seqs, height, length = left.shape
-    width = right.shape[1]
-    half = height // 2
-    specs = [
-        pl.BlockSpec((seqs, half, length), lambda i, at: (0, at[0], 0)),
-        pl.BlockSpec((seqs, width, length), lambda i, at: (0, 0, 0)),
-    ]
+def grads_kernel(at, *refs, pair, taps, keep, units):
+    refs = list(refs)
+    take = lambda n: [refs.pop(0) for _ in range(n)]
+    sources = []
+    left = right = act2 = rows3 = before = after = mask = got = None
+    if pair:
+        left, right = take(2)
+    if taps:
+        act2, rows3, before, after, mask = take(5)
+    if keep:
+        (got,) = take(1)
+    outs = take(2 if keep else len(units))
+    sems = refs.pop(-1)
+    loads = []
+
+    def load(source, target):
+        copy = pltpu.make_async_copy(source, target, sems.at[len(loads)])
+        copy.start()
+        loads.append(copy)
+        return copy
+
+    if pair:
+        left_here, right_here = take(2)
+        half = left_here.shape[1]
+        columns = right_here.shape[1] // pair
+        first = [load(left.at[:, pl.ds(pl.multiple_of(at[0] * half, half), half), :], left_here)]
+        blocks = []
+        for i in range(pair):
+            span = pl.ds(i * columns, columns)
+            blocks.append(load(right.at[:, span, :], right_here.at[:, span, :]))
+    if taps:
+        act2_here, whole, mask_here, masked = take(4)
+        seqs, length = rows3.shape[0], rows3.shape[1]
+        half2 = act2_here.shape[1]
+        ready = [load(act2.at[:, pl.ds(pl.multiple_of(at[0] * half2, half2), half2), :], act2_here)]
+        for seq in range(seqs):
+            ready.append(load(rows3.at[seq], whole.at[seq, pl.ds(BORDER, length), :]))
+        ready.append(load(before, whole.at[:, pl.ds(0, BORDER), :]))
+        ready.append(load(after, whole.at[:, pl.ds(BORDER + length, BORDER), :]))
+        ready.append(load(mask, mask_here))
+    if keep:
+        got_here, total = take(2)
+        got_load = load(got, got_here)
+
+    def give(step, value):
+        if not keep:
+            place = step
+            for out, size in zip(outs, units):
+                if place < size:
+                    out[place] = value.astype(BF16)
+                    return
+                place -= size
+        if step == 0:
+            got_load.wait()
+        total[...] = value + got_here[step].astype(F32)
+        rows = outs[0].shape[1]
+        for place, out in enumerate(outs):
+            start = pl.multiple_of((at[1] ^ place) * rows, 8)
+            out[step] = total[pl.ds(start, rows), :].astype(BF16)
+
+    for i in range(pair):
+        if i == 0:
+            first[0].wait()
+        blocks[i].wait()
+        value = None
+        for seq in range(left_here.shape[0]):
+            part = dot(left_here[seq], right_here[seq, i * columns : (i + 1) * columns, :], NT)
+            value = part if value is None else value + part
+        give(i, value)
+    for step, tap in enumerate(taps):
+        by = (tap - KERNEL_TAPS // 2) * DILATION_STEP
+        if step == 0:
+            for copy in ready:
+                copy.wait()
+        value = None
+        for seq in range(seqs):
+            if by > 0:
+                mask_rows(whole.at[seq], mask_here, masked, seq, by)
+                rows = masked[...]
+            else:
+                rows = whole[seq, BORDER - by : BORDER - by + length, :]
+            part = dot(act2_here[seq], rows)
+            value = part if value is None else value + part
+        give(pair + step, value)
+
+
+def tap_grads_kernel(left, rows3, before, after, mask, out, left_here, whole, mask_here, masked, total, done, sems):
+    seqs, length = rows3.shape[0], rows3.shape[1]
+    count, size = out.shape[0], left.shape[1] // out.shape[0]
+
+    def copy(place, source, target):
+        moving = pltpu.make_async_copy(source, target, sems.at[place])
+        moving.start()
+        return moving
+
+    loads = [copy(0, left, left_here), copy(1, mask, mask_here)]
+    loads.append(copy(2, before, whole.at[:, pl.ds(0, BORDER), :]))
+    loads.append(copy(3, after, whole.at[:, pl.ds(BORDER + length, BORDER), :]))
+    for seq in range(seqs):
+        loads.append(copy(4 + seq, rows3.at[seq], whole.at[seq, pl.ds(BORDER, length), :]))
+    for load in loads:
+        load.wait()
+    stores = []
+    for tap in range(KERNEL_TAPS):
+        by = (tap - KERNEL_TAPS // 2) * DILATION_STEP
+        value = None
+        for seq in range(seqs):
+            if by > 0:
+                mask_rows(whole.at[seq], mask_here, masked, seq, by)
+                rows = masked[...]
+            else:
+                rows = whole[seq, BORDER - by : BORDER - by + length, :]
+            part = dot(left_here[seq], rows)
+            value = part if value is None else value + part
+        total[tap % 2] = value
+        last = tap == KERNEL_TAPS - 1
+        if tap % 2 == 0 and not last:
+            continue
+        start = tap // 2 * 2 * size
+        height = out.shape[1] - start if last else 2 * size
+        fill = jnp.zeros((height - size, total.shape[2]), F32)
+        for shard in range(count):
+            span = slice(shard * size, (shard + 1) * size)
+            below = fill if last else total[1, span, :]
+            done[tap // 2, shard, :height, :] = jnp.concatenate([total[0, span, :], below], axis=0).astype(BF16)
+            place = 4 + seqs + tap // 2 * count + shard
+            stores.append(copy(place, done.at[tap // 2, shard, pl.ds(0, height), :], out.at[shard, pl.ds(start, height), :]))
+    for store in stores:
+        store.wait()
+
+
+def tap_grads(count, padded, left, rows3, before, after, mask):
+    seqs, length, inner = rows3.shape
+    steps = -(-KERNEL_TAPS // 2)
+    operands = (left, rows3, before, after, mask)
+    return pl.pallas_call(
+        tap_grads_kernel,
+        in_specs=[pl.BlockSpec(memory_space=pl.ANY)] * len(operands),
+        out_specs=pl.BlockSpec(memory_space=pl.ANY),
+        out_shape=shape((count, padded, inner)),
+        scratch_shapes=[
+            pltpu.VMEM(left.shape, BF16),
+            pltpu.VMEM((seqs, length + 2 * BORDER, inner), BF16),
+            pltpu.VMEM(mask.shape, BF16),
+            pltpu.VMEM((length, inner), BF16),
+            pltpu.VMEM((2, inner, inner), F32),
+            pltpu.VMEM((steps, count, 2 * inner // count, inner), BF16),
+            pltpu.SemaphoreType.DMA((4 + seqs + steps * count,)),
+        ],
+        compiler_params=params(),
+        cost_estimate=cost(2 * KERNEL_TAPS * left.size * inner, 4 * left.size + 10 * inner * inner),
+        name="tap_grads",
+    )(*operands)
+
+
+def mask_rows(whole, mask, masked, seq, by):
+    length, inner = masked.shape
+    chunk = 128
+
+    def body(i, carry):
+        kept = mask[seq, by // DILATION_STEP - 1, rows_at(i, chunk), :]
+        kept = jnp.concatenate([kept] * -(-inner // LANES), axis=1)[:, :inner]
+        start = pl.multiple_of(i * chunk + BORDER - by, DILATION_STEP)
+        masked[rows_at(i, chunk), :] = whole[pl.ds(start, chunk), :] * kept
+        return carry
+
+    each(length // chunk, body, 0, 1)
+
+
+def grads(at, columns, pair=None, taps=(), conv=(), got=None, units=None):
+    operands, scratch = [], []
+    count, flops, copies = 0, 0, 0
+    if pair is not None:
+        left, right = pair
+        half = left.shape[1] // 2
+        count = right.shape[1] // columns
+        operands += [left, right]
+        scratch += [pltpu.VMEM((left.shape[0], half, left.shape[2]), BF16), pltpu.VMEM(right.shape, BF16)]
+        copies += 1 + count
+        flops += left.size * right.shape[1]
+    if taps:
+        act2, rows3, _, _, mask = conv
+        seqs, length, inner = rows3.shape
+        half = inner // 2
+        operands += conv
+        scratch += [
+            pltpu.VMEM((seqs, half, length), BF16),
+            pltpu.VMEM((seqs, length + 2 * BORDER, inner), BF16),
+            pltpu.VMEM(mask.shape, BF16),
+            pltpu.VMEM((length, inner), BF16),
+        ]
+        copies += 4 + seqs
+        flops += act2.size * inner * len(taps)
+    total = count + len(taps)
     if got is None:
-        outs, out_specs = shape((half, width)), held((half, width))
+        units = units or (total,)
+        dims = [(size, half, columns) for size in units]
     else:
-        specs.append(held((half, width)))
-        outs = [shape((half // 2, width))] * 2
-        out_specs = [held((half // 2, width))] * 2
-    return pl.pallas_call(
-        functools.partial(outer_kernel, count=0 if got is None else 2),
+        operands.append(got)
+        scratch += [pltpu.VMEM(got.shape, BF16), pltpu.VMEM((half, columns), F32)]
+        copies += 1
+        dims = [(total, half // 2, columns)] * 2
+    scratch.append(pltpu.SemaphoreType.DMA((copies,)))
+    return pl.pallas_call(
+        functools.partial(grads_kernel, pair=count, taps=taps, keep=got is not None, units=units),
         grid_spec=pltpu.PrefetchScalarGridSpec(
             num_scalar_prefetch=1,
             grid=(1,),
-            in_specs=specs,
-            out_specs=out_specs,
-            scratch_shapes=[pltpu.VMEM((half, width) if got is not None else (8, LANES), F32)],
-        ),
-        out_shape=outs,
-        compiler_params=params(1),
-        cost_estimate=cost(seqs * length * height * width, 2 * seqs * length * (height + width)),
-        name="outer",
-    )(at, left, right, *(() if got is None else (got,)))
-
-
-def outer_taps_kernel(at, left, rows, before, after, mask, *rest, first, groups, keep):
-    got = rest[0] if keep else None
-    outs = rest[1:3] if keep else rest[: len(groups)]
-    whole, masked, total = rest[-3:]
-    seqs, length = rows.shape[0], rows.shape[1]
-    for seq in range(seqs):
-        extend(rows, before, after, mask, whole.at[seq], masked.at[seq], seq, -1)
-    places = [(group, i) for group, size in enumerate(groups) for i in range(size)]
-    for step, (group, i) in enumerate(places):
-        value = None
-        for seq in range(seqs):
-            right = tap_rows(whole.at[seq], masked.at[seq], first + step, -1, 0, length)
-            part = dot(left[seq], right)
-            value = part if value is None else value + part
-        if not keep:
-            outs[group][i] = value.astype(BF16)
-            continue
-        total[...] = value + got[i].astype(F32)
-        size = outs[0].shape[1]
-        for place, out in enumerate(outs):
-            start = pl.multiple_of((at[1] ^ place) * size, 8)
-            out[i] = total[pl.ds(start, size), :].astype(BF16)
-
-
-def outer_taps(at, left, rows, before, after, mask, first, groups, got=None):
-    seqs, length, inner = rows.shape
-    half = inner // 2
-    keep = got is not None
-    specs = [
-        pl.BlockSpec((seqs, half, length), lambda i, at: (0, at[0], 0)),
-        held(rows.shape),
-        held(before.shape),
-        held(after.shape),
-        held(mask.shape),
-    ]
-    if keep:
-        specs.append(held((groups[0], half, inner)))
-        dims = [(groups[0], half // 2, inner)] * 2
-    else:
-        dims = [(count, half, inner) for count in groups]
-    return pl.pallas_call(
-        functools.partial(outer_taps_kernel, first=first, groups=groups, keep=keep),
-        grid_spec=pltpu.PrefetchScalarGridSpec(
-            num_scalar_prefetch=1,
-            grid=(1,),
-            in_specs=specs,
+            in_specs=[pl.BlockSpec(memory_space=pl.ANY)] * len(operands),
             out_specs=[held(d) for d in dims],
-            scratch_shapes=[
-                pltpu.VMEM((seqs, length + 2 * BORDER, inner), BF16),
-                pltpu.VMEM((seqs, KERNEL_TAPS // 2, length, inner), BF16),
-                pltpu.VMEM((half, inner), F32),
-            ],
+            scratch_shapes=scratch,
         ),
         out_shape=[shape(d) for d in dims],
         compiler_params=params(1),
-        cost_estimate=cost(rows.size * inner * sum(groups), 4 * rows.size),
-        name="outer_taps",
-    )(at, left, rows, before, after, mask, *((got,) if keep else ()))
+        cost_estimate=cost(flops, 2 * sum(o.size for o in operands)),
+        name="grads",
+    )(at, *operands)
 
 
 def flip_kernel(w, out):
@@ -757,11 +870,11 @@
     return assemble(at, shard, mine, swapped(mine))
 
 
-def conv_weights(shard):
+def halves_of(shard, *others):
     taps, rows, columns = shard.shape
     half = halved(rows)
     own = lax.dynamic_slice_in_dim(shard, lax.axis_index("core") * (rows - half), half, axis=1)
-    pieces = lax.all_gather(own, ("ws", "core"), axis=0)
+    pieces = lax.all_gather(after(own, *others), ("ws", "core"), axis=0)
     return pieces.reshape(-1, 2, taps, half, columns)
 
 
@@ -778,46 +891,65 @@
 
 class Share:
     def __init__(self, first, second):
-        self.sum, self.second, self.came = first, second, ()
+        self.dims = first.shape
+        rows = lambda x: x.reshape(-1, x.shape[-1])
+        self.sum, self.second = rows(first), rows(second)
+        self.rows = self.sum.shape[0]
+        self.half = halved(self.rows)
+        run = lax.axis_index("run")
+        self.outer = (run == 0) | (run == 3)
 
     def land(self, *kernels):
-        came = after(self.came, *kernels)
-        if self.second is None and self.last:
-            run = lax.axis_index("run")
-            self.sum = jnp.where((run == 1) | (run == 2), self.sum, came[0])
-        else:
-            self.sum = summed(self.sum, *came)
-        self.second = None
-        return self.sum
+        return self.add(after(self.came, *kernels))
 
     def spread(self):
         near = [(2 * i + active(i), 2 * (i ^ 1) + active(i)) for i in range(4)]
         far = lambda bit: [(2 * i + 1 - active(i), 2 * (i ^ bit) + 1 - active(i)) for i in range(4)]
         move = lambda x, pairs: lax.ppermute(x, ("ws", "core"), pairs)
         self.came = (move(self.second, near), move(self.sum, far(2)), move(self.second, far(3)))
-
-    def along(self, *pairs):
+        self.add = self.add_all
+
+    def add_all(self, came):
+        self.sum = summed(self.sum, *came)
+        return self.sum
+
+    def along(self, x, bits):
         every = []
         for shard in range(4):
-            every += [((shard * 4 + i) * 2 + active(shard), (shard * 4 + j) * 2 + active(shard)) for i, j in pairs]
-        self.came = (lax.ppermute(self.sum, ("ws", "run", "core"), every),)
+            every += [((shard * 4 + i) * 2 + active(shard), (shard * 4 + (i ^ bits)) * 2 + active(shard)) for i in range(4)]
+        self.came = (lax.ppermute(x, ("ws", "run", "core"), every),)
+
+    def cut(self, low):
+        start = jnp.where(low, 0, self.rows - self.half)
+        return lax.dynamic_slice_in_dim(self.sum, start, self.half, axis=0)
 
     def inward(self):
-        self.along((0, 1), (3, 2))
-        self.last = False
+        self.along(self.cut(~self.outer), 1)
+        self.add = self.add_half
+
+    def add_half(self, came):
+        self.sum = summed(self.cut(self.outer), *came)
+        return self.sum
 
     def middle(self):
-        self.along((1, 2), (2, 1))
+        self.along(self.sum, 3)
+        self.add = self.add_all
 
     def outward(self):
-        self.along((1, 0), (2, 3))
-        self.last = True
+        self.along(self.sum, 1)
+        self.add = self.join
+
+    def join(self, came):
+        low = jnp.where(self.outer, self.sum, came[0])
+        high = jnp.where(self.outer, came[0], self.sum)
+        self.sum = jnp.concatenate([low, high[2 * self.half - self.rows :]], axis=0)
+        return self.sum
 
     def both(self):
         shard, core = lax.axis_index("ws"), lax.axis_index("core")
         pairs = [(2 * i + active(i), 2 * i + 1 - active(i)) for i in range(4)]
         other = lax.ppermute(self.sum, ("ws", "core"), pairs)
-        return jnp.where(core == active(shard), self.sum, other).astype(F32)
+        return jnp.where(core == active(shard), self.sum, other).astype(F32).reshape(self.dims)
 
 
 def plain(low, high, axis):
@@ -826,13 +958,20 @@
     return lax.psum(owned, ("run", "core")).astype(F32)
 
 
-def small_sums(sums):
-    if not square():
-        return lax.psum(sums, ("ws", "run", "core"))
-    sums = sums + swapped(sums)
-    for axis, bit in (("ws", 1), ("ws", 2), ("run", 1), ("run", 2)):
-        sums = sums + lax.ppermute(sums, axis, [(i, i ^ bit) for i in range(4)])
-    return sums
+class Small:
+    def __init__(self, mine):
+        self.sum = mine
+
+    def send(self, axis, bit):
+        self.came = lax.ppermute(self.sum, axis, [(i, i ^ bit) for i in range(lax.axis_size(axis))])
+
+    def land(self, *kernels):
+        self.sum = self.sum + after(self.came, *kernels)
+
+
+def totals_of(count, sums1, bias, sums2, sums3):
+    every = (sums1[0], sums1[1], bias, sums2[0], sums2[1], sums3[0], sums3[1])
+    return jnp.concatenate([s.sum(axis=-1).reshape(count, -1) for s in every], axis=1)
 
 
 def shards(
@@ -864,8 +1003,8 @@
     else:
         parts = lax.all_gather(flat, "ws", axis=0).astype(F32)
         vectors = spread(jnp.zeros_like(place), parts, sizes)
-    in_pieces = fetched(weight_in) if easy else None
-    own_conv = conv_weights(weight_conv) if easy else None
+    in_pieces = fetched(after(weight_in, parts)) if easy else None
+    conv_halves = halves_of(weight_conv) if easy else None
     length = block_ids.shape[1]
     ids_before, ids_after = neighbours(block_ids[:, :BORDER], block_ids[:, -BORDER:])
     ids = jnp.concatenate([ids_before, block_ids, ids_after], axis=1)
@@ -891,7 +1030,7 @@
     w_out, w_out_t = whole_weight(place, weight_out, out_pieces)
     grad_act3, bias_sums = project(w_out, g)
     if easy:
-        w_conv, w_conv_t = join(after(own_conv, grad_act3), weight_conv.shape[1])
+        w_conv, w_conv_t = join(after(conv_halves, grad_act3), weight_conv.shape[1])
     else:
         w_conv = lax.all_gather(weight_conv, "ws", axis=1, tiled=True)
         w_conv_t = flip(w_conv)
@@ -907,77 +1046,67 @@
         rows, *halo, mask_back, w_conv, vectors, normed2, stats2, seq, number, into
     )
     close = lambda low, seq, number, into: leave(low, w_in, x, g, vectors, stats1, seq, number, into)
+    width, inner = x.shape[1], act2.shape[1]
     if not easy:
-        taps = (act2, rows3, *halo, mask_back)
-        out_grad = plain(outer(give, act3, g), outer(keep, act3, g), 0)
-        (low,), (high,) = outer_taps(give, *taps, 0, (5,)), outer_taps(keep, *taps, 0, (5,))
-        conv_grad = plain(low, high, 1)
+        conv = (act2, rows3, *halo, mask_back)
+        halves = lambda **kw: [grads(at, inner, **kw)[0] for at in (give, keep)]
+        out_grad = plain(*halves(pair=(act3, g)), 1)
+        out_grad = out_grad.transpose(1, 0, 2).reshape(-1, width)
+        conv_grad = plain(*halves(taps=tuple(range(KERNEL_TAPS)), conv=conv), 1)
         low2, sums2 = back(rows3, 0, seqs, None)
-        in_grad = plain(outer(give, act1, low2), outer(keep, act1, low2), 0)
+        in_grad = plain(*halves(pair=(act1, low2)), 1)[0]
         input_grad, sums1 = close(low2, 0, seqs, None)
         block_output = finish(w_out_t, act3, x, vectors, 0, seqs)
     else:
-        out_send = outer(give, act3, g)
-        halo = after(halo, out_send)
-        taps = (act2, rows3, *halo, mask_back)
-        send_a, send_b = outer_taps(give, *taps, 0, (3, 2))
+        shard_rows = inner // count
+        padded = -(-KERNEL_TAPS * shard_rows // LANES) * LANES
+        taps = tap_grads(count, padded, act2, rows3, *halo, mask_back)
+        (out_send,) = grads(give, inner, pair=(after(act3, taps), g))
+        rows3, act3_late = after((rows3, act3), out_send)
+        taps = lax.psum_scatter(taps.reshape(-1, inner), "ws", scatter_dimension=0, tiled=True)
         got_out = swapped(out_send)
-        got_a, got_b = swapped(send_a), swapped(send_b)
-        out = Share(*outer(keep, act3, g, after(got_out, send_a)))
-        out.spread()
-        got_a, got_b = after((got_a, got_b), out.sum)
-        tap_a = Share(*outer_taps(keep, *taps, 0, (3,), got_a))
-        tap_a.spread()
-        tap_b = Share(*outer_taps(keep, *after(taps, tap_a.sum), 3, (2,), got_b))
-        tap_b.spread()
-        out.land(tap_b.sum)
-        out.inward()
-        low2, sums2a = back(after(rows3, tap_b.sum, out.sum), 0, 1, None)
-        out.land(sums2a)
-        out.middle()
-        tap_a.land(sums2a)
-        tap_a.inward()
-        low2, sums2b = back(after(rows3, sums2a, out.sum, tap_a.sum), 1, seqs - 1, low2)
-        sums2 = sums2a + sums2b
-        tap_b.land(sums2b)
-        tap_b.inward()
-        in_send = outer(give, *after((act1, low2), tap_b.sum))
-        got_in = swapped(in_send)
-        out.land(in_send)
-        out.outward()
-        tap_a.land(in_send)
-        tap_a.middle()
-        block_output = finish(*after((w_out_t, act3), in_send, out.sum, tap_a.sum), x, vectors, 0, 1)
-        inner = Share(*outer(keep, act1, low2, after(got_in, block_output)))
-        inner.spread()
-        tap_b.land(inner.sum)
-        tap_b.middle()
-        out.land(inner.sum)
-        input_grad, sums1a = close(after(low2, inner.sum, tap_b.sum), 0, 1, None)
-        inner.land(sums1a)
-        inner.inward()
-        tap_a.land(sums1a)
-        tap_a.outward()
-        input_grad, sums1b = close(after(low2, inner.sum, tap_a.sum), 1, seqs - 1, input_grad)
-        sums1 = sums1a + sums1b
-        inner.land(sums1b)
-        inner.middle()
-        tap_b.land(sums1b)
-        tap_b.outward()
-        tap_a.land(sums1b)
-        block_output = finish(
-            *after((w_out_t, act3), sums1b, inner.sum, tap_b.sum), x, vectors, 1, seqs - 1, block_output
-        )
-        inner.land(block_output)
-        inner.outward()
-        tap_b.land(block_output)
-        out_grad = out.both()
-        conv_grad = jnp.concatenate([tap_a.both(), tap_b.both()], axis=0)
-        inner.land()
-        in_grad = inner.both()
-
-    totals = [s.sum(axis=-1) for s in (sums1[0], sums1[1], bias_sums, sums2[0], sums2[1], sums3[0], sums3[1])]
-    small = small_sums(jnp.concatenate([t.reshape(count, -1) for t in totals], axis=1))
+        low2, sums2 = back(rows3, 0, seqs, None)
+        (in_send,) = grads(give, inner, pair=(act1, low2))
+        got_out, act3_late = after((got_out, act3_late), in_send)
+        out_parts = grads(keep, inner, pair=(act3_late, g), got=got_out)
+        got_in = after(swapped(in_send), *out_parts)
+        in_parts = grads(keep, inner, pair=(act1, low2), got=got_in)
+        flat = lambda part: part.reshape(-1, inner)
+        both = Share(*[jnp.concatenate([flat(o), flat(i)], axis=0) for o, i in zip(out_parts, in_parts)])
+        both.spread()
+        low2, taps = after((low2, taps), *in_parts)
+        taps = lax.psum_scatter(taps, ("run", "core"), scatter_dimension=0, tiled=True)
+        input_grad, sums1 = close(low2, 0, seqs, None)
+        small = Small(totals_of(count, sums1, bias_sums, sums2, sums3))
+        small.send("core", 1)
+        both.land(sums1)
+        both.inward()
+        (w_out_t, act3), taps = after(((w_out_t, act3), taps), both.sum, small.sum)
+        taps_sum = lax.all_gather(taps, ("run", "core"), axis=0, tiled=True)
+        block_output = finish(w_out_t, act3, x, vectors, 0, seqs)
+        small.land(block_output)
+        both.land(block_output, small.sum)
+        small.send("ws", 1)
+        both.middle()
+        small.land(both.sum)
+        small.send("ws", 2)
+        small.land()
+        both.land(small.sum, taps_sum)
+        small.send("run", 1)
+        both.outward()
+        small.land(both.sum)
+        small.send("run", 2)
+        small.land()
+        both.land(small.sum)
+        rows = both.both()
+        taps = taps_sum[: KERNEL_TAPS * shard_rows].astype(F32)
+        conv_grad = taps.reshape(KERNEL_TAPS, shard_rows, inner)
+        out_grad = jnp.concatenate([rows[:shard_rows], rows[shard_rows : 2 * shard_rows]], axis=1)
+        in_grad = rows[2 * shard_rows :]
+        small = small.sum
+
+    if not easy:
+        small = lax.psum(totals_of(count, sums1, bias_sums, sums2, sums3), ("ws", "run", "core"))
     small = lax.dynamic_index_in_dim(small, shard, axis=0, keepdims=False)
     at, vector_grads = 0, []
     for size in sizes:

time: 483 us -> 401 us (0.83)
  starting transfers between devices: 94.1 us -> 57.9 us
  Pallas kernels: 259 us -> 231 us
  other arithmetic: 36.6 us -> 19.1 us
    convert_element_type x12 -> x3, other arithmetic: 20.1 us -> 3.33 us  [summed(): return total.astype(BF16)]
    ppermute x12 -> x3, starting transfers between devices: 22 us -> 5.96 us  [spread(): move = lambda x, pairs: lax.ppermute(x, ('ws', 'core'), pairs)]
    ppermute x9, waiting for transfers between devices: 22.7 us -> 10.2 us  [from_ws(): lax.ppermute(x, 'ws', [(i, i ^ bit) for i in range(lax.axis_size('ws'))])]
    pallas_call x7 -> x5, Pallas kernels: 69.5 us -> 57.1 us  [the longest x4 33.6 us: grads(): pl.pallas_call(functools.partial(grads_kernel, pair=count, taps=taps, kee...]
    ppermute x16 -> x8, starting transfers between devices: 31.7 us -> 19.3 us  [the longest x3 15.8 us: along(): self.came = (lax.ppermute(x, ('ws', 'run', 'core'), every),)]
    reduce_scatter x0 -> x2, waiting for transfers between devices: none -> 10.6 us  [the longest x1 10.6 us: shards(): lax.psum_scatter(taps.reshape(-1, inner), 'ws', scatter_dimension=0, tile...]
    ppermute x4 -> x1, starting transfers between devices: 11.8 us -> 2.43 us  [both(): other = lax.ppermute(self.sum, ('ws', 'core'), pairs)]
    ppermute x7 -> x4, waiting for transfers between devices: 7.64 us -> 0.01 us  [swapped(): return lax.ppermute(x, 'core', [(0, 1), (1, 0)])]
  transfers between devices with their start and end apart: 55 -> 35, of which waited for: 9 -> 14; matrix products, arithmetic and copies ran while one was open for 8% -> 5% of each run, Pallas kernels for 42% -> 41%
where the time goes in v2:
time: 401 us; the launch traced here: 395 us
  Pallas kernels  231 us (58%)
  starting transfers between devices  57.9 us (14%)
  waiting for transfers between devices  54.6 us (14%)
  other arithmetic  19.1 us (5%)
  local copies, waits for them, and re-layouts  17.6 us (4%)
  between operations  14.7 us (4%)
    pallas_call x1, Pallas kernels, conv_block(): pl.pallas_call(functools.partial(conv_kernel, chunk=chunk), grid=(seqs, l...  34.5 us
    pallas_call x4, Pallas kernels, grads(): pl.pallas_call(functools.partial(grads_kernel, pair=count, taps=taps, kee...  33.6 us
    pallas_call x1, Pallas kernels, conv_back(): pl.pallas_call(functools.partial(conv_back_kernel, chunk=chunk), grid=(co...  31.2 us
    pallas_call x1, Pallas kernels, leave(): pl.pallas_call(functools.partial(leave_kernel, chunk=chunk), grid=(count,...  29 us
    pallas_call x1, Pallas kernels, tap_grads(): pl.pallas_call(tap_grads_kernel, in_specs=[pl.BlockSpec(memory_space=pl.A...  23.5 us
    ppermute x5, waiting for transfers between devices, send(): lax.ppermute(self.sum, axis, [(i, i ^ bit) for i in range(lax.axis_size(a...  19.1 us
    pallas_call x1, Pallas kernels, enter(): pl.pallas_call(functools.partial(enter_kernel, chunk=chunk), grid=(seqs,...  15.9 us
    ppermute x3, starting transfers between devices, along(): self.came = (lax.ppermute(x, ('ws', 'run', 'core'), every),)  15.8 us
  transfers between devices with their start and end apart: 35, of which 14 were waited for; matrix products, arithmetic and copies ran while one was open for 5% of the time, Pallas kernels for 41%

profile of v2, /device:TPU:0, one launch (start us, length us, event | category | flops | bytes accessed | tf_op | source)
XLA Modules:
  0.0 395.3 jit_solution(14093018505415274627)
XLA Ops:
  7.3 1.3 copy-done
  8.7 1.0 constant_dynamic-slice_fusion.2
  9.9 4.0 %collective-permute-start.2 = (bf16[2000]{0:T(1024)(128)(2,1)S(1)}, bf16[2000]{0:T(1024)(128)(2,1)S(1)}, u32[]{:S(2)}, u32[]{:S(2)}) collective-permute-start(bf16[2000]{0:T(1024)(128)(2,1)S(1)} %concatenate.27), channel_id=1, source_target_pairs={{0,24},{8,16},{16,8},{24,0},{1,25},{9,17},{17,9},{25,1},{2,26},{10... | collective-permute-start | bytes 12008 | tf_op jit(solution)/shard_map/ppermute | solution.py:840
  15.5 2.0 collective-permute-done.1
  18.9 1.9 collective-permute-start.4
  20.8 1.4 collective-permute-start.5
  22.8 4.9 %spread.1.gain.shift.bias = f32[8000,128]{1,0:T(8,128)} custom-call(s32[2]{0:T(128)} %pad_add_fusion.1.at, f32[4,2000]{1,0:T(4,128)} %maximum_convert_fusion.parts), custom_call_target="tpu_custom_call" | custom-call | bytes 256000 | tf_op jit(solution)/shard_map/spread/pallas_call | solution.py:815
  27.7 11.5 %open_block.1 = (bf16[2,1600,1024]{2,1,0:T(8,128)(2,1)}, f32[2,8,1024]{2,1,0:T(8,128)}) custom-call(bf16[2,1600,1024]{2,1,0:T(8,128)(2,1)} %bitcast.41, f32[8000,128]{1,0:T(8,128)} %spread.1.gain.shift.bias, f32[8000,128]{1,0:T(8,128)} %spread.1.gain.shift.bias), custom_call_target="tpu_custom_call" | custom-call | flops 8192000 | bytes 819200 | tf_op jit(solution)/shard_map/open_block/pallas_call | solution.py:137
  39.2 6.6 %collective-permute-done.5 = bf16[200,800]{1,0:T(8,128)(2,1)S(1)} collective-permute-done((bf16[200,800]{1,0:T(8,128)(2,1)S(1)}, bf16[200,800]{1,0:T(8,128)(2,1)S(1)}, u32[]{:S(2)}, u32[]{:S(2)}) %collective-permute-start.5) | collective-permute-done | bytes 320032 | tf_op jit(solution)/shard_map/ppermute | solution.py:840
  47.1 2.5 collective-permute-start.8
  50.6 6.8 %assemble.2 = (bf16[1600,800]{1,0:T(8,128)(2,1)}, bf16[800,1600]{1,0:T(8,128)(2,1)}) custom-call(s32[2]{0:T(128)} %pad_add_fusion.1.at, bf16[400,800]{1,0:T(8,128)(2,1)} %own.2, bf16[3,200,800]{2,1,0:T(8,128)(2,1)} %copy-done.2, bf16[3,200,800]{2,1,0:T(8,128)(2,1)} %copy-done.10), custom_call_target="tpu_custom_call" | custom-call | bytes 480000 | tf_op jit(solution)/shard_map/assemble/pallas_call | solution.py:757
  57.5 15.9 %enter.1 = (bf16[2,800,1024]{2,1,0:T(8,128)(2,1)}, bf16[2,1024,800]{2,1,0:T(8,128)(2,1)}, f32[2,800,1024]{2,1,0:T(8,128)}, f32[2,8,1024]{2,1,0:T(8,128)}) custom-call(bf16[2,1600,1024]{2,1,0:T(8,128)(2,1)} %get-tuple-element.69.act1.refs_0_, bf16[800,1600]{1,0:T(8,128)(2,1)} %get-tuple-element.74.w_in, f32[8000,128]{1,0:T(8,128)} %spread.1.gain.shift.bias, ...), custom_call_target="tpu_custom_call" | custom-call | flops 327680000 | bytes 1228800 | tf_op jit(solution)/shard_map/enter/pallas_call | solution.py:171
  74.1 2.1 collective-permute-start.16
  76.2 1.3 collective-permute-start.13
  77.5 2.6 collective-permute-done.13
  81.2 4.7 %collective-permute-start.11 = (bf16[2,32,800]{2,1,0:T(8,128)(2,1)S(1)}, bf16[2,32,800]{2,1,0:T(8,128)(2,1)S(1)}, u32[]{:S(2)}, u32[]{:S(2)}) collective-permute-start(bf16[2,32,800]{2,1,0:T(8,128)(2,1)S(1)} %get-tuple-element.133), channel_id=1, source_target_pairs={{0,1},{1,2},{2,3},{3,4},{4,5},{5,6},{6,7},{8,9},{9,10},{10,11},{11... | collective-permute-start | bytes 307208 | tf_op jit(solution)/shard_map/ppermute | solution.py:847
  85.9 1.6 collective-permute-start.12
  88.5 5.9 %assemble.3 = (bf16[800,1600]{1,0:T(8,128)(2,1)}, bf16[1600,800]{1,0:T(8,128)(2,1)}) custom-call(s32[2]{0:T(128)} %pad_add_fusion.1.at, bf16[200,1600]{1,0:T(8,128)(2,1)} %own.3, bf16[3,104,1600]{2,1,0:T(8,128)(2,1)} %copy-done.3, bf16[3,104,1600]{2,1,0:T(8,128)(2,1)} %copy-done.11), custom_call_target="tpu_custom_call" | custom-call | bytes 480000 | tf_op jit(solution)/shard_map/assemble/pallas_call | solution.py:757
  94.4 11.7 %project.1 = (f32[2,800,1024]{2,1,0:T(8,128)}, f32[1600,128]{1,0:T(8,128)}) custom-call(bf16[800,1600]{1,0:T(8,128)(2,1)} %get-tuple-element.81.weight, bf16[2,1600,1024]{2,1,0:T(8,128)(2,1)} %bitcast.37), custom_call_target="tpu_custom_call" | custom-call | flops 327680000 | bytes 819200 | tf_op jit(solution)/shard_map/project/pallas_call | solution.py:210
  106.2 9.6 %join.1 = (bf16[5,800,800]{2,1,0:T(8,128)(2,1)}, bf16[5,800,800]{2,1,0:T(8,128)(2,1)}) custom-call(bf16[4,2,5,104,800]{4,3,2,1,0:T(8,128)(2,1)} %bitcast.45), custom_call_target="tpu_custom_call" | custom-call | bytes 1200000 | tf_op jit(solution)/shard_map/join/pallas_call | solution.py:787
  115.8 1.6 broadcast_in_dim.4.mask
  117.4 34.5 %conv_block.1 = (bf16[2,800,1024]{2,1,0:T(8,128)(2,1)}, bf16[2,1024,800]{2,1,0:T(8,128)(2,1)}, f32[2,800,128]{2,1,0:T(8,128)}) custom-call(bf16[2,1024,800]{2,1,0:T(8,128)(2,1)} %get-tuple-element.80.rows, bf16[2,32,800]{2,1,0:T(8,128)(2,1)} %copy-done.14, bf16[2,32,800]{2,1,0:T(8,128)(2,1)} %copy-done.15, bf16[2,2,1024,128]{3,2,1,0:T(8,128)(2,1)} %broadcast_in_dim.4.mask, ...), custom_call_target="tpu_custom_call" | custom-call | flops 819200000 | bytes 1228800 | tf_op jit(solution)/shard_map/conv_block/pallas_call | solution.py:298
  152.9 3.0 collective-permute-start.14
  155.9 1.8 collective-permute-start.15
  157.8 2.1 collective-permute-done.15.after
  159.9 1.6 broadcast_in_dim.5.mask
  161.5 23.5 %tap_grads.1 = bf16[4,1024,800]{2,1,0:T(8,128)(2,1)} custom-call(bf16[2,800,1024]{2,1,0:T(8,128)(2,1)} %get-tuple-element.75.left, bf16[2,1024,800]{2,1,0:T(8,128)(2,1)} %get-tuple-element.90.rows3.rows, bf16[2,32,800]{2,1,0:T(8,128)(2,1)} %copy-done.12, bf16[2,32,800]{2,1,0:T(8,128)(2,1)} %copy-done.13, bf16[2,2,1024,128]{3,2,1,0:T(8,128)(2,1)} %broadcast_in_dim.5.mask), custom_call_target="tpu_custom_call" | custom-call | flops 819200000 | bytes 809600 | tf_op jit(solution)/shard_map/tap_grads/pallas_call | solution.py:642
  185.8 8.0 %grads.4 = bf16[2,400,800]{2,1,0:T(8,128)(2,1)} custom-call(s32[2]{0:T(128)} %pad_add_fusion.2.at, bf16[2,800,1024]{2,1,0:T(8,128)(2,1)} %get-tuple-element.115.refs_0_.act3, bf16[2,1600,1024]{2,1,0:T(8,128)(2,1)} %bitcast.38), custom_call_target="tpu_custom_call" | custom-call | flops 163840000 | bytes 614400 | tf_op jit(solution)/shard_map/grads/pallas_call | solution.py:710
  193.8 3.5 collective-permute-start.18
  197.3 31.2 %conv_back.1 = (bf16[2,800,1024]{2,1,0:T(8,128)(2,1)}, f32[2,800,128]{2,1,0:T(8,128)}) custom-call(bf16[2,1024,800]{2,1,0:T(8,128)(2,1)} %get-tuple-element.90.rows3.rows, bf16[2,32,800]{2,1,0:T(8,128)(2,1)} %copy-done.12, bf16[2,32,800]{2,1,0:T(8,128)(2,1)} %copy-done.13, bf16[2,2,1024,128]{3,2,1,0:T(8,128)(2,1)} %broadcast_in_dim.5.mask, ...), custom_call_target="tpu_custom_call" | custom-call | flops 819200000 | bytes 1024000 | tf_op jit(solution)/shard_map/conv_back/pallas_call | solution.py:382
  228.4 8.3 %grads.5 = bf16[1,800,800]{2,1,0:T(8,128)(2,1)} custom-call(s32[2]{0:T(128)} %pad_add_fusion.2.at, bf16[2,1600,1024]{2,1,0:T(8,128)(2,1)} %get-tuple-element.69.act1.refs_0_, bf16[2,800,1024]{2,1,0:T(8,128)(2,1)} %get-tuple-element.104.refs_1_.low), custom_call_target="tpu_custom_call" | custom-call | flops 163840000 | bytes 614400 | tf_op jit(solution)/shard_map/grads/pallas_call | solution.py:710
  237.4 1.1 copy-done.8
  238.5 8.4 %grads.6 = (bf16[2,200,800]{2,1,0:T(8,128)(2,1)}, bf16[2,200,800]{2,1,0:T(8,128)(2,1)}) custom-call(s32[2]{0:T(128)} %pad_add_fusion.3.at, bf16[2,800,1024]{2,1,0:T(8,128)(2,1)} %get-tuple-element.115.refs_0_.act3, bf16[2,1600,1024]{2,1,0:T(8,128)(2,1)} %bitcast.39, bf16[2,400,800]{2,1,0:T(8,128)(2,1)} %copy-done.8), custom_call_target="tpu_custom_call" | custom-call | flops 163840000 | bytes 694400 | tf_op jit(solution)/shard_map/grads/pallas_call | solution.py:710
  246.9 1.1 copy-done.9
  248.0 8.9 %grads.7 = (bf16[1,400,800]{2,1,0:T(8,128)(2,1)}, bf16[1,400,800]{2,1,0:T(8,128)(2,1)}) custom-call(s32[2]{0:T(128)} %pad_add_fusion.3.at, bf16[2,1600,1024]{2,1,0:T(8,128)(2,1)} %get-tuple-element.69.act1.refs_0_, bf16[2,800,1024]{2,1,0:T(8,128)(2,1)} %get-tuple-element.104.refs_1_.low, bf16[1,800,800]{2,1,0:T(8,128)(2,1)} %copy-done.9), custom_call_target="tpu_custom_call" | custom-call | flops 163840000 | bytes 694400 | tf_op jit(solution)/shard_map/grads/pallas_call | solution.py:710
  257.0 10.6 %reduce-scatter.3.cloned.1.call-done = bf16[1024,800]{1,0:T(8,128)(2,1)} async-done(((bf16[4096,800]{1,0:T(8,128)(2,1)}), bf16[1024,800]{1,0:T(8,128)(2,1)}) %reduce-scatter.3.cloned.1.call-update) | async-done | bytes 1638416 | tf_op jit(solution)/shard_map/reduce_scatter | solution.py:1066
  267.7 1.5 pad_maximum_fusion.1
  269.2 3.2 collective-permute-start.19
  272.4 1.2 pad_maximum_fusion
  273.6 1.3 collective-permute-start.20
  274.9 1.5 collective-permute-start.21
  276.4 1.5 reduce_sum.65
  278.0 1.4 slice_reduce_fusion.2
  279.6 1.4 slice_reduce_fusion.4
  281.2 29.0 %leave.1 = (bf16[2,1600,1024]{2,1,0:T(8,128)(2,1)}, f32[2,1600,128]{2,1,0:T(8,128)}) custom-call(bf16[2,800,1024]{2,1,0:T(8,128)(2,1)} %get-tuple-element.104.refs_1_.low, bf16[1600,800]{1,0:T(8,128)(2,1)} %get-tuple-element.105.w_in, bf16[2,1600,1024]{2,1,0:T(8,128)(2,1)} %bitcast.42, bf16[2,1600,1024]{2,1,0:T(8,128)(2,1)} %bitcast.40, ...), custom_call_target="tpu_custom_call" | custom-call | flops 327680000 | bytes 1433600 | tf_op jit(solution)/shard_map/leave/pallas_call | solution.py:452
  310.2 1.9 slice_reduce_fusion
  312.4 3.0 add_convert_fusion
  315.5 3.4 collective-permute-start.24
  319.2 13.4 %finish.1 = bf16[2,1600,1024]{2,1,0:T(8,128)(2,1)} custom-call(bf16[1600,800]{1,0:T(8,128)(2,1)} %get-tuple-element.114.w_out, bf16[2,800,1024]{2,1,0:T(8,128)(2,1)} %get-tuple-element.115.refs_0_.act3, bf16[2,1600,1024]{2,1,0:T(8,128)(2,1)} %bitcast.43, f32[8000,128]{1,0:T(8,128)} %spread.1.gain.shift.bias), custom_call_target="tpu_custom_call" | custom-call | tf_op jit(solution)/shard_map/finish/pallas_call | solution.py:492
  332.8 5.3 %collective-permute-start.27 = (bf16[400,800]{1,0:T(8,128)(2,1)S(1)}, bf16[400,800]{1,0:T(8,128)(2,1)S(1)}, u32[]{:S(2)}, u32[]{:S(2)}) collective-permute-start(bf16[400,800]{1,0:T(8,128)(2,1)S(1)} %add_convert_fusion.2), channel_id=1, source_target_pairs={{0,6},{2,4},{4,2},{6,0},{8,14},{10,12},{12,10},{14,8},{17,23},{19,... | collective-permute-start | bytes 1920008 | tf_op jit(solution)/shard_map/ppermute | solution.py:920
  338.0 1.3 collective-permute-start.23
  339.3 2.7 collective-permute-done.23
  342.1 3.9 collective-permute-done.25
  346.0 7.6 %collective-permute-done.27 = bf16[400,800]{1,0:T(8,128)(2,1)S(1)} collective-permute-done((bf16[400,800]{1,0:T(8,128)(2,1)S(1)}, bf16[400,800]{1,0:T(8,128)(2,1)S(1)}, u32[]{:S(2)}, u32[]{:S(2)}) %collective-permute-start.27) | collective-permute-done | bytes 640032 | tf_op jit(solution)/shard_map/ppermute | solution.py:920
  353.6 2.3 all-gather.4.cloned.1.call-done
  356.0 7.1 %collective-permute-start.29 = (bf16[400,800]{1,0:T(8,128)(2,1)S(1)}, bf16[400,800]{1,0:T(8,128)(2,1)S(1)}, u32[]{:S(2)}, u32[]{:S(2)}) collective-permute-start(bf16[400,800]{1,0:T(8,128)(2,1)S(1)} %add_convert_fusion.1), channel_id=1, source_target_pairs={{0,2},{2,0},{4,6},{6,4},{8,10},{10,8},{12,14},{14,12},{17,19},{19,... | collective-permute-start | bytes 1920008 | tf_op jit(solution)/shard_map/ppermute | solution.py:920
  363.2 9.5 %collective-permute-done.26 = f32[4,2000]{1,0:T(4,128)S(1)} collective-permute-done((f32[4,2000]{1,0:T(4,128)S(1)}, f32[4,2000]{1,0:T(4,128)S(1)}, u32[]{:S(2)}, u32[]{:S(2)}) %collective-permute-start.26) | collective-permute-done | bytes 32032 | tf_op jit(solution)/shard_map/ppermute | solution.py:966
  372.7 1.9 collective-permute-start.28
  374.6 3.0 collective-permute-done.28
  377.9 2.4 collective-permute-start.30
  380.3 1.5 slice-done
  381.8 2.0 convert.1
  385.5 1.2 slice.144
  386.8 1.3 pad_maximum_fusion.3
  (133 shorter events, 15.6 us)
Async XLA Ops:
  7.2 1.5 copy-start
  7.2 2.6 copy-start.17
  7.2 2.6 copy-start.18
  7.2 2.6 copy-start.19
  7.2 2.6 copy-start.20
  7.2 2.6 copy-start.21
  7.2 2.6 copy-start.22
  7.3 2.6 copy-start.23
  7.3 11.4 %copy-start.6 = (bf16[400,800]{1,0:T(8,128)(2,1)S(1)}, bf16[400,800]{1,0:T(8,128)(2,1)}, u32[]{:S(2)}) copy-start(bf16[400,800]{1,0:T(8,128)(2,1)} %own.2) | copy-start | bytes 1920004
  7.3 98.9 %all-gather.6.cloned.1.call-start = ((), (), s32[]{:S(2)}) async-start(), calls=%async_computation.5 | async-start | bytes 8386560 | tf_op jit(solution)/shard_map/all_gather | solution.py:877
  9.7 257.8 %reduce-scatter.3.cloned.1.call-start = ((), (), s32[]{:S(2)}) async-start(), calls=%async_computation.2 | async-start | bytes 9175040 | tf_op jit(solution)/shard_map/reduce_scatter | solution.py:1066
  9.9 5.5 %collective-permute-start.2 = (bf16[2000]{0:T(1024)(128)(2,1)S(1)}, bf16[2000]{0:T(1024)(128)(2,1)S(1)}, u32[]{:S(2)}, u32[]{:S(2)}) collective-permute-start(bf16[2000]{0:T(1024)(128)(2,1)S(1)} %concatenate.27), channel_id=1, source_target_pairs={{0,24},{8,16},{16,8},{24,0},{1,25},{9,17},{17,9},{25,1},{2,26},{10... | collective-permute-start | bytes 12008 | tf_op jit(solution)/shard_map/ppermute | solution.py:840
  13.9 3.6 collective-permute-start.1
  14.4 3.6 collective-permute-start
  18.7 20.5 %collective-permute-start.3 = (bf16[200,800]{1,0:T(8,128)(2,1)S(1)}, bf16[200,800]{1,0:T(8,128)(2,1)S(1)}, u32[]{:S(2)}, u32[]{:S(2)}) collective-permute-start(bf16[200,800]{1,0:T(8,128)(2,1)S(1)} %constant_dynamic-slice_fusion.4), channel_id=1, source_target_pairs={{0,8},{8,0},{16,24},{24,16},{1,9},{9,1},{17,25},{25,17},{2,10},{10... | collective-permute-start | bytes 960008 | tf_op jit(solution)/shard_map/ppermute | solution.py:840
  18.9 20.3 %collective-permute-start.4 = (bf16[200,800]{1,0:T(8,128)(2,1)S(1)}, bf16[200,800]{1,0:T(8,128)(2,1)S(1)}, u32[]{:S(2)}, u32[]{:S(2)}) collective-permute-start(bf16[200,800]{1,0:T(8,128)(2,1)S(1)} %constant_dynamic-slice_fusion.4), channel_id=1, source_target_pairs={{0,16},{8,24},{16,0},{24,8},{1,17},{9,25},{17,1},{25,9},{2,18},{10... | collective-permute-start | bytes 960008 | tf_op jit(solution)/shard_map/ppermute | solution.py:840
  20.8 25.0 %collective-permute-start.5 = (bf16[200,800]{1,0:T(8,128)(2,1)S(1)}, bf16[200,800]{1,0:T(8,128)(2,1)S(1)}, u32[]{:S(2)}, u32[]{:S(2)}) collective-permute-start(bf16[200,800]{1,0:T(8,128)(2,1)S(1)} %constant_dynamic-slice_fusion.4), channel_id=1, source_target_pairs={{0,24},{8,16},{16,8},{24,0},{1,25},{9,17},{17,9},{25,1},{2,26},{10... | collective-permute-start | bytes 960008 | tf_op jit(solution)/shard_map/ppermute | solution.py:840
  39.2 6.8 %copy-start.7 = (bf16[200,1600]{1,0:T(8,128)(2,1)S(1)}, bf16[200,1600]{1,0:T(8,128)(2,1)}, u32[]{:S(2)}) copy-start(bf16[200,1600]{1,0:T(8,128)(2,1)} %own.3) | copy-start | bytes 1920004
  45.9 3.7 copy-start.2
  46.0 3.7 collective-permute-start.9
  46.1 27.2 %collective-permute-start.6 = (bf16[104,1600]{1,0:T(8,128)(2,1)S(1)}, bf16[104,1600]{1,0:T(8,128)(2,1)S(1)}, u32[]{:S(2)}, u32[]{:S(2)}) collective-permute-start(bf16[104,1600]{1,0:T(8,128)(2,1)S(1)} %constant_dynamic-slice_fusion.3), channel_id=1, source_target_pairs={{0,8},{8,0},{16,24},{24,16},{1,9},{9,1},{17,25},{25,17},{2,10},{10... | collective-permute-start | bytes 998408 | tf_op jit(solution)/shard_map/ppermute | solution.py:840
  46.9 26.5 %collective-permute-start.7 = (bf16[104,1600]{1,0:T(8,128)(2,1)S(1)}, bf16[104,1600]{1,0:T(8,128)(2,1)S(1)}, u32[]{:S(2)}, u32[]{:S(2)}) collective-permute-start(bf16[104,1600]{1,0:T(8,128)(2,1)S(1)} %constant_dynamic-slice_fusion.3), channel_id=1, source_target_pairs={{0,16},{8,24},{16,0},{24,8},{1,17},{9,25},{17,1},{25,9},{2,18},{10... | collective-permute-start | bytes 998408 | tf_op jit(solution)/shard_map/ppermute | solution.py:840
  47.1 26.4 %collective-permute-start.8 = (bf16[104,1600]{1,0:T(8,128)(2,1)S(1)}, bf16[104,1600]{1,0:T(8,128)(2,1)S(1)}, u32[]{:S(2)}, u32[]{:S(2)}) collective-permute-start(bf16[104,1600]{1,0:T(8,128)(2,1)S(1)} %constant_dynamic-slice_fusion.3), channel_id=1, source_target_pairs={{0,24},{8,16},{16,8},{24,0},{1,25},{9,17},{17,9},{25,1},{2,26},{10... | collective-permute-start | bytes 998408 | tf_op jit(solution)/shard_map/ppermute | solution.py:840
  49.6 1.0 copy-start.10
  73.3 0.7 copy-start.16
  73.6 13.9 %copy-start.3 = (bf16[3,104,1600]{2,1,0:T(8,128)(2,1)}, bf16[3,104,1600]{2,1,0:T(8,128)(2,1)S(1)}, u32[]{:S(2)}) copy-start(bf16[3,104,1600]{2,1,0:T(8,128)(2,1)S(1)} %pad_maximum_fusion.5.mine) | copy-start | bytes 2995204
  73.6 13.9 %collective-permute-start.10 = (bf16[3,104,1600]{2,1,0:T(8,128)(2,1)S(1)}, bf16[3,104,1600]{2,1,0:T(8,128)(2,1)S(1)}, u32[]{:S(2)}, u32[]{:S(2)}) collective-permute-start(bf16[3,104,1600]{2,1,0:T(8,128)(2,1)S(1)} %pad_maximum_fusion.5.mine), channel_id=1, source_target_pairs={{0,1},{1,0},{2,3},{3,2},{4,5},{5,4},{6,7},{7,6},{8,9},{9,8},{10,11... | collective-permute-start | bytes 2995208 | tf_op jit(solution)/shard_map/ppermute | solution.py:836
  74.1 6.0 %collective-permute-start.16 = (s32[2,32]{1,0:T(2,128)S(1)}, s32[2,32]{1,0:T(2,128)S(1)}, u32[]{:S(2)}, u32[]{:S(2)}) collective-permute-start(s32[2,32]{1,0:T(2,128)S(1)} %get-tuple-element.151), channel_id=1, source_target_pairs={{0,1},{1,2},{2,3},{3,4},{4,5},{5,6},{6,7},{8,9},{9,10},{10,11},{11... | collective-permute-start | bytes 776 | tf_op jit(solution)/shard_map/ppermute | solution.py:847
  76.2 3.9 collective-permute-start.13
  81.2 24.9 %collective-permute-start.11 = (bf16[2,32,800]{2,1,0:T(8,128)(2,1)S(1)}, bf16[2,32,800]{2,1,0:T(8,128)(2,1)S(1)}, u32[]{:S(2)}, u32[]{:S(2)}) collective-permute-start(bf16[2,32,800]{2,1,0:T(8,128)(2,1)S(1)} %get-tuple-element.133), channel_id=1, source_target_pairs={{0,1},{1,2},{2,3},{3,4},{4,5},{5,6},{6,7},{8,9},{9,10},{10,11},{11... | collective-permute-start | bytes 307208 | tf_op jit(solution)/shard_map/ppermute | solution.py:847
  85.9 20.3 %collective-permute-start.12 = (bf16[2,32,800]{2,1,0:T(8,128)(2,1)S(1)}, bf16[2,32,800]{2,1,0:T(8,128)(2,1)S(1)}, u32[]{:S(2)}, u32[]{:S(2)}) collective-permute-start(bf16[2,32,800]{2,1,0:T(8,128)(2,1)S(1)} %get-tuple-element.132), channel_id=1, source_target_pairs={{1,0},{2,1},{3,2},{4,3},{5,4},{6,5},{7,6},{9,8},{10,9},{11,10},{12... | collective-permute-start | bytes 307208 | tf_op jit(solution)/shard_map/ppermute | solution.py:847
  87.6 1.0 copy-start.11
  106.2 9.6 %copy-start.14 = (bf16[2,32,800]{2,1,0:T(8,128)(2,1)}, bf16[2,32,800]{2,1,0:T(8,128)(2,1)S(1)}, u32[]{:S(2)}) copy-start(bf16[2,32,800]{2,1,0:T(8,128)(2,1)S(1)} %collective-permute-done.11.before) | copy-start | bytes 307204
  106.2 9.6 %copy-start.15 = (bf16[2,32,800]{2,1,0:T(8,128)(2,1)}, bf16[2,32,800]{2,1,0:T(8,128)(2,1)S(1)}, u32[]{:S(2)}) copy-start(bf16[2,32,800]{2,1,0:T(8,128)(2,1)S(1)} %collective-permute-done.12.after) | copy-start | bytes 307204
  152.9 4.9 %collective-permute-start.14 = (bf16[2,32,800]{2,1,0:T(8,128)(2,1)S(1)}, bf16[2,32,800]{2,1,0:T(8,128)(2,1)S(1)}, u32[]{:S(2)}, u32[]{:S(2)}) collective-permute-start(bf16[2,32,800]{2,1,0:T(8,128)(2,1)S(1)} %get-tuple-element.131), channel_id=1, source_target_pairs={{0,1},{1,2},{2,3},{3,4},{4,5},{5,6},{6,7},{8,9},{9,10},{10,11},{11... | collective-permute-start | bytes 307208 | tf_op jit(solution)/shard_map/ppermute | solution.py:847
  155.9 4.0 %collective-permute-start.15 = (bf16[2,32,800]{2,1,0:T(8,128)(2,1)S(1)}, bf16[2,32,800]{2,1,0:T(8,128)(2,1)S(1)}, u32[]{:S(2)}, u32[]{:S(2)}) collective-permute-start(bf16[2,32,800]{2,1,0:T(8,128)(2,1)S(1)} %get-tuple-element.130), channel_id=1, source_target_pairs={{1,0},{2,1},{3,2},{4,3},{5,4},{6,5},{7,6},{9,8},{10,9},{11,10},{12... | collective-permute-start | bytes 307208 | tf_op jit(solution)/shard_map/ppermute | solution.py:847
  157.7 3.7 copy-start.12
  159.9 1.6 copy-start.13
  185.0 130.4 %reduce-scatter.5.cloned.1.call-start = ((), (), s32[]{:S(2)}) async-start(), calls=%async_computation.3 | async-start | bytes 2064384 | tf_op jit(solution)/shard_map/reduce_scatter | solution.py:1078
  193.8 43.6 %collective-permute-start.18 = (bf16[2,400,800]{2,1,0:T(8,128)(2,1)}, bf16[2,400,800]{2,1,0:T(8,128)(2,1)S(1)}, u32[]{:S(2)}, u32[]{:S(2)}) collective-permute-start(bf16[2,400,800]{2,1,0:T(8,128)(2,1)} %grads.4), channel_id=1, source_target_pairs={{0,1},{1,0},{2,3},{3,2},{4,5},{5,4},{6,7},{7,6},{8,9},{9,8},{10,11... | collective-permute-start | bytes 3840008 | tf_op jit(solution)/shard_map/ppermute | solution.py:836
  236.7 10.2 %collective-permute-start.17 = (bf16[1,800,800]{2,1,0:T(8,128)(2,1)}, bf16[1,800,800]{2,1,0:T(8,128)(2,1)S(1)}, u32[]{:S(2)}, u32[]{:S(2)}) collective-permute-start(bf16[1,800,800]{2,1,0:T(8,128)(2,1)} %grads.5), channel_id=1, source_target_pairs={{0,1},{1,0},{2,3},{3,2},{4,5},{5,4},{6,7},{7,6},{8,9},{9,8},{10,11... | collective-permute-start | bytes 3840008 | tf_op jit(solution)/shard_map/ppermute | solution.py:836
  237.4 1.1 copy-start.8
  246.9 1.1 copy-start.9
  267.6 4.8 %copy-start.4 = (bf16[2,200,800]{2,1,0:T(8,128)(2,1)S(1)}, bf16[2,200,800]{2,1,0:T(8,128)(2,1)}, u32[]{:S(2)}) copy-start(bf16[2,200,800]{2,1,0:T(8,128)(2,1)} %get-tuple-element.98) | copy-start | bytes 1920004
  267.6 4.8 %copy-start.5 = (bf16[1,400,800]{2,1,0:T(8,128)(2,1)S(1)}, bf16[1,400,800]{2,1,0:T(8,128)(2,1)}, u32[]{:S(2)}) copy-start(bf16[1,400,800]{2,1,0:T(8,128)(2,1)} %get-tuple-element.101) | copy-start | bytes 1920004
  267.6 88.3 %all-gather.4.cloned.1.call-start = ((), (), s32[]{:S(2)}) async-start(), calls=%async_computation.4 | async-start | bytes 2064384 | tf_op jit(solution)/shard_map/all_gather | solution.py:1085
  269.2 41.0 %collective-permute-start.19 = (bf16[800,800]{1,0:T(8,128)(2,1)S(1)}, bf16[800,800]{1,0:T(8,128)(2,1)}, u32[]{:S(2)}, u32[]{:S(2)}) collective-permute-start(bf16[800,800]{1,0:T(8,128)(2,1)S(1)} %pad_maximum_fusion.1), channel_id=1, source_target_pairs={{0,8},{8,0},{17,25},{25,17},{2,10},{10,2},{19,27},{27,19},{4,12},{... | collective-permute-start | bytes 3840008 | tf_op jit(solution)/shard_map/ppermute | solution.py:908
  273.6 36.6 %collective-permute-start.20 = (bf16[800,800]{1,0:T(8,128)(2,1)}, bf16[800,800]{1,0:T(8,128)(2,1)}, u32[]{:S(2)}, u32[]{:S(2)}) collective-permute-start(bf16[800,800]{1,0:T(8,128)(2,1)} %pad_maximum_fusion), channel_id=1, source_target_pairs={{1,17},{9,25},{16,0},{24,8},{3,19},{11,27},{18,2},{26,10},{5,21},{... | collective-permute-start | bytes 3840008 | tf_op jit(solution)/shard_map/ppermute | solution.py:908
  274.9 35.3 %collective-permute-start.21 = (bf16[800,800]{1,0:T(8,128)(2,1)S(1)}, bf16[800,800]{1,0:T(8,128)(2,1)}, u32[]{:S(2)}, u32[]{:S(2)}) collective-permute-start(bf16[800,800]{1,0:T(8,128)(2,1)S(1)} %pad_maximum_fusion.1), channel_id=1, source_target_pairs={{1,25},{9,17},{16,8},{24,0},{3,27},{11,19},{18,10},{26,2},{5,29},{... | collective-permute-start | bytes 3840008 | tf_op jit(solution)/shard_map/ppermute | solution.py:908
  315.5 17.0 %collective-permute-start.24 = (bf16[400,800]{1,0:T(8,128)(2,1)S(1)}, bf16[400,800]{1,0:T(8,128)(2,1)S(1)}, u32[]{:S(2)}, u32[]{:S(2)}) collective-permute-start(bf16[400,800]{1,0:T(8,128)(2,1)S(1)} %constant_dynamic-slice_fusion.1), channel_id=1, source_target_pairs={{0,2},{2,0},{4,6},{6,4},{8,10},{10,8},{12,14},{14,12},{17,19},{19,... | collective-permute-start | bytes 1920008 | tf_op jit(solution)/shard_map/ppermute | solution.py:920
  318.9 13.6 %collective-permute-start.22 = (f32[4,2000]{1,0:T(4,128)S(1)}, f32[4,2000]{1,0:T(4,128)S(1)}, u32[]{:S(2)}, u32[]{:S(2)}) collective-permute-start(f32[4,2000]{1,0:T(4,128)S(1)} %concatenate.32), channel_id=1, source_target_pairs={{0,1},{1,0},{2,3},{3,2},{4,5},{5,4},{6,7},{7,6},{8,9},{9,8},{10,11... | collective-permute-start | bytes 96008 | tf_op jit(solution)/shard_map/ppermute | solution.py:966
  332.8 20.9 %collective-permute-start.27 = (bf16[400,800]{1,0:T(8,128)(2,1)S(1)}, bf16[400,800]{1,0:T(8,128)(2,1)S(1)}, u32[]{:S(2)}, u32[]{:S(2)}) collective-permute-start(bf16[400,800]{1,0:T(8,128)(2,1)S(1)} %add_convert_fusion.2), channel_id=1, source_target_pairs={{0,6},{2,4},{4,2},{6,0},{8,14},{10,12},{12,10},{14,8},{17,23},{19,... | collective-permute-start | bytes 1920008 | tf_op jit(solution)/shard_map/ppermute | solution.py:920
  338.0 4.0 %collective-permute-start.23 = (f32[4,2000]{1,0:T(4,128)S(1)}, f32[4,2000]{1,0:T(4,128)S(1)}, u32[]{:S(2)}, u32[]{:S(2)}) collective-permute-start(f32[4,2000]{1,0:T(4,128)S(1)} %add.52), channel_id=1, source_target_pairs={{0,8},{8,0},{16,24},{24,16},{1,9},{9,1},{17,25},{25,17},{2,10},{10... | collective-permute-start | bytes 96008 | tf_op jit(solution)/shard_map/ppermute | solution.py:966
  342.0 4.0 %collective-permute-start.25 = (f32[4,2000]{1,0:T(4,128)S(1)}, f32[4,2000]{1,0:T(4,128)S(1)}, u32[]{:S(2)}, u32[]{:S(2)}) collective-permute-start(f32[4,2000]{1,0:T(4,128)S(1)} %add.54), channel_id=1, source_target_pairs={{0,16},{8,24},{16,0},{24,8},{1,17},{9,25},{17,1},{25,9},{2,18},{10... | collective-permute-start | bytes 96008 | tf_op jit(solution)/shard_map/ppermute | solution.py:966
  356.0 21.6 %collective-permute-start.29 = (bf16[400,800]{1,0:T(8,128)(2,1)S(1)}, bf16[400,800]{1,0:T(8,128)(2,1)S(1)}, u32[]{:S(2)}, u32[]{:S(2)}) collective-permute-start(bf16[400,800]{1,0:T(8,128)(2,1)S(1)} %add_convert_fusion.1), channel_id=1, source_target_pairs={{0,2},{2,0},{4,6},{6,4},{8,10},{10,8},{12,14},{14,12},{17,19},{19,... | collective-permute-start | bytes 1920008 | tf_op jit(solution)/shard_map/ppermute | solution.py:920
  363.2 9.6 %collective-permute-start.26 = (f32[4,2000]{1,0:T(4,128)S(1)}, f32[4,2000]{1,0:T(4,128)S(1)}, u32[]{:S(2)}, u32[]{:S(2)}) collective-permute-start(f32[4,2000]{1,0:T(4,128)S(1)} %add.55), channel_id=1, source_target_pairs={{0,2},{2,0},{4,6},{6,4},{1,3},{3,1},{5,7},{7,5},{8,10},{10,8},{12,... | collective-permute-start | bytes 96008 | tf_op jit(solution)/shard_map/ppermute | solution.py:966
  372.7 4.9 %collective-permute-start.28 = (f32[4,2000]{1,0:T(4,128)S(1)}, f32[4,2000]{1,0:T(4,128)S(1)}, u32[]{:S(2)}, u32[]{:S(2)}) collective-permute-start(f32[4,2000]{1,0:T(4,128)S(1)} %add.57), channel_id=1, source_target_pairs={{0,4},{2,6},{4,0},{6,2},{1,5},{3,7},{5,1},{7,3},{8,12},{10,14},{12... | collective-permute-start | bytes 96008 | tf_op jit(solution)/shard_map/ppermute | solution.py:966
  377.9 7.3 %collective-permute-start.30 = (bf16[800,800]{1,0:T(8,128)(2,1)S(1)}, bf16[800,800]{1,0:T(8,128)(2,1)}, u32[]{:S(2)}, u32[]{:S(2)}) collective-permute-start(bf16[800,800]{1,0:T(8,128)(2,1)S(1)} %pad_maximum_fusion.2), channel_id=1, source_target_pairs={{0,1},{8,9},{17,16},{25,24},{2,3},{10,11},{19,18},{27,26},{4,5},{1... | collective-permute-start | bytes 3840008 | tf_op jit(solution)/shard_map/ppermute | solution.py:951
  380.3 1.5 slice-start
  386.7 1.9 copy-start.1
Sparse Core Ops, SparseCore 0:
  10.0 76.3 all-gather.5
  185.1 82.3 reduce-scatter.2
  269.9 35.1 reduce-scatter.4
  315.6 40.2 all-gather.3
